TPU v7x, 32 devices: a whole 2x2x4 slice. The times are simulated.
32 devices in a mesh: ty: 8 (over y, x, core), tx: 4 (over z).
Axes of the slice: x: 2, y: 2, z: 4, core: 2. Of those that a mesh axis runs over, the one named last changes fastest.
Arguments:
- object_slices: float32 [2, 2, 1024, 512], P(None, None, 'ty', 'tx'), may hold values from -5 to 5
- probe: float32 [4, 2, 128, 128], replicated, may hold values from -4 to 4
- measured: float32 [8, 4, 4, 128, 128], P('ty', 'tx'), may hold values from 0 to 2
- offsets: int32 [2, 8, 4, 4], P(None, 'ty', 'tx'), may hold values from 0 to 127, as said below
- counts: int32 [8, 4], P('ty', 'tx'), may hold values from 1 to 4, as said below
Outputs:
- object_grad: float32 [2, 2, 1024, 512], P(None, None, 'ty', 'tx')
- probe_grad: float32 [4, 2, 128, 128], replicated
Inputs may be any that keep to these rules, and one draw needn't show every extreme that they name: `counts`: each tile has 1 to 4 live slots, and some tile has all 4 live. Every window lies inside the object: in the last tile row (column) the row (column) offset is at most 0. Slot 0 of every tile sits at the largest row and column offsets that its tile allows.
All inputs are finite; a program needn't handle non-finite values.
Results may differ from a plain program's by a relative error of at most 0.0003.
Values sent between devices are 32-bit elements; how exact they have to be, the bound alone decides.
No kernel may reach another device: no remote copies, remote signals or barrier semaphores. Data moves between devices by JAX's collectives and lax.ppermute only.
A program may use at most 64 MiB of HBM per device.

v0:
```python
import functools

import jax
import jax.numpy as jnp
import numpy as np
from jax import lax
from jax.experimental import pallas as pl
from jax.experimental.pallas import tpu as pltpu
from jax.sharding import PartitionSpec as P

BF16 = jnp.bfloat16
F32 = jnp.float32


def moved(array, axis, by):
    length = lax.axis_size(axis)
    pairs = [(i, i + by) for i in range(length) if 0 <= i + by < length]
    return lax.ppermute(array, axis, pairs)


def moved_both(array, rows_by, cols_by):
    rows, cols = lax.axis_size("ty"), lax.axis_size("tx")
    pairs = [
        (a * cols + b, (a + rows_by) * cols + b + cols_by)
        for a in range(rows)
        for b in range(cols)
        if 0 <= a + rows_by < rows and 0 <= b + cols_by < cols
    ]
    return lax.ppermute(array, ("ty", "tx"), pairs)


def swapped(array, axis, bit):
    length = lax.axis_size(axis)
    return lax.ppermute(array, axis, [(i, i ^ bit) for i in range(length)])


def summed_everywhere(array):
    shape = array.shape
    steps = []
    for axis in ("ty", "tx"):
        bit = 1
        while bit < lax.axis_size(axis):
            steps.append((axis, bit))
            bit *= 2
    part = array.reshape(-1, shape[-1])
    for axis, bit in steps:
        half = part.shape[0] // 2
        side = (lax.axis_index(axis) // bit) % 2
        mine = lax.dynamic_slice_in_dim(part, side * half, half, 0)
        other = lax.dynamic_slice_in_dim(part, (1 - side) * half, half, 0)
        part = mine + swapped(other, axis, bit)
    for axis, bit in steps[::-1]:
        side = (lax.axis_index(axis) // bit) % 2
        other = swapped(part, axis, bit)
        low = jnp.where(side == 0, part, other)
        high = jnp.where(side == 0, other, part)
        part = jnp.concatenate([low, high], axis=0)
    return part.reshape(shape)


def real_forms(table):
    right = np.block([[table.real, table.imag], [-table.imag, table.real]]).astype(np.float32)
    high = right.astype(BF16)
    low = (right - high.astype(np.float32)).astype(BF16)
    return (
        np.concatenate([high, high, low], axis=0),
        np.concatenate([high.T, high.T, low.T], axis=1),
    )


def tables(size):
    positions = np.arange(size)
    dft = np.exp(-2j * np.pi * (positions[:, None] * positions[None, :] % size) / size) / np.sqrt(size)
    freq = (positions + size // 2) % size - size // 2
    chirp = np.exp(-2j * np.pi * (freq * freq % (4 * size)) / (4 * size))
    through = dft.conj() @ (chirp[:, None] * dft)
    return real_forms(dft), real_forms(through)


def halves(x):
    high = x.astype(BF16)
    return high, (x - high.astype(F32)).astype(BF16)


def from_right(x, table):
    high, low = halves(x)
    return jnp.dot(jnp.concatenate([high, low, high], axis=1), table, preferred_element_type=F32)


def from_left(x, table):
    high, low = halves(x)
    return jnp.dot(table, jnp.concatenate([high, low, high], axis=0), preferred_element_type=F32)


def rows_to_lanes(x, size):
    count = x.shape[0] // size
    parts = [x[m * size:(m + 1) * size] for m in range(count)]
    return jnp.concatenate(
        [jnp.concatenate([p[:, :size] for p in parts], axis=1),
         jnp.concatenate([p[:, size:] for p in parts], axis=1)], axis=0)


def both_sides(fields, right_table, left_table):
    size = fields[0][0].shape[-1]
    x = jnp.concatenate([jnp.concatenate([re, im], axis=1) for re, im in fields], axis=0)
    y = rows_to_lanes(from_right(x, right_table), size)
    z = from_left(y, left_table)
    return [
        (z[:size, m * size:(m + 1) * size], z[size:, m * size:(m + 1) * size])
        for m in range(len(fields))
    ]


def product(a, b):
    return (a[0] * b[0] - a[1] * b[1], a[0] * b[1] + a[1] * b[0])


def fill(wide, own, right, down, corner, size):
    wide[:, :size, :size] = own[...]
    wide[:, :size, size:] = right[...]
    wide[:, size:, :size] = down[...]
    wide[:, size:, size:] = corner[...]


SUBLANES = 8


def window_of(wide, at, slot, size):
    row, col = at[0, slot], at[1, slot]
    shift = lax.rem(row, SUBLANES)
    rows = pl.ds(pl.multiple_of(row - shift, SUBLANES), size + SUBLANES)
    left = lax.rem(2 * size - col, 2 * size)
    up = lax.rem(size + SUBLANES - shift, size + SUBLANES)
    return [
        pltpu.roll(pltpu.roll(wide[c, rows, :], left, axis=1)[:, :size], up, axis=0)[:size]
        for c in range(2)
    ]


def add_window(total, at, slot, grads, size):
    row, col = at[0, slot], at[1, slot]
    shift = lax.rem(row, SUBLANES)
    rows = pl.ds(pl.multiple_of(row - shift, SUBLANES), size + SUBLANES)
    for c in range(2):
        taller = jnp.concatenate([grads[c], jnp.zeros((SUBLANES, size), F32)], axis=0)
        lowered = pltpu.roll(taller, shift, axis=0)
        padded = jnp.concatenate([lowered, jnp.zeros_like(lowered)], axis=1)
        total[c, rows, :] += pltpu.roll(padded, col, axis=1)


def give(total, own, right, down, corner, size):
    own[...] = total[:, :size, :size]
    right[...] = total[:, :size, size:]
    down[...] = total[:, size:, :size]
    corner[...] = total[:, size:, size:]


def first_kernel(at, own, right, down, corner, probe, right_table, left_table, psi, window, wide):
    size = own.shape[-1]
    modes = probe.shape[0]
    slot = pl.program_id(0)

    @pl.when(slot == 0)
    def _():
        fill(wide, own, right, down, corner, size)

    w = window_of(wide, at, slot, size)
    window[0, 0], window[0, 1] = w[0], w[1]
    fields = [product((probe[m, 0], probe[m, 1]), w) for m in range(modes)]
    waves = both_sides(fields, right_table[...], left_table[...])
    for m in range(modes):
        psi[0, m, 0], psi[0, m, 1] = waves[m]


def second_kernel(at, count, own, right, down, corner, psi, measured, right_table, left_table,
                  back, g_own, g_right, g_down, g_corner, wide, total):
    size = own.shape[-1]
    modes = psi.shape[1]
    slot = pl.program_id(0)

    @pl.when(slot == 0)
    def _():
        fill(wide, own, right, down, corner, size)
        total[...] = jnp.zeros_like(total)

    w = window_of(wide, at, slot, size)
    fields = [product((psi[0, m, 0], psi[0, m, 1]), w) for m in range(modes)]
    far = both_sides(fields, right_table[...], left_table[...])
    intensity = sum(re * re + im * im for re, im in far)
    live = jnp.where(slot < count[0], 2.0, 0.0).astype(F32)
    diff = (intensity - measured[0]) * live
    conj = both_sides([(re * diff, -(im * diff)) for re, im in far], right_table[...], left_table[...])
    g_re, g_im = 0.0, 0.0
    for m in range(modes):
        back[0, m, 0], back[0, m, 1] = product(conj[m], w)
        re, im = product(conj[m], (psi[0, m, 0], psi[0, m, 1]))
        g_re, g_im = g_re + re, g_im - im
    add_window(total, at, slot, (g_re, g_im), size)

    @pl.when(slot == pl.num_programs(0) - 1)
    def _():
        give(total, g_own, g_right, g_down, g_corner, size)


def third_kernel(at, back, window, probe, right_table, left_table,
                 g_probe, g_own, g_right, g_down, g_corner, total):
    size = window.shape[-1]
    modes = probe.shape[0]
    slot = pl.program_id(0)

    @pl.when(slot == 0)
    def _():
        total[...] = jnp.zeros_like(total)
        g_probe[...] = jnp.zeros_like(g_probe)

    conj = both_sides(
        [(back[0, m, 0], back[0, m, 1]) for m in range(modes)], right_table[...], left_table[...]
    )
    w = (window[0, 0], window[0, 1])
    g_re, g_im = 0.0, 0.0
    for m in range(modes):
        re, im = product(conj[m], w)
        g_probe[m, 0] += re
        g_probe[m, 1] -= im
        re, im = product(conj[m], (probe[m, 0], probe[m, 1]))
        g_re, g_im = g_re + re, g_im - im
    add_window(total, at, slot, (g_re, g_im), size)

    @pl.when(slot == pl.num_programs(0) - 1)
    def _():
        give(total, g_own, g_right, g_down, g_corner, size)


def whole(shape):
    return pl.BlockSpec(shape, lambda s: (0,) * len(shape))


def by_slot(shape):
    return pl.BlockSpec((1,) + shape[1:], lambda s: (s,) + (0,) * (len(shape) - 1))


SCALARS = pl.BlockSpec(memory_space=pltpu.SMEM)


def call(kernel, slots, args, in_specs, outs, out_specs, scratch, flops):
    return pl.pallas_call(
        kernel,
        grid=(slots,),
        in_specs=in_specs,
        out_specs=out_specs,
        out_shape=[jax.ShapeDtypeStruct(s, F32) for s in outs],
        scratch_shapes=[pltpu.VMEM(s, F32) for s in scratch],
        compiler_params=pltpu.CompilerParams(vmem_limit_bytes=48 * 1024 * 1024),
        cost_estimate=pl.CostEstimate(flops=flops, bytes_accessed=4 * 1024 * 1024, transcendentals=0),
    )(*args)


def halo(tile):
    return tile, moved(tile, "tx", -1), moved(tile, "ty", -1), moved_both(tile, -1, -1)


def returned(own, right, down, corner):
    return (own + moved(right, "tx", 1)) + (moved(down, "ty", 1) + moved_both(corner, 1, 1))


def on_device(object_slices, probe, measured, offsets, counts):
    size = object_slices.shape[-1]
    slots = offsets.shape[-1]
    modes = probe.shape[0]
    at = offsets.reshape(2, slots)
    count = counts.reshape(1)
    (dft_right, dft_left), (through_right, through_left) = tables(size)
    tile = (2, size, size)
    wide = (2, 2 * size, 2 * size)
    field = (slots, modes, 2, size, size)
    right_t, left_t = dft_right.shape, dft_left.shape
    flops = slots * modes * 2 * size * (2 * size) * (6 * size) * 2

    psi, window = call(
        first_kernel, slots,
        (at, *halo(object_slices[0]), probe, through_right, through_left),
        [SCALARS] + [whole(tile)] * 4 + [whole(probe.shape), whole(right_t), whole(left_t)],
        [field, (slots, 2, size, size)],
        [by_slot(field), by_slot((slots, 2, size, size))],
        [wide], flops,
    )
    back, *grad_1 = call(
        second_kernel, slots,
        (at, count, *halo(object_slices[1]), psi, measured.reshape(slots, size, size), dft_right, dft_left),
        [SCALARS, SCALARS] + [whole(tile)] * 4
        + [by_slot(field), by_slot((slots, size, size)), whole(right_t), whole(left_t)],
        [field] + [tile] * 4,
        [by_slot(field)] + [whole(tile)] * 4,
        [wide, wide], 2 * flops,
    )
    grad_probe, *grad_0 = call(
        third_kernel, slots,
        (at, back, window, probe, through_right, through_left),
        [SCALARS, by_slot(field), by_slot((slots, 2, size, size)), whole(probe.shape), whole(right_t), whole(left_t)],
        [probe.shape] + [tile] * 4,
        [whole(probe.shape)] + [whole(tile)] * 4,
        [wide], flops,
    )
    object_grad = jnp.stack([returned(*grad_0), returned(*grad_1)])
    return object_grad, summed_everywhere(grad_probe)


def solution(mesh):
    in_specs = (
        P(None, None, "ty", "tx"),
        P(),
        P("ty", "tx", None, None, None),
        P(None, "ty", "tx", None),
        P("ty", "tx"),
    )
    out_specs = (P(None, None, "ty", "tx"), P())
    return jax.shard_map(
        on_device, mesh=mesh, in_specs=in_specs, out_specs=out_specs, check_vma=False
    )
```

profile of v0, /device:TPU:0, one launch (start us, length us, event | category | flops | bytes accessed | tf_op | source)
XLA Modules:
  0.0 100.8 jit_solution(11017128850191636176)
XLA Ops:
  1.6 1.3 %collective-permute-start.3 = (f32[2,128,128]{2,1,0:T(8,128)S(1)}, f32[2,128,128]{2,1,0:T(8,128)S(1)}, u32[]{:S(2)}, u32[]{:S(2)}) collective-permute-start(f32[2,128,128]{2,1,0:T(8,128)S(1)} %get-tuple-element.30.own), channel_id=1, source_target_pairs={{1,0},{2,1},{3,2},{5,4},{6,5},{7,6},{9,8},{10,9},{11,10},{13,12},{... | collective-permute-start | bytes 393224 | tf_op jit(solution)/shard_map/ppermute | solution.py:18
  2.9 1.3 %collective-permute-start.4 = (f32[2,128,128]{2,1,0:T(8,128)S(1)}, f32[2,128,128]{2,1,0:T(8,128)S(1)}, u32[]{:S(2)}, u32[]{:S(2)}) collective-permute-start(f32[2,128,128]{2,1,0:T(8,128)S(1)} %get-tuple-element.30.own), channel_id=1, source_target_pairs={{4,0},{8,4},{12,8},{16,12},{20,16},{24,20},{28,24},{5,1},{9,5},{13... | collective-permute-start | bytes 393224 | tf_op jit(solution)/shard_map/ppermute | solution.py:18
  4.2 1.3 %collective-permute-start.5 = (f32[2,128,128]{2,1,0:T(8,128)S(1)}, f32[2,128,128]{2,1,0:T(8,128)S(1)}, u32[]{:S(2)}, u32[]{:S(2)}) collective-permute-start(f32[2,128,128]{2,1,0:T(8,128)S(1)} %get-tuple-element.30.own), channel_id=1, source_target_pairs={{5,0},{6,1},{7,2},{9,4},{10,5},{11,6},{13,8},{14,9},{15,10},{17,12... | collective-permute-start | bytes 393224 | tf_op jit(solution)/shard_map/ppermute | solution.py:29
  5.5 1.3 %collective-permute-start = (f32[2,128,128]{2,1,0:T(8,128)S(1)}, f32[2,128,128]{2,1,0:T(8,128)S(1)}, u32[]{:S(2)}, u32[]{:S(2)}) collective-permute-start(f32[2,128,128]{2,1,0:T(8,128)S(1)} %get-tuple-element.31.own), channel_id=1, source_target_pairs={{1,0},{2,1},{3,2},{5,4},{6,5},{7,6},{9,8},{10,9},{11,10},{13,12},{... | collective-permute-start | bytes 393224 | tf_op jit(solution)/shard_map/ppermute | solution.py:18
  6.8 1.3 %collective-permute-start.1 = (f32[2,128,128]{2,1,0:T(8,128)S(1)}, f32[2,128,128]{2,1,0:T(8,128)S(1)}, u32[]{:S(2)}, u32[]{:S(2)}) collective-permute-start(f32[2,128,128]{2,1,0:T(8,128)S(1)} %get-tuple-element.31.own), channel_id=1, source_target_pairs={{4,0},{8,4},{12,8},{16,12},{20,16},{24,20},{28,24},{5,1},{9,5},{13... | collective-permute-start | bytes 393224 | tf_op jit(solution)/shard_map/ppermute | solution.py:18
  10.0 1.3 %collective-permute-start.2 = (f32[2,128,128]{2,1,0:T(8,128)S(1)}, f32[2,128,128]{2,1,0:T(8,128)S(1)}, u32[]{:S(2)}, u32[]{:S(2)}) collective-permute-start(f32[2,128,128]{2,1,0:T(8,128)S(1)} %get-tuple-element.31.own), channel_id=1, source_target_pairs={{5,0},{6,1},{7,2},{9,4},{10,5},{11,6},{13,8},{14,9},{15,10},{17,12... | collective-permute-start | bytes 393224 | tf_op jit(solution)/shard_map/ppermute | solution.py:29
  11.3 2.4 %collective-permute-done.5.corner = f32[2,128,128]{2,1,0:T(8,128)S(1)} collective-permute-done((f32[2,128,128]{2,1,0:T(8,128)S(1)}, f32[2,128,128]{2,1,0:T(8,128)S(1)}, u32[]{:S(2)}, u32[]{:S(2)}) %collective-permute-start.5) | collective-permute-done | bytes 131104 | tf_op jit(solution)/shard_map/ppermute | solution.py:29
  17.4 5.3 %shard_map.104 = (f32[4,4,2,128,128]{4,3,2,1,0:T(8,128)S(1)}, f32[4,2,128,128]{3,2,1,0:T(8,128)S(1)}) custom-call(s32[2,4]{1,0:T(2,128)S(1)} %bitcast.17, f32[2,128,128]{2,1,0:T(8,128)S(1)} %get-tuple-element.30.own, f32[2,128,128]{2,1,0:T(8,128)S(1)} %collective-permute-done.3.right, f32[2,128,128]{2,1,0:T(8,128)S(1)} %collective-permute-done.4.down, ...), custom_call_target="tpu_custom_call" | custom-call | flops 1610612736 | bytes 4194304 | tf_op jit(solution)/shard_map/pallas_call | solution.py:246
  22.7 1.3 %copy-done.9 = f32[4,4,2,128,128]{4,3,2,1,0:T(8,128)} copy-done((f32[4,4,2,128,128]{4,3,2,1,0:T(8,128)}, f32[4,4,2,128,128]{4,3,2,1,0:T(8,128)S(1)}, u32[]{:S(2)}) %copy-start.9) | copy-done | bytes 2097176
  24.1 10.6 %shard_map.105 = (f32[4,4,2,128,128]{4,3,2,1,0:T(8,128)S(1)}, f32[2,128,128]{2,1,0:T(8,128)S(1)}, f32[2,128,128]{2,1,0:T(8,128)S(1)}, f32[2,128,128]{2,1,0:T(8,128)S(1)}, f32[2,128,128]{2,1,0:T(8,128)S(1)}) custom-call(s32[2,4]{1,0:T(2,128)S(1)} %bitcast.18, s32[1]{0:T(128)} %bitcast.13.count, f32[2,128,128]{2,1,0:T(8,128)S(1)} %get-tuple-element.31.own, ...), custom_call_target="tpu_custom_call" | custom-call | flops 3221225472 | bytes 4194304 | tf_op jit(solution)/shard_map/pallas_call | solution.py:246
  34.8 5.6 %shard_map.106 = (f32[4,2,128,128]{3,2,1,0:T(8,128)S(1)}, f32[2,128,128]{2,1,0:T(8,128)S(1)}, f32[2,128,128]{2,1,0:T(8,128)S(1)}, f32[2,128,128]{2,1,0:T(8,128)S(1)}, f32[2,128,128]{2,1,0:T(8,128)S(1)}) custom-call(s32[2,4]{1,0:T(2,128)S(1)} %bitcast.19, f32[4,4,2,128,128]{4,3,2,1,0:T(8,128)S(1)} %get-tuple-element.15.back, ...), custom_call_target="tpu_custom_call" | custom-call | flops 1610612736 | bytes 4194304 | tf_op jit(solution)/shard_map/pallas_call | solution.py:246
  40.5 2.3 %collective-permute-start.12 = (f32[512,128]{1,0:T(8,128)S(1)}, f32[512,128]{1,0:T(8,128)S(1)}, u32[]{:S(2)}, u32[]{:S(2)}) collective-permute-start(f32[512,128]{1,0:T(8,128)S(1)} %constant_dynamic-slice_fusion.4), channel_id=1, source_target_pairs={{0,4},{4,0},{8,12},{12,8},{16,20},{20,16},{24,28},{28,24},{1,5},{5... | collective-permute-start | bytes 786440 | tf_op jit(solution)/shard_map/ppermute | solution.py:34
  44.0 2.1 %collective-permute-start.13 = (f32[256,128]{1,0:T(8,128)S(1)}, f32[256,128]{1,0:T(8,128)S(1)}, u32[]{:S(2)}, u32[]{:S(2)}) collective-permute-start(f32[256,128]{1,0:T(8,128)S(1)} %constant_dynamic-slice_fusion.3), channel_id=1, source_target_pairs={{0,8},{4,12},{8,0},{12,4},{16,24},{20,28},{24,16},{28,20},{1,9},{5... | collective-permute-start | bytes 393224 | tf_op jit(solution)/shard_map/ppermute | solution.py:34
  46.1 4.0 %collective-permute-done.13 = f32[256,128]{1,0:T(8,128)S(1)} collective-permute-done((f32[256,128]{1,0:T(8,128)S(1)}, f32[256,128]{1,0:T(8,128)S(1)}, u32[]{:S(2)}, u32[]{:S(2)}) %collective-permute-start.13) | collective-permute-done | bytes 131104 | tf_op jit(solution)/shard_map/ppermute | solution.py:34
  50.2 1.3 %collective-permute-start.14 = (f32[128,128]{1,0:T(8,128)S(1)}, f32[128,128]{1,0:T(8,128)S(1)}, u32[]{:S(2)}, u32[]{:S(2)}) collective-permute-start(f32[128,128]{1,0:T(8,128)S(1)} %constant_dynamic-slice_fusion.2), channel_id=1, source_target_pairs={{0,16},{4,20},{8,24},{12,28},{16,0},{20,4},{24,8},{28,12},{1,17},{... | collective-permute-start | bytes 196616 | tf_op jit(solution)/shard_map/ppermute | solution.py:34
  51.4 3.1 %collective-permute-done.14 = f32[128,128]{1,0:T(8,128)S(1)} collective-permute-done((f32[128,128]{1,0:T(8,128)S(1)}, f32[128,128]{1,0:T(8,128)S(1)}, u32[]{:S(2)}, u32[]{:S(2)}) %collective-permute-start.14) | collective-permute-done | bytes 65568 | tf_op jit(solution)/shard_map/ppermute | solution.py:34
  54.5 2.4 %collective-permute-start.15 = (f32[64,128]{1,0:T(8,128)S(1)}, f32[64,128]{1,0:T(8,128)S(1)}, u32[]{:S(2)}, u32[]{:S(2)}) collective-permute-start(f32[64,128]{1,0:T(8,128)S(1)} %constant_dynamic-slice_fusion.1), channel_id=1, source_target_pairs={{0,1},{1,0},{2,3},{3,2},{4,5},{5,4},{6,7},{7,6},{8,9},{9,8},{10,11... | collective-permute-start | bytes 98312 | tf_op jit(solution)/shard_map/ppermute | solution.py:34
  56.9 1.9 %collective-permute-done.15 = f32[64,128]{1,0:T(8,128)S(1)} collective-permute-done((f32[64,128]{1,0:T(8,128)S(1)}, f32[64,128]{1,0:T(8,128)S(1)}, u32[]{:S(2)}, u32[]{:S(2)}) %collective-permute-start.15) | collective-permute-done | bytes 32800 | tf_op jit(solution)/shard_map/ppermute | solution.py:34
  58.9 3.4 %collective-permute-start.16 = (f32[32,128]{1,0:T(8,128)S(1)}, f32[32,128]{1,0:T(8,128)S(1)}, u32[]{:S(2)}, u32[]{:S(2)}) collective-permute-start(f32[32,128]{1,0:T(8,128)S(1)} %constant_dynamic-slice_fusion), channel_id=1, source_target_pairs={{0,2},{1,3},{2,0},{3,1},{4,6},{5,7},{6,4},{7,5},{8,10},{9,11},{10,... | collective-permute-start | bytes 49160 | tf_op jit(solution)/shard_map/ppermute | solution.py:34
  62.3 1.7 %collective-permute-done.16 = f32[32,128]{1,0:T(8,128)S(1)} collective-permute-done((f32[32,128]{1,0:T(8,128)S(1)}, f32[32,128]{1,0:T(8,128)S(1)}, u32[]{:S(2)}, u32[]{:S(2)}) %collective-permute-start.16) | collective-permute-done | bytes 16416 | tf_op jit(solution)/shard_map/ppermute | solution.py:34
  64.0 3.0 %collective-permute-start.17 = (f32[32,128]{1,0:T(8,128)S(1)}, f32[32,128]{1,0:T(8,128)S(1)}, u32[]{:S(2)}, u32[]{:S(2)}) collective-permute-start(f32[32,128]{1,0:T(8,128)S(1)} %dynamic-slice_add_fusion.4), channel_id=1, source_target_pairs={{0,2},{1,3},{2,0},{3,1},{4,6},{5,7},{6,4},{7,5},{8,10},{9,11},{10,... | collective-permute-start | bytes 49160 | tf_op jit(solution)/shard_map/ppermute | solution.py:34
  67.0 1.7 %collective-permute-done.17 = f32[32,128]{1,0:T(8,128)S(1)} collective-permute-done((f32[32,128]{1,0:T(8,128)S(1)}, f32[32,128]{1,0:T(8,128)S(1)}, u32[]{:S(2)}, u32[]{:S(2)}) %collective-permute-start.17) | collective-permute-done | bytes 16416 | tf_op jit(solution)/shard_map/ppermute | solution.py:34
  68.8 1.9 %collective-permute-start.18 = (f32[64,128]{1,0:T(8,128)S(1)}, f32[64,128]{1,0:T(8,128)S(1)}, u32[]{:S(2)}, u32[]{:S(2)}) collective-permute-start(f32[64,128]{1,0:T(8,128)S(1)} %pad_maximum_fusion.5), channel_id=1, source_target_pairs={{0,1},{1,0},{2,3},{3,2},{4,5},{5,4},{6,7},{7,6},{8,9},{9,8},{10,11... | collective-permute-start | bytes 98312 | tf_op jit(solution)/shard_map/ppermute | solution.py:34
  70.7 2.0 %collective-permute-done.18 = f32[64,128]{1,0:T(8,128)S(1)} collective-permute-done((f32[64,128]{1,0:T(8,128)S(1)}, f32[64,128]{1,0:T(8,128)S(1)}, u32[]{:S(2)}, u32[]{:S(2)}) %collective-permute-start.18) | collective-permute-done | bytes 32800 | tf_op jit(solution)/shard_map/ppermute | solution.py:34
  72.8 2.2 %collective-permute-start.19 = (f32[128,128]{1,0:T(8,128)S(1)}, f32[128,128]{1,0:T(8,128)S(1)}, u32[]{:S(2)}, u32[]{:S(2)}) collective-permute-start(f32[128,128]{1,0:T(8,128)S(1)} %pad_maximum_fusion.4), channel_id=1, source_target_pairs={{0,16},{4,20},{8,24},{12,28},{16,0},{20,4},{24,8},{28,12},{1,17},{... | collective-permute-start | bytes 196616 | tf_op jit(solution)/shard_map/ppermute | solution.py:34
  75.0 1.3 %collective-permute-start.10 = (f32[2,128,128]{2,1,0:T(8,128)S(1)}, f32[2,128,128]{2,1,0:T(8,128)S(1)}, u32[]{:S(2)}, u32[]{:S(2)}) collective-permute-start(f32[2,128,128]{2,1,0:T(8,128)S(1)} %get-tuple-element.23), channel_id=1, source_target_pairs={{0,4},{4,8},{8,12},{12,16},{16,20},{20,24},{24,28},{1,5},{5,9},{9,... | collective-permute-start | bytes 393224 | tf_op jit(solution)/shard_map/ppermute | solution.py:18
  76.3 5.1 %collective-permute-start.11 = (f32[2,128,128]{2,1,0:T(8,128)S(1)}, f32[2,128,128]{2,1,0:T(8,128)S(1)}, u32[]{:S(2)}, u32[]{:S(2)}) collective-permute-start(f32[2,128,128]{2,1,0:T(8,128)S(1)} %get-tuple-element.24), channel_id=1, source_target_pairs={{0,5},{1,6},{2,7},{4,9},{5,10},{6,11},{8,13},{9,14},{10,15},{12,17... | collective-permute-start | bytes 393224 | tf_op jit(solution)/shard_map/ppermute | solution.py:29
  81.4 3.4 %collective-permute-start.9 = (f32[2,128,128]{2,1,0:T(8,128)S(1)}, f32[2,128,128]{2,1,0:T(8,128)S(1)}, u32[]{:S(2)}, u32[]{:S(2)}) collective-permute-start(f32[2,128,128]{2,1,0:T(8,128)S(1)} %get-tuple-element.22), channel_id=1, source_target_pairs={{0,1},{1,2},{2,3},{4,5},{5,6},{6,7},{8,9},{9,10},{10,11},{12,13},{... | collective-permute-start | bytes 393224 | tf_op jit(solution)/shard_map/ppermute | solution.py:18
  84.8 1.5 %collective-permute-start.7 = (f32[2,128,128]{2,1,0:T(8,128)S(1)}, f32[2,128,128]{2,1,0:T(8,128)S(1)}, u32[]{:S(2)}, u32[]{:S(2)}) collective-permute-start(f32[2,128,128]{2,1,0:T(8,128)S(1)} %get-tuple-element.19), channel_id=1, source_target_pairs={{0,4},{4,8},{8,12},{12,16},{16,20},{20,24},{24,28},{1,5},{5,9},{9,... | collective-permute-start | bytes 393224 | tf_op jit(solution)/shard_map/ppermute | solution.py:18
  86.3 4.4 %collective-permute-start.8 = (f32[2,128,128]{2,1,0:T(8,128)S(1)}, f32[2,128,128]{2,1,0:T(8,128)S(1)}, u32[]{:S(2)}, u32[]{:S(2)}) collective-permute-start(f32[2,128,128]{2,1,0:T(8,128)S(1)} %get-tuple-element.20), channel_id=1, source_target_pairs={{0,5},{1,6},{2,7},{4,9},{5,10},{6,11},{8,13},{9,14},{10,15},{12,17... | collective-permute-start | bytes 393224 | tf_op jit(solution)/shard_map/ppermute | solution.py:29
  90.8 2.0 %collective-permute-start.6 = (f32[2,128,128]{2,1,0:T(8,128)S(1)}, f32[2,128,128]{2,1,0:T(8,128)S(1)}, u32[]{:S(2)}, u32[]{:S(2)}) collective-permute-start(f32[2,128,128]{2,1,0:T(8,128)S(1)} %get-tuple-element.18), channel_id=1, source_target_pairs={{0,1},{1,2},{2,3},{4,5},{5,6},{6,7},{8,9},{9,10},{10,11},{12,13},{... | collective-permute-start | bytes 393224 | tf_op jit(solution)/shard_map/ppermute | solution.py:18
  93.9 4.3 %collective-permute-done.20 = f32[256,128]{1,0:T(8,128)S(1)} collective-permute-done((f32[256,128]{1,0:T(8,128)S(1)}, f32[256,128]{1,0:T(8,128)S(1)}, u32[]{:S(2)}, u32[]{:S(2)}) %collective-permute-start.20) | collective-permute-done | bytes 131104 | tf_op jit(solution)/shard_map/ppermute | solution.py:34
  (59 shorter events, 11.0 us)
Async XLA Ops:
  1.6 8.4 %collective-permute-start.3 = (f32[2,128,128]{2,1,0:T(8,128)S(1)}, f32[2,128,128]{2,1,0:T(8,128)S(1)}, u32[]{:S(2)}, u32[]{:S(2)}) collective-permute-start(f32[2,128,128]{2,1,0:T(8,128)S(1)} %get-tuple-element.30.own), channel_id=1, source_target_pairs={{1,0},{2,1},{3,2},{5,4},{6,5},{7,6},{9,8},{10,9},{11,10},{13,12},{... | collective-permute-start | bytes 393224 | tf_op jit(solution)/shard_map/ppermute | solution.py:18
  2.9 8.4 %collective-permute-start.4 = (f32[2,128,128]{2,1,0:T(8,128)S(1)}, f32[2,128,128]{2,1,0:T(8,128)S(1)}, u32[]{:S(2)}, u32[]{:S(2)}) collective-permute-start(f32[2,128,128]{2,1,0:T(8,128)S(1)} %get-tuple-element.30.own), channel_id=1, source_target_pairs={{4,0},{8,4},{12,8},{16,12},{20,16},{24,20},{28,24},{5,1},{9,5},{13... | collective-permute-start | bytes 393224 | tf_op jit(solution)/shard_map/ppermute | solution.py:18
  4.2 9.5 %collective-permute-start.5 = (f32[2,128,128]{2,1,0:T(8,128)S(1)}, f32[2,128,128]{2,1,0:T(8,128)S(1)}, u32[]{:S(2)}, u32[]{:S(2)}) collective-permute-start(f32[2,128,128]{2,1,0:T(8,128)S(1)} %get-tuple-element.30.own), channel_id=1, source_target_pairs={{5,0},{6,1},{7,2},{9,4},{10,5},{11,6},{13,8},{14,9},{15,10},{17,12... | collective-permute-start | bytes 393224 | tf_op jit(solution)/shard_map/ppermute | solution.py:29
  5.5 18.5 %collective-permute-start = (f32[2,128,128]{2,1,0:T(8,128)S(1)}, f32[2,128,128]{2,1,0:T(8,128)S(1)}, u32[]{:S(2)}, u32[]{:S(2)}) collective-permute-start(f32[2,128,128]{2,1,0:T(8,128)S(1)} %get-tuple-element.31.own), channel_id=1, source_target_pairs={{1,0},{2,1},{3,2},{5,4},{6,5},{7,6},{9,8},{10,9},{11,10},{13,12},{... | collective-permute-start | bytes 393224 | tf_op jit(solution)/shard_map/ppermute | solution.py:18
  6.8 17.2 %collective-permute-start.1 = (f32[2,128,128]{2,1,0:T(8,128)S(1)}, f32[2,128,128]{2,1,0:T(8,128)S(1)}, u32[]{:S(2)}, u32[]{:S(2)}) collective-permute-start(f32[2,128,128]{2,1,0:T(8,128)S(1)} %get-tuple-element.31.own), channel_id=1, source_target_pairs={{4,0},{8,4},{12,8},{16,12},{20,16},{24,20},{28,24},{5,1},{9,5},{13... | collective-permute-start | bytes 393224 | tf_op jit(solution)/shard_map/ppermute | solution.py:18
  10.0 14.0 %collective-permute-start.2 = (f32[2,128,128]{2,1,0:T(8,128)S(1)}, f32[2,128,128]{2,1,0:T(8,128)S(1)}, u32[]{:S(2)}, u32[]{:S(2)}) collective-permute-start(f32[2,128,128]{2,1,0:T(8,128)S(1)} %get-tuple-element.31.own), channel_id=1, source_target_pairs={{5,0},{6,1},{7,2},{9,4},{10,5},{11,6},{13,8},{14,9},{15,10},{17,12... | collective-permute-start | bytes 393224 | tf_op jit(solution)/shard_map/ppermute | solution.py:29
  13.7 1.0 %copy-start = (f32[4,2,128,128]{3,2,1,0:T(8,128)S(1)}, f32[4,2,128,128]{3,2,1,0:T(8,128)}, u32[]{:S(2)}) copy-start(f32[4,2,128,128]{3,2,1,0:T(8,128)} %probe.3) | copy-start | bytes 1572868
  14.8 0.7 copy-start.3
  15.4 1.0 copy-start.4
  16.4 1.0 copy-start.5
  17.4 6.6 %copy-start.2 = (f32[1,1,4,128,128]{4,3,2,1,0:T(8,128)S(1)}, f32[1,1,4,128,128]{4,3,2,1,0:T(8,128)}, u32[]{:S(2)}) copy-start(f32[1,1,4,128,128]{4,3,2,1,0:T(8,128)} %param.11) | copy-start | bytes 786436
  17.4 6.7 %copy-start.7 = (bf16[768,256]{1,0:T(8,128)(2,1)S(1)}, bf16[768,256]{1,0:T(8,128)(2,1)}, u32[]{:S(2)}) copy-start(bf16[768,256]{1,0:T(8,128)(2,1)} %constant.125.clone.right_table) | copy-start | bytes 1179652
  17.4 6.7 %copy-start.8 = (bf16[256,768]{1,0:T(8,128)(2,1)S(1)}, bf16[256,768]{1,0:T(8,128)(2,1)}, u32[]{:S(2)}) copy-start(bf16[256,768]{1,0:T(8,128)(2,1)} %constant.126.clone.left_table) | copy-start | bytes 1179652
  22.7 1.4 %copy-start.9 = (f32[4,4,2,128,128]{4,3,2,1,0:T(8,128)}, f32[4,4,2,128,128]{4,3,2,1,0:T(8,128)S(1)}, u32[]{:S(2)}) copy-start(f32[4,4,2,128,128]{4,3,2,1,0:T(8,128)S(1)} %get-tuple-element.14.psi) | copy-start | bytes 6291460
  24.1 10.7 %copy-start.1 = (f32[4,2,128,128]{3,2,1,0:T(8,128)S(1)}, f32[4,2,128,128]{3,2,1,0:T(8,128)}, u32[]{:S(2)}) copy-start(f32[4,2,128,128]{3,2,1,0:T(8,128)} %probe.3) | copy-start | bytes 1572868
  24.1 10.7 %copy-start.6 = (bf16[256,768]{1,0:T(8,128)(2,1)S(1)}, bf16[256,768]{1,0:T(8,128)(2,1)}, u32[]{:S(2)}) copy-start(bf16[256,768]{1,0:T(8,128)(2,1)} %constant.124.clone.left_table) | copy-start | bytes 1179652
  40.5 3.4 %collective-permute-start.12 = (f32[512,128]{1,0:T(8,128)S(1)}, f32[512,128]{1,0:T(8,128)S(1)}, u32[]{:S(2)}, u32[]{:S(2)}) collective-permute-start(f32[512,128]{1,0:T(8,128)S(1)} %constant_dynamic-slice_fusion.4), channel_id=1, source_target_pairs={{0,4},{4,0},{8,12},{12,8},{16,20},{20,16},{24,28},{28,24},{1,5},{5... | collective-permute-start | bytes 786440 | tf_op jit(solution)/shard_map/ppermute | solution.py:34
  44.0 6.1 %collective-permute-start.13 = (f32[256,128]{1,0:T(8,128)S(1)}, f32[256,128]{1,0:T(8,128)S(1)}, u32[]{:S(2)}, u32[]{:S(2)}) collective-permute-start(f32[256,128]{1,0:T(8,128)S(1)} %constant_dynamic-slice_fusion.3), channel_id=1, source_target_pairs={{0,8},{4,12},{8,0},{12,4},{16,24},{20,28},{24,16},{28,20},{1,9},{5... | collective-permute-start | bytes 393224 | tf_op jit(solution)/shard_map/ppermute | solution.py:34
  50.2 4.3 %collective-permute-start.14 = (f32[128,128]{1,0:T(8,128)S(1)}, f32[128,128]{1,0:T(8,128)S(1)}, u32[]{:S(2)}, u32[]{:S(2)}) collective-permute-start(f32[128,128]{1,0:T(8,128)S(1)} %constant_dynamic-slice_fusion.2), channel_id=1, source_target_pairs={{0,16},{4,20},{8,24},{12,28},{16,0},{20,4},{24,8},{28,12},{1,17},{... | collective-permute-start | bytes 196616 | tf_op jit(solution)/shard_map/ppermute | solution.py:34
  54.5 4.3 %collective-permute-start.15 = (f32[64,128]{1,0:T(8,128)S(1)}, f32[64,128]{1,0:T(8,128)S(1)}, u32[]{:S(2)}, u32[]{:S(2)}) collective-permute-start(f32[64,128]{1,0:T(8,128)S(1)} %constant_dynamic-slice_fusion.1), channel_id=1, source_target_pairs={{0,1},{1,0},{2,3},{3,2},{4,5},{5,4},{6,7},{7,6},{8,9},{9,8},{10,11... | collective-permute-start | bytes 98312 | tf_op jit(solution)/shard_map/ppermute | solution.py:34
  58.9 5.2 %collective-permute-start.16 = (f32[32,128]{1,0:T(8,128)S(1)}, f32[32,128]{1,0:T(8,128)S(1)}, u32[]{:S(2)}, u32[]{:S(2)}) collective-permute-start(f32[32,128]{1,0:T(8,128)S(1)} %constant_dynamic-slice_fusion), channel_id=1, source_target_pairs={{0,2},{1,3},{2,0},{3,1},{4,6},{5,7},{6,4},{7,5},{8,10},{9,11},{10,... | collective-permute-start | bytes 49160 | tf_op jit(solution)/shard_map/ppermute | solution.py:34
  64.0 4.7 %collective-permute-start.17 = (f32[32,128]{1,0:T(8,128)S(1)}, f32[32,128]{1,0:T(8,128)S(1)}, u32[]{:S(2)}, u32[]{:S(2)}) collective-permute-start(f32[32,128]{1,0:T(8,128)S(1)} %dynamic-slice_add_fusion.4), channel_id=1, source_target_pairs={{0,2},{1,3},{2,0},{3,1},{4,6},{5,7},{6,4},{7,5},{8,10},{9,11},{10,... | collective-permute-start | bytes 49160 | tf_op jit(solution)/shard_map/ppermute | solution.py:34
  68.8 4.0 %collective-permute-start.18 = (f32[64,128]{1,0:T(8,128)S(1)}, f32[64,128]{1,0:T(8,128)S(1)}, u32[]{:S(2)}, u32[]{:S(2)}) collective-permute-start(f32[64,128]{1,0:T(8,128)S(1)} %pad_maximum_fusion.5), channel_id=1, source_target_pairs={{0,1},{1,0},{2,3},{3,2},{4,5},{5,4},{6,7},{7,6},{8,9},{9,8},{10,11... | collective-permute-start | bytes 98312 | tf_op jit(solution)/shard_map/ppermute | solution.py:34
  72.8 13.5 %collective-permute-start.19 = (f32[128,128]{1,0:T(8,128)S(1)}, f32[128,128]{1,0:T(8,128)S(1)}, u32[]{:S(2)}, u32[]{:S(2)}) collective-permute-start(f32[128,128]{1,0:T(8,128)S(1)} %pad_maximum_fusion.4), channel_id=1, source_target_pairs={{0,16},{4,20},{8,24},{12,28},{16,0},{20,4},{24,8},{28,12},{1,17},{... | collective-permute-start | bytes 196616 | tf_op jit(solution)/shard_map/ppermute | solution.py:34
  75.0 15.8 %collective-permute-start.10 = (f32[2,128,128]{2,1,0:T(8,128)S(1)}, f32[2,128,128]{2,1,0:T(8,128)S(1)}, u32[]{:S(2)}, u32[]{:S(2)}) collective-permute-start(f32[2,128,128]{2,1,0:T(8,128)S(1)} %get-tuple-element.23), channel_id=1, source_target_pairs={{0,4},{4,8},{8,12},{12,16},{16,20},{20,24},{24,28},{1,5},{5,9},{9,... | collective-permute-start | bytes 393224 | tf_op jit(solution)/shard_map/ppermute | solution.py:18
  76.3 16.4 %collective-permute-start.11 = (f32[2,128,128]{2,1,0:T(8,128)S(1)}, f32[2,128,128]{2,1,0:T(8,128)S(1)}, u32[]{:S(2)}, u32[]{:S(2)}) collective-permute-start(f32[2,128,128]{2,1,0:T(8,128)S(1)} %get-tuple-element.24), channel_id=1, source_target_pairs={{0,5},{1,6},{2,7},{4,9},{5,10},{6,11},{8,13},{9,14},{10,15},{12,17... | collective-permute-start | bytes 393224 | tf_op jit(solution)/shard_map/ppermute | solution.py:29
  81.4 12.5 %collective-permute-start.9 = (f32[2,128,128]{2,1,0:T(8,128)S(1)}, f32[2,128,128]{2,1,0:T(8,128)S(1)}, u32[]{:S(2)}, u32[]{:S(2)}) collective-permute-start(f32[2,128,128]{2,1,0:T(8,128)S(1)} %get-tuple-element.22), channel_id=1, source_target_pairs={{0,1},{1,2},{2,3},{4,5},{5,6},{6,7},{8,9},{9,10},{10,11},{12,13},{... | collective-permute-start | bytes 393224 | tf_op jit(solution)/shard_map/ppermute | solution.py:18
  84.8 13.6 %collective-permute-start.7 = (f32[2,128,128]{2,1,0:T(8,128)S(1)}, f32[2,128,128]{2,1,0:T(8,128)S(1)}, u32[]{:S(2)}, u32[]{:S(2)}) collective-permute-start(f32[2,128,128]{2,1,0:T(8,128)S(1)} %get-tuple-element.19), channel_id=1, source_target_pairs={{0,4},{4,8},{8,12},{12,16},{16,20},{20,24},{24,28},{1,5},{5,9},{9,... | collective-permute-start | bytes 393224 | tf_op jit(solution)/shard_map/ppermute | solution.py:18
  86.3 12.2 %collective-permute-start.8 = (f32[2,128,128]{2,1,0:T(8,128)S(1)}, f32[2,128,128]{2,1,0:T(8,128)S(1)}, u32[]{:S(2)}, u32[]{:S(2)}) collective-permute-start(f32[2,128,128]{2,1,0:T(8,128)S(1)} %get-tuple-element.20), channel_id=1, source_target_pairs={{0,5},{1,6},{2,7},{4,9},{5,10},{6,11},{8,13},{9,14},{10,15},{12,17... | collective-permute-start | bytes 393224 | tf_op jit(solution)/shard_map/ppermute | solution.py:29
  90.8 7.7 %collective-permute-start.6 = (f32[2,128,128]{2,1,0:T(8,128)S(1)}, f32[2,128,128]{2,1,0:T(8,128)S(1)}, u32[]{:S(2)}, u32[]{:S(2)}) collective-permute-start(f32[2,128,128]{2,1,0:T(8,128)S(1)} %get-tuple-element.18), channel_id=1, source_target_pairs={{0,1},{1,2},{2,3},{4,5},{5,6},{6,7},{8,9},{9,10},{10,11},{12,13},{... | collective-permute-start | bytes 393224 | tf_op jit(solution)/shard_map/ppermute | solution.py:18
  92.7 5.5 %collective-permute-start.20 = (f32[256,128]{1,0:T(8,128)S(1)}, f32[256,128]{1,0:T(8,128)S(1)}, u32[]{:S(2)}, u32[]{:S(2)}) collective-permute-start(f32[256,128]{1,0:T(8,128)S(1)} %pad_maximum_fusion.3), channel_id=1, source_target_pairs={{0,8},{4,12},{8,0},{12,4},{16,24},{20,28},{24,16},{28,20},{1,9},{5... | collective-permute-start | bytes 393224 | tf_op jit(solution)/shard_map/ppermute | solution.py:34
  98.3 1.6 %collective-permute-start.21 = (f32[512,128]{1,0:T(8,128)S(1)}, f32[512,128]{1,0:T(8,128)S(1)}, u32[]{:S(2)}, u32[]{:S(2)}) collective-permute-start(f32[512,128]{1,0:T(8,128)S(1)} %pad_maximum_fusion.2), channel_id=1, source_target_pairs={{0,4},{4,0},{8,12},{12,8},{16,20},{20,16},{24,28},{28,24},{1,5},{5... | collective-permute-start | bytes 786440 | tf_op jit(solution)/shard_map/ppermute | solution.py:34
where the time goes:
time: 101 us
  starting transfers between devices  45.3 us (45%)
  waiting for transfers between devices  24.3 us (24%)
  Pallas kernels  21.5 us (21%)
  local copies, waits for them, and re-layouts  6.15 us (6%)
  other arithmetic  1.83 us (2%)
  between operations  1.66 us (2%)
    pallas_call x3, Pallas kernels, call(): pl.pallas_call(kernel, grid=(slots,), in_specs=in_specs, out_specs=out_sp...  21.5 us
    ppermute x10, waiting for transfers between devices, swapped(): return lax.ppermute(array, axis, [(i, i ^ bit) for i in range(length)])  20.7 us
    ppermute x10, starting transfers between devices, swapped(): return lax.ppermute(array, axis, [(i, i ^ bit) for i in range(length)])  19.9 us
    ppermute x8, starting transfers between devices, moved(): return lax.ppermute(array, axis, pairs)  13.3 us
    ppermute x4, starting transfers between devices, moved_both(): return lax.ppermute(array, ('ty', 'tx'), pairs)  12.1 us
    unnamed x20, local copies, waits for them, and re-layouts  5.09 us
    ppermute x4, waiting for transfers between devices, moved_both(): return lax.ppermute(array, ('ty', 'tx'), pairs)  2.38 us
  transfers between devices with their start and end apart: 22, of which 11 were waited for; matrix products, arithmetic and copies ran while one was open for 1% of the time, Pallas kernels for 5%

commit v1 on v0

v1 whole, which is shorter than its diff:
```python
import functools

import jax
import jax.numpy as jnp
import numpy as np
from jax import lax
from jax.experimental import pallas as pl
from jax.experimental.pallas import tpu as pltpu
from jax.sharding import PartitionSpec as P

BF16 = jnp.bfloat16
F32 = jnp.float32


def moved(array, axis, by):
    length = lax.axis_size(axis)
    pairs = [(i, i + by) for i in range(length) if 0 <= i + by < length]
    return lax.ppermute(array, axis, pairs)


def moved_both(array, rows_by, cols_by):
    rows, cols = lax.axis_size("ty"), lax.axis_size("tx")
    pairs = [
        (a * cols + b, (a + rows_by) * cols + b + cols_by)
        for a in range(rows)
        for b in range(cols)
        if 0 <= a + rows_by < rows and 0 <= b + cols_by < cols
    ]
    return lax.ppermute(array, ("ty", "tx"), pairs)


def swapped(array, axis, bit):
    length = lax.axis_size(axis)
    return lax.ppermute(array, axis, [(i, i ^ bit) for i in range(length)])


def picked(array, index):
    return lax.dynamic_index_in_dim(array, index, 0, keepdims=False)


def scattered(part, axis, unit, ways):
    me = (lax.axis_index(axis) // unit) % ways
    blocks = part.reshape(ways, -1, part.shape[-1])
    others = [swapped(picked(blocks, me ^ d), axis, d * unit) for d in range(1, ways)]
    return functools.reduce(jnp.add, others, picked(blocks, me))


def gathered(part, axis, unit, ways):
    me = (lax.axis_index(axis) // unit) % ways
    out = jnp.zeros((ways,) + part.shape, part.dtype)
    out = lax.dynamic_update_index_in_dim(out, part, me, 0)
    for d in range(1, ways):
        out = lax.dynamic_update_index_in_dim(out, swapped(part, axis, d * unit), me ^ d, 0)
    return out.reshape(-1, part.shape[-1])


def real_forms(table):
    right = np.block([[table.real, table.imag], [-table.imag, table.real]]).astype(np.float32)
    high = right.astype(BF16)
    low = (right - high.astype(np.float32)).astype(BF16)
    return (
        np.concatenate([high, high, low], axis=0),
        np.concatenate([high.T, high.T, low.T], axis=1),
    )


def tables(size):
    positions = np.arange(size)
    dft = np.exp(-2j * np.pi * (positions[:, None] * positions[None, :] % size) / size) / np.sqrt(size)
    freq = (positions + size // 2) % size - size // 2
    chirp = np.exp(-2j * np.pi * (freq * freq % (4 * size)) / (4 * size))
    through = dft.conj() @ (chirp[:, None] * dft)
    return real_forms(dft), real_forms(through)


def halves(x):
    high = x.astype(BF16)
    return high, (x - high.astype(F32)).astype(BF16)


def from_right(x, table):
    high, low = halves(x)
    return jnp.dot(jnp.concatenate([high, low, high], axis=1), table, preferred_element_type=F32)


def from_left(x, table):
    high, low = halves(x)
    return jnp.dot(table, jnp.concatenate([high, low, high], axis=0), preferred_element_type=F32)


def both_sides(fields, right_table, left_table):
    size = fields[0][0].shape[-1]
    done = []
    for first in range(0, len(fields), 2):
        pair = fields[first:first + 2]
        x = jnp.concatenate([jnp.concatenate(field, axis=1) for field in pair], axis=0)
        y = from_right(x, right_table)
        rows = [y[k * size:(k + 1) * size] for k in range(len(pair))]
        y = jnp.concatenate(
            [jnp.concatenate([r[:, :size], r[:, size:]], axis=0) for r in rows], axis=1
        )
        z = from_left(y, left_table)
        for k in range(len(pair)):
            lanes = slice(k * size, (k + 1) * size)
            done.append((z[:size, lanes], z[size:, lanes]))
    return done


def product(a, b):
    return (a[0] * b[0] - a[1] * b[1], a[0] * b[1] + a[1] * b[0])


def fill(wide, layer, own, right, down, corner, size):
    wide[:, :size, :size] = own[layer]
    wide[:, :size, size:] = right[...]
    wide[:, size:, :size] = down[layer]
    wide[:, size:, size:] = corner[...]


SUBLANES = 8


def window_of(wide, at, slot, size):
    row, col = at[0, slot], at[1, slot]
    shift = lax.rem(row, SUBLANES)
    rows = pl.ds(pl.multiple_of(row - shift, SUBLANES), size + SUBLANES)
    left = lax.rem(2 * size - col, 2 * size)
    up = lax.rem(size + SUBLANES - shift, size + SUBLANES)
    return [
        pltpu.roll(pltpu.roll(wide[c, rows, :], left, axis=1)[:, :size], up, axis=0)[:size]
        for c in range(2)
    ]


def add_window(total, at, slot, grads, size):
    row, col = at[0, slot], at[1, slot]
    shift = lax.rem(row, SUBLANES)
    rows = pl.ds(pl.multiple_of(row - shift, SUBLANES), size + SUBLANES)
    for c in range(2):
        taller = jnp.concatenate([grads[c], jnp.zeros((SUBLANES, size), F32)], axis=0)
        lowered = pltpu.roll(taller, shift, axis=0)
        padded = jnp.concatenate([lowered, jnp.zeros_like(lowered)], axis=1)
        total[c, rows, :] += pltpu.roll(padded, col, axis=1)


def stage_kernel(*refs):
    count = (len(refs) - 1) // 2
    sources, targets, sems = refs[:count], refs[count:2 * count], refs[-1]
    copies = [pltpu.make_async_copy(a, b, sems.at[i]) for i, (a, b) in enumerate(zip(sources, targets))]
    for copy in copies:
        copy.start()
    for copy in copies:
        copy.wait()


def first_kernel(at, own, right, down, corner, probe, right_table, left_table, psi, window, wide):
    size = own.shape[-1]
    slots, modes = psi.shape[:2]
    fill(wide, 0, own, right, down, corner, size)
    fields = []
    for slot in range(slots):
        w = window_of(wide, at, slot, size)
        window[slot, 0], window[slot, 1] = w
        fields += [product((probe[m, 0], probe[m, 1]), w) for m in range(modes)]
    waves = both_sides(fields, right_table[...], left_table[...])
    for i, wave in enumerate(waves):
        psi[i // modes, i % modes, 0], psi[i // modes, i % modes, 1] = wave


def second_kernel(at, count, own, right, down, corner, psi, window, probe, measured,
                  dft_right, dft_left, through_right, through_left,
                  g_probe, g_upper, g_lower, wide, total):
    size = own.shape[-1]
    slots, modes = psi.shape[:2]
    fill(wide, 1, own, right, down, corner, size)
    total[...] = jnp.zeros_like(total)
    w = [window_of(wide, at, slot, size) for slot in range(slots)]
    waves = [[(psi[s, m, 0], psi[s, m, 1]) for m in range(modes)] for s in range(slots)]
    fields = [product(waves[s][m], w[s]) for s in range(slots) for m in range(modes)]
    far = both_sides(fields, dft_right[...], dft_left[...])
    fields = []
    for s in range(slots):
        own_far = far[s * modes:(s + 1) * modes]
        intensity = sum(re * re + im * im for re, im in own_far)
        live = jnp.where(s < count[0], 2.0, 0.0).astype(F32)
        diff = (intensity - measured[s]) * live
        fields += [(re * diff, -(im * diff)) for re, im in own_far]
    conj = both_sides(fields, dft_right[...], dft_left[...])
    fields = [product(conj[s * modes + m], w[s]) for s in range(slots) for m in range(modes)]
    start = both_sides(fields, through_right[...], through_left[...])
    for m in range(modes):
        parts = [product(start[s * modes + m], (window[s, 0], window[s, 1])) for s in range(slots)]
        g_probe[m, 0] = sum(re for re, _ in parts)
        g_probe[m, 1] = -sum(im for _, im in parts)
    for s in range(slots):
        for layer, (grads, by) in enumerate((
            (start, [(probe[m, 0], probe[m, 1]) for m in range(modes)]),
            (conj, waves[s]),
        )):
            parts = [product(grads[s * modes + m], by[m]) for m in range(modes)]
            pair = (sum(re for re, _ in parts), -sum(im for _, im in parts))
            add_window(total.at[layer], at, s, pair, size)
    g_upper[...] = total[:, :, :size, :]
    g_lower[...] = total[:, :, size:, :]


VMEM = pl.BlockSpec(memory_space=pltpu.VMEM)
SMEM = pl.BlockSpec(memory_space=pltpu.SMEM)
HBM = pl.BlockSpec(memory_space=pl.ANY)


def call(kernel, args, in_specs, outs, scratch, flops):
    return pl.pallas_call(
        kernel,
        in_specs=in_specs,
        out_specs=[VMEM] * len(outs),
        out_shape=[jax.ShapeDtypeStruct(shape, dtype) for shape, dtype in outs],
        scratch_shapes=scratch,
        compiler_params=pltpu.CompilerParams(vmem_limit_bytes=40 * 1024 * 1024),
        cost_estimate=pl.CostEstimate(flops=flops, bytes_accessed=4 * 1024 * 1024, transcendentals=0),
    )(*args)


def on_device(object_slices, probe, measured, offsets, counts):
    layers, _, _, size = object_slices.shape
    slots = offsets.shape[-1]
    modes = probe.shape[0]
    at = offsets.reshape(2, slots)
    count = counts.reshape(1)
    (dft_right, dft_left), (through_right, through_left) = tables(size)
    flops = slots * modes * 2 * size * (2 * size) * (6 * size) * 2
    wide = pltpu.VMEM((2, 2 * size, 2 * size), F32)

    rights = [moved(object_slices[k], "tx", -1) for k in range(layers)]
    corners = [moved_both(object_slices[k], -1, -1) for k in range(layers)]
    downs = moved(object_slices, "ty", -1)

    early = (probe, jnp.asarray(through_right), jnp.asarray(through_left))
    early = call(
        stage_kernel, early, [HBM] * 3, [(a.shape, a.dtype) for a in early],
        [pltpu.SemaphoreType.DMA((3,))], flops,
    )
    psi, window = call(
        first_kernel,
        (at, object_slices, rights[0], downs, corners[0], *early),
        [SMEM] + [VMEM] * 7,
        [((slots, modes, 2, size, size), F32), ((slots, 2, size, size), F32)],
        [wide], flops,
    )
    g_probe, g_upper, g_lower = call(
        second_kernel,
        (at, count, object_slices, rights[1], downs, corners[1], psi, window, early[0],
         measured.reshape(slots, size, size), dft_right, dft_left, early[1], early[2]),
        [SMEM] * 2 + [VMEM] * 12,
        [(probe.shape, F32)] + [((layers, 2, size, 2 * size), F32)] * 2,
        [wide, pltpu.VMEM((layers, 2, 2 * size, 2 * size), F32)], 3 * flops,
    )

    rows = lax.axis_size("ty")
    part = scattered(g_probe.reshape(-1, size), "ty", 1, 2)
    part = scattered(part, "ty", 2, rows // 2)
    part, g_lower = lax.optimization_barrier((part, g_lower))
    from_above = moved(g_lower, "ty", 1)
    bit = 1
    while bit < lax.axis_size("tx"):
        part = part + swapped(part, "tx", bit)
        bit *= 2
    g_wide = g_upper + from_above
    g_right, part = lax.optimization_barrier((g_wide[..., size:], part))
    from_left_tile = moved(g_right, "tx", 1)
    part = gathered(part, "ty", 2, rows // 2)
    part = gathered(part, "ty", 1, 2)
    object_grad = g_wide[..., :size] + from_left_tile
    return object_grad, part.reshape(probe.shape)


def solution(mesh):
    in_specs = (
        P(None, None, "ty", "tx"),
        P(),
        P("ty", "tx", None, None, None),
        P(None, "ty", "tx", None),
        P("ty", "tx"),
    )
    out_specs = (P(None, None, "ty", "tx"), P())
    return jax.shard_map(
        on_device, mesh=mesh, in_specs=in_specs, out_specs=out_specs, check_vma=False
    )
```

time: 101 us -> 67.3 us (0.67)
  starting transfers between devices: 45.3 us -> 26.4 us
  Pallas kernels: 21.5 us -> 11.7 us
  waiting for transfers between devices: 24.3 us -> 21.3 us
  local copies, waits for them, and re-layouts: 6.15 us -> 5.04 us
    pallas_call x3, Pallas kernels: 21.5 us -> 11.7 us  [call(): pl.pallas_call(kernel, in_specs=in_specs, out_specs=[VMEM] * len(outs), o...]
    ppermute x4 -> x2, starting transfers between devices: 12.1 us -> 2.58 us  [moved_both(): return lax.ppermute(array, ('ty', 'tx'), pairs)]
    ppermute x10, waiting for transfers between devices: 20.7 us -> 12.6 us  [swapped(): return lax.ppermute(array, axis, [(i, i ^ bit) for i in range(length)])]
    ppermute x8 -> x5, starting transfers between devices: 13.3 us -> 7.51 us  [moved(): return lax.ppermute(array, axis, pairs)]
    ppermute x8 -> x5, waiting for transfers between devices: 1.27 us -> 6.4 us  [moved(): return lax.ppermute(array, axis, pairs)]
    ppermute x10, starting transfers between devices: 19.9 us -> 16.3 us  [swapped(): return lax.ppermute(array, axis, [(i, i ^ bit) for i in range(length)])]
    unnamed x20 -> x18, local copies, waits for them, and re-layouts: 5.09 us -> 3.84 us
    ppermute x4 -> x2, waiting for transfers between devices: 2.38 us -> 2.33 us  [moved_both(): return lax.ppermute(array, ('ty', 'tx'), pairs)]
  transfers between devices with their start and end apart: 22 -> 17, of which waited for: 11 -> 11; matrix products, arithmetic and copies ran while one was open for 1% -> 3% of each run, Pallas kernels for 5% -> 5%
where the time goes in v1:
time: 67.3 us; the launch traced here: 66.9 us
  starting transfers between devices  26.4 us (39%)
  waiting for transfers between devices  21.3 us (32%)
  Pallas kernels  11.7 us (17%)
  local copies, waits for them, and re-layouts  5.04 us (7%)
  between operations  1.6 us (2%)
  other arithmetic  0.86 us (1%)
    ppermute x10, starting transfers between devices, swapped(): return lax.ppermute(array, axis, [(i, i ^ bit) for i in range(length)])  16.3 us
    ppermute x10, waiting for transfers between devices, swapped(): return lax.ppermute(array, axis, [(i, i ^ bit) for i in range(length)])  12.6 us
    pallas_call x3, Pallas kernels, call(): pl.pallas_call(kernel, in_specs=in_specs, out_specs=[VMEM] * len(outs), o...  11.7 us
    ppermute x5, starting transfers between devices, moved(): return lax.ppermute(array, axis, pairs)  7.51 us
    ppermute x5, waiting for transfers between devices, moved(): return lax.ppermute(array, axis, pairs)  6.4 us
    unnamed x18, local copies, waits for them, and re-layouts  3.84 us
    ppermute x2, starting transfers between devices, moved_both(): return lax.ppermute(array, ('ty', 'tx'), pairs)  2.58 us
    ppermute x2, waiting for transfers between devices, moved_both(): return lax.ppermute(array, ('ty', 'tx'), pairs)  2.33 us
  transfers between devices with their start and end apart: 17, of which 11 were waited for; matrix products, arithmetic and copies ran while one was open for 3% of the time, Pallas kernels for 5%

profile of v1, /device:TPU:0, one launch (start us, length us, event | category | flops | bytes accessed | tf_op | source)
XLA Modules:
  0.0 66.9 jit_solution(4950408746593028307)
XLA Ops:
  0.6 1.3 %collective-permute-start.1 = (f32[2,2,128,128]{3,2,1,0:T(8,128)}, f32[2,2,128,128]{3,2,1,0:T(8,128)S(1)}, u32[]{:S(2)}, u32[]{:S(2)}) collective-permute-start(f32[2,2,128,128]{3,2,1,0:T(8,128)} %own.3), channel_id=1, source_target_pairs={{4,0},{8,4},{12,8},{16,12},{20,16},{24,20},{28,24},{5,1},{9,5},{13... | collective-permute-start | bytes 786440 | tf_op jit(solution)/shard_map/ppermute | solution.py:18
  1.9 1.0 %slice_bitcast_fusion = (f32[2,128,128]{2,1,0:T(8,128)S(1)}, f32[2,128,128]{2,1,0:T(8,128)S(1)}) fusion(f32[2,2,128,128]{3,2,1,0:T(8,128)} %own.3), kind=kLoop, calls=%fused_computation.5 | loop fusion | bytes 524288 | tf_op jit(solution)/shard_map/squeeze | solution.py:234
  2.9 1.3 %collective-permute-start = (f32[2,128,128]{2,1,0:T(8,128)S(1)}, f32[2,128,128]{2,1,0:T(8,128)S(1)}, u32[]{:S(2)}, u32[]{:S(2)}) collective-permute-start(f32[2,128,128]{2,1,0:T(8,128)S(1)} %get-tuple-element.30), channel_id=1, source_target_pairs={{1,0},{2,1},{3,2},{5,4},{6,5},{7,6},{9,8},{10,9},{11,10},{13,12},{... | collective-permute-start | bytes 393224 | tf_op jit(solution)/shard_map/ppermute | solution.py:18
  4.2 1.3 %collective-permute-start.2 = (f32[2,128,128]{2,1,0:T(8,128)S(1)}, f32[2,128,128]{2,1,0:T(8,128)S(1)}, u32[]{:S(2)}, u32[]{:S(2)}) collective-permute-start(f32[2,128,128]{2,1,0:T(8,128)S(1)} %get-tuple-element.30), channel_id=1, source_target_pairs={{5,0},{6,1},{7,2},{9,4},{10,5},{11,6},{13,8},{14,9},{15,10},{17,12... | collective-permute-start | bytes 393224 | tf_op jit(solution)/shard_map/ppermute | solution.py:29
  5.5 1.3 %collective-permute-start.3 = (f32[2,128,128]{2,1,0:T(8,128)S(1)}, f32[2,128,128]{2,1,0:T(8,128)S(1)}, u32[]{:S(2)}, u32[]{:S(2)}) collective-permute-start(f32[2,128,128]{2,1,0:T(8,128)S(1)} %get-tuple-element.29), channel_id=1, source_target_pairs={{1,0},{2,1},{3,2},{5,4},{6,5},{7,6},{9,8},{10,9},{11,10},{13,12},{... | collective-permute-start | bytes 393224 | tf_op jit(solution)/shard_map/ppermute | solution.py:18
  6.8 1.3 %collective-permute-start.4 = (f32[2,128,128]{2,1,0:T(8,128)S(1)}, f32[2,128,128]{2,1,0:T(8,128)S(1)}, u32[]{:S(2)}, u32[]{:S(2)}) collective-permute-start(f32[2,128,128]{2,1,0:T(8,128)S(1)} %get-tuple-element.29), channel_id=1, source_target_pairs={{5,0},{6,1},{7,2},{9,4},{10,5},{11,6},{13,8},{14,9},{15,10},{17,12... | collective-permute-start | bytes 393224 | tf_op jit(solution)/shard_map/ppermute | solution.py:29
  8.8 1.0 %copy-done.1 = f32[4,2,128,128]{3,2,1,0:T(8,128)S(1)} copy-done((f32[4,2,128,128]{3,2,1,0:T(8,128)S(1)}, f32[4,2,128,128]{3,2,1,0:T(8,128)}, u32[]{:S(2)}) %copy-start.1) | copy-done | bytes 524312
  9.8 1.0 %copy-done.6 = bf16[768,256]{1,0:T(8,128)(2,1)S(1)} copy-done((bf16[768,256]{1,0:T(8,128)(2,1)S(1)}, bf16[768,256]{1,0:T(8,128)(2,1)}, u32[]{:S(2)}) %copy-start.6) | copy-done | bytes 393240
  10.8 1.0 %copy-done.7 = bf16[256,768]{1,0:T(8,128)(2,1)S(1)} copy-done((bf16[256,768]{1,0:T(8,128)(2,1)S(1)}, bf16[256,768]{1,0:T(8,128)(2,1)}, u32[]{:S(2)}) %copy-start.7) | copy-done | bytes 393240
  12.3 3.2 %collective-permute-done.3.right = f32[2,128,128]{2,1,0:T(8,128)S(1)} collective-permute-done((f32[2,128,128]{2,1,0:T(8,128)S(1)}, f32[2,128,128]{2,1,0:T(8,128)S(1)}, u32[]{:S(2)}, u32[]{:S(2)}) %collective-permute-start.3) | collective-permute-done | bytes 131104 | tf_op jit(solution)/shard_map/ppermute | solution.py:18
  15.5 2.3 %collective-permute-done.4.corner = f32[2,128,128]{2,1,0:T(8,128)S(1)} collective-permute-done((f32[2,128,128]{2,1,0:T(8,128)S(1)}, f32[2,128,128]{2,1,0:T(8,128)S(1)}, u32[]{:S(2)}, u32[]{:S(2)}) %collective-permute-start.4) | collective-permute-done | bytes 131104 | tf_op jit(solution)/shard_map/ppermute | solution.py:29
  17.9 3.0 %shard_map.105 = (f32[4,4,2,128,128]{4,3,2,1,0:T(8,128)S(1)}, f32[4,2,128,128]{3,2,1,0:T(8,128)S(1)}) custom-call(s32[2,4]{1,0:T(2,128)S(1)} %bitcast.44, f32[2,2,128,128]{3,2,1,0:T(8,128)S(1)} %copy-done, f32[2,128,128]{2,1,0:T(8,128)S(1)} %collective-permute-done.3.right, f32[2,2,128,128]{3,2,1,0:T(8,128)S(1)} %collective-permute-done.1.down, ...), custom_call_target="tpu_custom_call" | custom-call | flops 1610612736 | bytes 4194304 | tf_op jit(solution)/shard_map/pallas_call | solution.py:213
  21.0 8.2 %shard_map.106 = (f32[4,2,128,128]{3,2,1,0:T(8,128)S(1)}, f32[2,2,128,256]{3,2,1,0:T(8,128)S(1)}, f32[2,2,128,256]{3,2,1,0:T(8,128)S(1)}) custom-call(s32[2,4]{1,0:T(2,128)S(1)} %bitcast.45, s32[1]{0:T(128)} %bitcast.40.count, f32[2,2,128,128]{3,2,1,0:T(8,128)S(1)} %copy-done, f32[2,128,128]{2,1,0:T(8,128)S(1)} %collective-permute-done.right, ...), custom_call_target="tpu_custom_call" | custom-call | flops 4831838208 | bytes 4194304 | tf_op jit(solution)/shard_map/pallas_call | solution.py:213
  29.2 4.2 %collective-permute-start.5 = (f32[512,128]{1,0:T(8,128)S(1)}, f32[512,128]{1,0:T(8,128)S(1)}, u32[]{:S(2)}, u32[]{:S(2)}) collective-permute-start(f32[512,128]{1,0:T(8,128)S(1)} %dynamic-slice_bitcast_fusion), channel_id=1, source_target_pairs={{0,4},{4,0},{8,12},{12,8},{16,20},{20,16},{24,28},{28,24},{1,5},{5... | collective-permute-start | bytes 786440 | tf_op jit(solution)/shard_map/ppermute | solution.py:34
  33.5 1.2 %collective-permute-done.5 = f32[512,128]{1,0:T(8,128)S(1)} collective-permute-done((f32[512,128]{1,0:T(8,128)S(1)}, f32[512,128]{1,0:T(8,128)S(1)}, u32[]{:S(2)}, u32[]{:S(2)}) %collective-permute-start.5) | collective-permute-done | bytes 262176 | tf_op jit(solution)/shard_map/ppermute | solution.py:34
  34.7 1.7 %collective-permute-start.8 = (f32[128,128]{1,0:T(8,128)S(1)}, f32[128,128]{1,0:T(8,128)S(1)}, u32[]{:S(2)}, u32[]{:S(2)}) collective-permute-start(f32[128,128]{1,0:T(8,128)S(1)} %get-tuple-element.27), channel_id=1, source_target_pairs={{0,24},{4,28},{8,16},{12,20},{16,8},{20,12},{24,0},{28,4},{1,25},{... | collective-permute-start | bytes 196616 | tf_op jit(solution)/shard_map/ppermute | solution.py:34
  36.4 1.3 %collective-permute-start.7 = (f32[128,128]{1,0:T(8,128)S(1)}, f32[128,128]{1,0:T(8,128)S(1)}, u32[]{:S(2)}, u32[]{:S(2)}) collective-permute-start(f32[128,128]{1,0:T(8,128)S(1)} %get-tuple-element.28), channel_id=1, source_target_pairs={{0,16},{4,20},{8,24},{12,28},{16,0},{20,4},{24,8},{28,12},{1,17},{... | collective-permute-start | bytes 196616 | tf_op jit(solution)/shard_map/ppermute | solution.py:34
  38.3 1.9 %collective-permute-done.8 = f32[128,128]{1,0:T(8,128)S(1)} collective-permute-done((f32[128,128]{1,0:T(8,128)S(1)}, f32[128,128]{1,0:T(8,128)S(1)}, u32[]{:S(2)}, u32[]{:S(2)}) %collective-permute-start.8) | collective-permute-done | bytes 65568 | tf_op jit(solution)/shard_map/ppermute | solution.py:34
  40.1 1.3 %collective-permute-done.7 = f32[128,128]{1,0:T(8,128)S(1)} collective-permute-done((f32[128,128]{1,0:T(8,128)S(1)}, f32[128,128]{1,0:T(8,128)S(1)}, u32[]{:S(2)}, u32[]{:S(2)}) %collective-permute-start.7) | collective-permute-done | bytes 65568 | tf_op jit(solution)/shard_map/ppermute | solution.py:34
  41.4 0.6 collective-permute-done.6
  42.0 1.4 %collective-permute-start.9 = (f32[2,2,128,256]{3,2,1,0:T(8,128)S(1)}, f32[2,2,128,256]{3,2,1,0:T(8,128)S(1)}, u32[]{:S(2)}, u32[]{:S(2)}) collective-permute-start(f32[2,2,128,256]{3,2,1,0:T(8,128)S(1)} %get-tuple-element.22), channel_id=1, source_target_pairs={{0,4},{4,8},{8,12},{12,16},{16,20},{20,24},{24,28},{1,5},{5,9},{9,... | collective-permute-start | bytes 1572872 | tf_op jit(solution)/shard_map/ppermute | solution.py:18
  43.4 1.9 %collective-permute-start.10 = (f32[128,128]{1,0:T(8,128)S(1)}, f32[128,128]{1,0:T(8,128)S(1)}, u32[]{:S(2)}, u32[]{:S(2)}) collective-permute-start(f32[128,128]{1,0:T(8,128)S(1)} %fusion.1), channel_id=1, source_target_pairs={{0,1},{1,0},{2,3},{3,2},{4,5},{5,4},{6,7},{7,6},{8,9},{9,8},{10,11... | collective-permute-start | bytes 196616 | tf_op jit(solution)/shard_map/ppermute | solution.py:34
  45.3 2.4 %collective-permute-done.10 = f32[128,128]{1,0:T(8,128)S(1)} collective-permute-done((f32[128,128]{1,0:T(8,128)S(1)}, f32[128,128]{1,0:T(8,128)S(1)}, u32[]{:S(2)}, u32[]{:S(2)}) %collective-permute-start.10) | collective-permute-done | bytes 65568 | tf_op jit(solution)/shard_map/ppermute | solution.py:34
  47.8 3.0 %collective-permute-start.11 = (f32[128,128]{1,0:T(8,128)S(1)}, f32[128,128]{1,0:T(8,128)S(1)}, u32[]{:S(2)}, u32[]{:S(2)}) collective-permute-start(f32[128,128]{1,0:T(8,128)S(1)} %add.76), channel_id=1, source_target_pairs={{0,2},{1,3},{2,0},{3,1},{4,6},{5,7},{6,4},{7,5},{8,10},{9,11},{10,... | collective-permute-start | bytes 196616 | tf_op jit(solution)/shard_map/ppermute | solution.py:34
  50.8 4.1 %collective-permute-done.11 = f32[128,128]{1,0:T(8,128)S(1)} collective-permute-done((f32[128,128]{1,0:T(8,128)S(1)}, f32[128,128]{1,0:T(8,128)S(1)}, u32[]{:S(2)}, u32[]{:S(2)}) %collective-permute-start.11) | collective-permute-done | bytes 65568 | tf_op jit(solution)/shard_map/ppermute | solution.py:34
  55.0 1.9 %collective-permute-start.13 = (f32[128,128]{1,0:T(8,128)S(1)}, f32[128,128]{1,0:T(8,128)S(1)}, u32[]{:S(2)}, u32[]{:S(2)}) collective-permute-start(f32[128,128]{1,0:T(8,128)S(1)} %add.77), channel_id=1, source_target_pairs={{0,8},{4,12},{8,0},{12,4},{16,24},{20,28},{24,16},{28,20},{1,9},{5... | collective-permute-start | bytes 196616 | tf_op jit(solution)/shard_map/ppermute | solution.py:34
  56.8 1.7 %collective-permute-start.15 = (f32[128,128]{1,0:T(8,128)S(1)}, f32[128,128]{1,0:T(8,128)S(1)}, u32[]{:S(2)}, u32[]{:S(2)}) collective-permute-start(f32[128,128]{1,0:T(8,128)S(1)} %add.77), channel_id=1, source_target_pairs={{0,24},{4,28},{8,16},{12,20},{16,8},{20,12},{24,0},{28,4},{1,25},{... | collective-permute-start | bytes 196616 | tf_op jit(solution)/shard_map/ppermute | solution.py:34
  58.5 2.2 %collective-permute-start.12 = (f32[2,2,128,128]{3,2,1,0:T(8,128)S(1)}, f32[2,2,128,128]{3,2,1,0:T(8,128)S(1)}, u32[]{:S(2)}, u32[]{:S(2)}) collective-permute-start(f32[2,2,128,128]{3,2,1,0:T(8,128)S(1)} %slice.19), channel_id=1, source_target_pairs={{0,1},{1,2},{2,3},{4,5},{5,6},{6,7},{8,9},{9,10},{10,11},{12,13},{... | collective-permute-start | bytes 786440 | tf_op jit(solution)/shard_map/ppermute | solution.py:18
  61.1 0.9 %collective-permute-done.15 = f32[128,128]{1,0:T(8,128)S(1)} collective-permute-done((f32[128,128]{1,0:T(8,128)S(1)}, f32[128,128]{1,0:T(8,128)S(1)}, u32[]{:S(2)}, u32[]{:S(2)}) %collective-permute-start.15) | collective-permute-done | bytes 65568 | tf_op jit(solution)/shard_map/ppermute | solution.py:34
  62.2 3.2 %collective-permute-done.12 = f32[2,2,128,128]{3,2,1,0:T(8,128)S(1)} collective-permute-done((f32[2,2,128,128]{3,2,1,0:T(8,128)S(1)}, f32[2,2,128,128]{3,2,1,0:T(8,128)S(1)}, u32[]{:S(2)}, u32[]{:S(2)}) %collective-permute-start.12) | collective-permute-done | bytes 262176 | tf_op jit(solution)/shard_map/ppermute | solution.py:18
  65.4 0.7 %slice_add_fusion = f32[2,2,128,128]{3,2,1,0:T(8,128)} fusion(f32[2,2,128,128]{3,2,1,0:T(8,128)S(1)} %collective-permute-done.12, f32[2,2,128,256]{3,2,1,0:T(8,128)S(1)} %add.75), kind=kLoop, calls=%fused_computation | loop fusion | flops 65536 | bytes 786432 | tf_op jit(solution)/shard_map/add | solution.py:273
  66.1 0.8 %copy-done.8 = f32[2,512,128]{2,1,0:T(8,128)} copy-done((f32[2,512,128]{2,1,0:T(8,128)}, f32[2,512,128]{2,1,0:T(8,128)S(1)}, u32[]{:S(2)}) %copy-start.8) | copy-done | bytes 524312
  (41 shorter events, 1.7 us)
Async XLA Ops:
  0.6 17.2 %collective-permute-start.1 = (f32[2,2,128,128]{3,2,1,0:T(8,128)}, f32[2,2,128,128]{3,2,1,0:T(8,128)S(1)}, u32[]{:S(2)}, u32[]{:S(2)}) collective-permute-start(f32[2,2,128,128]{3,2,1,0:T(8,128)} %own.3), channel_id=1, source_target_pairs={{4,0},{8,4},{12,8},{16,12},{20,16},{24,20},{28,24},{5,1},{9,5},{13... | collective-permute-start | bytes 786440 | tf_op jit(solution)/shard_map/ppermute | solution.py:18
  2.9 18.0 %collective-permute-start = (f32[2,128,128]{2,1,0:T(8,128)S(1)}, f32[2,128,128]{2,1,0:T(8,128)S(1)}, u32[]{:S(2)}, u32[]{:S(2)}) collective-permute-start(f32[2,128,128]{2,1,0:T(8,128)S(1)} %get-tuple-element.30), channel_id=1, source_target_pairs={{1,0},{2,1},{3,2},{5,4},{6,5},{7,6},{9,8},{10,9},{11,10},{13,12},{... | collective-permute-start | bytes 393224 | tf_op jit(solution)/shard_map/ppermute | solution.py:18
  4.2 16.7 %collective-permute-start.2 = (f32[2,128,128]{2,1,0:T(8,128)S(1)}, f32[2,128,128]{2,1,0:T(8,128)S(1)}, u32[]{:S(2)}, u32[]{:S(2)}) collective-permute-start(f32[2,128,128]{2,1,0:T(8,128)S(1)} %get-tuple-element.30), channel_id=1, source_target_pairs={{5,0},{6,1},{7,2},{9,4},{10,5},{11,6},{13,8},{14,9},{15,10},{17,12... | collective-permute-start | bytes 393224 | tf_op jit(solution)/shard_map/ppermute | solution.py:29
  5.5 10.0 %collective-permute-start.3 = (f32[2,128,128]{2,1,0:T(8,128)S(1)}, f32[2,128,128]{2,1,0:T(8,128)S(1)}, u32[]{:S(2)}, u32[]{:S(2)}) collective-permute-start(f32[2,128,128]{2,1,0:T(8,128)S(1)} %get-tuple-element.29), channel_id=1, source_target_pairs={{1,0},{2,1},{3,2},{5,4},{6,5},{7,6},{9,8},{10,9},{11,10},{13,12},{... | collective-permute-start | bytes 393224 | tf_op jit(solution)/shard_map/ppermute | solution.py:18
  6.8 11.0 %collective-permute-start.4 = (f32[2,128,128]{2,1,0:T(8,128)S(1)}, f32[2,128,128]{2,1,0:T(8,128)S(1)}, u32[]{:S(2)}, u32[]{:S(2)}) collective-permute-start(f32[2,128,128]{2,1,0:T(8,128)S(1)} %get-tuple-element.29), channel_id=1, source_target_pairs={{5,0},{6,1},{7,2},{9,4},{10,5},{11,6},{13,8},{14,9},{15,10},{17,12... | collective-permute-start | bytes 393224 | tf_op jit(solution)/shard_map/ppermute | solution.py:29
  8.8 1.0 %copy-start.1 = (f32[4,2,128,128]{3,2,1,0:T(8,128)S(1)}, f32[4,2,128,128]{3,2,1,0:T(8,128)}, u32[]{:S(2)}) copy-start(f32[4,2,128,128]{3,2,1,0:T(8,128)} %refs_0_.1) | copy-start | bytes 1572868
  9.8 1.0 %copy-start.6 = (bf16[768,256]{1,0:T(8,128)(2,1)S(1)}, bf16[768,256]{1,0:T(8,128)(2,1)}, u32[]{:S(2)}) copy-start(bf16[768,256]{1,0:T(8,128)(2,1)} %constant.101.clone.refs_1_) | copy-start | bytes 1179652
  10.8 1.0 %copy-start.7 = (bf16[256,768]{1,0:T(8,128)(2,1)S(1)}, bf16[256,768]{1,0:T(8,128)(2,1)}, u32[]{:S(2)}) copy-start(bf16[256,768]{1,0:T(8,128)(2,1)} %constant.102.clone.refs_2_) | copy-start | bytes 1179652
  11.8 6.0 %copy-start = (f32[2,2,128,128]{3,2,1,0:T(8,128)S(1)}, f32[2,2,128,128]{3,2,1,0:T(8,128)}, u32[]{:S(2)}) copy-start(f32[2,2,128,128]{3,2,1,0:T(8,128)} %own.3) | copy-start | bytes 786436
  11.8 6.0 %copy-start.3 = (s32[2,1,1,4]{3,2,1,0:T(1,128)S(1)}, s32[2,1,1,4]{3,2,1,0:T(1,128)}, u32[]{:S(2)}) copy-start(s32[2,1,1,4]{3,2,1,0:T(1,128)} %param.12) | copy-start | bytes 100
  17.8 3.1 %copy-start.2 = (f32[1,1,4,128,128]{4,3,2,1,0:T(8,128)S(1)}, f32[1,1,4,128,128]{4,3,2,1,0:T(8,128)}, u32[]{:S(2)}) copy-start(f32[1,1,4,128,128]{4,3,2,1,0:T(8,128)} %param.11) | copy-start | bytes 786436
  17.8 3.1 %copy-start.4 = (bf16[768,256]{1,0:T(8,128)(2,1)S(1)}, bf16[768,256]{1,0:T(8,128)(2,1)}, u32[]{:S(2)}) copy-start(bf16[768,256]{1,0:T(8,128)(2,1)} %constant.103.clone.dft_right) | copy-start | bytes 1179652
  17.9 3.1 %copy-start.5 = (bf16[256,768]{1,0:T(8,128)(2,1)S(1)}, bf16[256,768]{1,0:T(8,128)(2,1)}, u32[]{:S(2)}) copy-start(bf16[256,768]{1,0:T(8,128)(2,1)} %constant.104.clone.dft_left) | copy-start | bytes 1179652
  29.2 5.4 %collective-permute-start.5 = (f32[512,128]{1,0:T(8,128)S(1)}, f32[512,128]{1,0:T(8,128)S(1)}, u32[]{:S(2)}, u32[]{:S(2)}) collective-permute-start(f32[512,128]{1,0:T(8,128)S(1)} %dynamic-slice_bitcast_fusion), channel_id=1, source_target_pairs={{0,4},{4,0},{8,12},{12,8},{16,20},{20,16},{24,28},{28,24},{1,5},{5... | collective-permute-start | bytes 786440 | tf_op jit(solution)/shard_map/ppermute | solution.py:34
  34.7 5.4 %collective-permute-start.8 = (f32[128,128]{1,0:T(8,128)S(1)}, f32[128,128]{1,0:T(8,128)S(1)}, u32[]{:S(2)}, u32[]{:S(2)}) collective-permute-start(f32[128,128]{1,0:T(8,128)S(1)} %get-tuple-element.27), channel_id=1, source_target_pairs={{0,24},{4,28},{8,16},{12,20},{16,8},{20,12},{24,0},{28,4},{1,25},{... | collective-permute-start | bytes 196616 | tf_op jit(solution)/shard_map/ppermute | solution.py:34
  36.4 5.0 %collective-permute-start.7 = (f32[128,128]{1,0:T(8,128)S(1)}, f32[128,128]{1,0:T(8,128)S(1)}, u32[]{:S(2)}, u32[]{:S(2)}) collective-permute-start(f32[128,128]{1,0:T(8,128)S(1)} %get-tuple-element.28), channel_id=1, source_target_pairs={{0,16},{4,20},{8,24},{12,28},{16,0},{20,4},{24,8},{28,12},{1,17},{... | collective-permute-start | bytes 196616 | tf_op jit(solution)/shard_map/ppermute | solution.py:34
  37.7 4.3 %collective-permute-start.6 = (f32[128,128]{1,0:T(8,128)S(1)}, f32[128,128]{1,0:T(8,128)S(1)}, u32[]{:S(2)}, u32[]{:S(2)}) collective-permute-start(f32[128,128]{1,0:T(8,128)S(1)} %get-tuple-element.26), channel_id=1, source_target_pairs={{0,8},{4,12},{8,0},{12,4},{16,24},{20,28},{24,16},{28,20},{1,9},{5... | collective-permute-start | bytes 196616 | tf_op jit(solution)/shard_map/ppermute | solution.py:34
  42.0 12.8 %collective-permute-start.9 = (f32[2,2,128,256]{3,2,1,0:T(8,128)S(1)}, f32[2,2,128,256]{3,2,1,0:T(8,128)S(1)}, u32[]{:S(2)}, u32[]{:S(2)}) collective-permute-start(f32[2,2,128,256]{3,2,1,0:T(8,128)S(1)} %get-tuple-element.22), channel_id=1, source_target_pairs={{0,4},{4,8},{8,12},{12,16},{16,20},{20,24},{24,28},{1,5},{5,9},{9,... | collective-permute-start | bytes 1572872 | tf_op jit(solution)/shard_map/ppermute | solution.py:18
  43.4 4.3 %collective-permute-start.10 = (f32[128,128]{1,0:T(8,128)S(1)}, f32[128,128]{1,0:T(8,128)S(1)}, u32[]{:S(2)}, u32[]{:S(2)}) collective-permute-start(f32[128,128]{1,0:T(8,128)S(1)} %fusion.1), channel_id=1, source_target_pairs={{0,1},{1,0},{2,3},{3,2},{4,5},{5,4},{6,7},{7,6},{8,9},{9,8},{10,11... | collective-permute-start | bytes 196616 | tf_op jit(solution)/shard_map/ppermute | solution.py:34
  47.8 7.1 %collective-permute-start.11 = (f32[128,128]{1,0:T(8,128)S(1)}, f32[128,128]{1,0:T(8,128)S(1)}, u32[]{:S(2)}, u32[]{:S(2)}) collective-permute-start(f32[128,128]{1,0:T(8,128)S(1)} %add.76), channel_id=1, source_target_pairs={{0,2},{1,3},{2,0},{3,1},{4,6},{5,7},{6,4},{7,5},{8,10},{9,11},{10,... | collective-permute-start | bytes 196616 | tf_op jit(solution)/shard_map/ppermute | solution.py:34
  55.0 5.8 %collective-permute-start.13 = (f32[128,128]{1,0:T(8,128)S(1)}, f32[128,128]{1,0:T(8,128)S(1)}, u32[]{:S(2)}, u32[]{:S(2)}) collective-permute-start(f32[128,128]{1,0:T(8,128)S(1)} %add.77), channel_id=1, source_target_pairs={{0,8},{4,12},{8,0},{12,4},{16,24},{20,28},{24,16},{28,20},{1,9},{5... | collective-permute-start | bytes 196616 | tf_op jit(solution)/shard_map/ppermute | solution.py:34
  56.8 4.3 %collective-permute-start.14 = (f32[128,128]{1,0:T(8,128)S(1)}, f32[128,128]{1,0:T(8,128)S(1)}, u32[]{:S(2)}, u32[]{:S(2)}) collective-permute-start(f32[128,128]{1,0:T(8,128)S(1)} %add.77), channel_id=1, source_target_pairs={{0,16},{4,20},{8,24},{12,28},{16,0},{20,4},{24,8},{28,12},{1,17},{... | collective-permute-start | bytes 196616 | tf_op jit(solution)/shard_map/ppermute | solution.py:34
  56.8 5.2 %collective-permute-start.15 = (f32[128,128]{1,0:T(8,128)S(1)}, f32[128,128]{1,0:T(8,128)S(1)}, u32[]{:S(2)}, u32[]{:S(2)}) collective-permute-start(f32[128,128]{1,0:T(8,128)S(1)} %add.77), channel_id=1, source_target_pairs={{0,24},{4,28},{8,16},{12,20},{16,8},{20,12},{24,0},{28,4},{1,25},{... | collective-permute-start | bytes 196616 | tf_op jit(solution)/shard_map/ppermute | solution.py:34
  58.5 6.8 %collective-permute-start.12 = (f32[2,2,128,128]{3,2,1,0:T(8,128)S(1)}, f32[2,2,128,128]{3,2,1,0:T(8,128)S(1)}, u32[]{:S(2)}, u32[]{:S(2)}) collective-permute-start(f32[2,2,128,128]{3,2,1,0:T(8,128)S(1)} %slice.19), channel_id=1, source_target_pairs={{0,1},{1,2},{2,3},{4,5},{5,6},{6,7},{8,9},{9,10},{10,11},{12,13},{... | collective-permute-start | bytes 786440 | tf_op jit(solution)/shard_map/ppermute | solution.py:18
  62.0 4.1 %collective-permute-start.16 = (f32[512,128]{1,0:T(8,128)S(1)}, f32[512,128]{1,0:T(8,128)S(1)}, u32[]{:S(2)}, u32[]{:S(2)}) collective-permute-start(f32[512,128]{1,0:T(8,128)S(1)} %bitcast.46), channel_id=1, source_target_pairs={{0,4},{4,0},{8,12},{12,8},{16,20},{20,16},{24,28},{28,24},{1,5},{5... | collective-permute-start | bytes 786440 | tf_op jit(solution)/shard_map/ppermute | solution.py:34
  66.1 0.8 %copy-start.8 = (f32[2,512,128]{2,1,0:T(8,128)}, f32[2,512,128]{2,1,0:T(8,128)S(1)}, u32[]{:S(2)}) copy-start(f32[2,512,128]{2,1,0:T(8,128)S(1)} %bitcast_dynamic-update-slice_fusion) | copy-start | bytes 1572868

commit v2 on v1

--- a/solution.py
+++ b/solution.py
@@ -12,19 +12,16 @@
 F32 = jnp.float32
 
 
-def moved(array, axis, by):
-    length = lax.axis_size(axis)
-    pairs = [(i, i + by) for i in range(length) if 0 <= i + by < length]
-    return lax.ppermute(array, axis, pairs)
-
-
-def moved_both(array, rows_by, cols_by):
+def moved(array, rows_by, cols_by):
     rows, cols = lax.axis_size("ty"), lax.axis_size("tx")
+    if not cols_by:
+        return lax.ppermute(array, "ty", [(i, (i + rows_by) % rows) for i in range(rows)])
+    if not rows_by:
+        return lax.ppermute(array, "tx", [(i, (i + cols_by) % cols) for i in range(cols)])
     pairs = [
-        (a * cols + b, (a + rows_by) * cols + b + cols_by)
+        (a * cols + b, (a + rows_by) % rows * cols + (b + cols_by) % cols)
         for a in range(rows)
         for b in range(cols)
-        if 0 <= a + rows_by < rows and 0 <= b + cols_by < cols
     ]
     return lax.ppermute(array, ("ty", "tx"), pairs)
 
@@ -54,14 +51,11 @@
     return out.reshape(-1, part.shape[-1])
 
 
-def real_forms(table):
+def real_form(table):
     right = np.block([[table.real, table.imag], [-table.imag, table.real]]).astype(np.float32)
     high = right.astype(BF16)
     low = (right - high.astype(np.float32)).astype(BF16)
-    return (
-        np.concatenate([high, high, low], axis=0),
-        np.concatenate([high.T, high.T, low.T], axis=1),
-    )
+    return np.stack([high, low])
 
 
 def tables(size):
@@ -70,7 +64,23 @@
     freq = (positions + size // 2) % size - size // 2
     chirp = np.exp(-2j * np.pi * (freq * freq % (4 * size)) / (4 * size))
     through = dft.conj() @ (chirp[:, None] * dft)
-    return real_forms(dft), real_forms(through)
+    return np.stack([real_form(dft), real_form(through)])
+
+
+def sided(pair):
+    high, low = pair[0], pair[1]
+    half = high.shape[0] // 2
+
+    def turned(x):
+        return jnp.concatenate(
+            [jnp.concatenate([x[:half, :half], x[half:, :half]], axis=1),
+             jnp.concatenate([x[:half, half:], x[half:, half:]], axis=1)], axis=0)
+
+    left_high, left_low = turned(high), turned(low)
+    return (
+        jnp.concatenate([high, high, low], axis=0),
+        jnp.concatenate([left_high, left_high, left_low], axis=1),
+    )
 
 
 def halves(x):
@@ -110,10 +120,9 @@
     return (a[0] * b[0] - a[1] * b[1], a[0] * b[1] + a[1] * b[0])
 
 
-def fill(wide, layer, own, right, down, corner, size):
-    wide[:, :size, :size] = own[layer]
+def fill(wide, right, down, corner, size):
     wide[:, :size, size:] = right[...]
-    wide[:, size:, :size] = down[layer]
+    wide[:, size:, :size] = down[...]
     wide[:, size:, size:] = corner[...]
 
 
@@ -121,7 +130,7 @@
 
 
 def window_of(wide, at, slot, size):
-    row, col = at[0, slot], at[1, slot]
+    row, col = at[0, 0, 0, slot], at[1, 0, 0, slot]
     shift = lax.rem(row, SUBLANES)
     rows = pl.ds(pl.multiple_of(row - shift, SUBLANES), size + SUBLANES)
     left = lax.rem(2 * size - col, 2 * size)
@@ -133,7 +142,7 @@
 
 
 def add_window(total, at, slot, grads, size):
-    row, col = at[0, slot], at[1, slot]
+    row, col = at[0, 0, 0, slot], at[1, 0, 0, slot]
     shift = lax.rem(row, SUBLANES)
     rows = pl.ds(pl.multiple_of(row - shift, SUBLANES), size + SUBLANES)
     for c in range(2):
@@ -143,51 +152,53 @@
         total[c, rows, :] += pltpu.roll(padded, col, axis=1)
 
 
-def stage_kernel(*refs):
-    count = (len(refs) - 1) // 2
-    sources, targets, sems = refs[:count], refs[count:2 * count], refs[-1]
-    copies = [pltpu.make_async_copy(a, b, sems.at[i]) for i, (a, b) in enumerate(zip(sources, targets))]
+def first_kernel(at_in, tile, probe_in, table_in, measured_in, right, down, corner,
+                 psi, window, at_out, own, probe, table, measured, at, wide, sems):
+    size = right.shape[-1]
+    slots, modes = psi.shape[:2]
+    soon = [(at_in, at), (tile.at[0], wide.at[:, pl.ds(0, size), pl.ds(0, size)]), (probe_in, probe),
+            (table_in, table)]
+    later = [(tile.at[1], own), (measured_in, measured), (at_in, at_out)]
+    copies = [pltpu.make_async_copy(a, b, sems.at[i]) for i, (a, b) in enumerate(soon + later)]
     for copy in copies:
         copy.start()
-    for copy in copies:
+    fill(wide, right, down.at[0], corner, size)
+    for copy in copies[:len(soon)]:
         copy.wait()
-
-
-def first_kernel(at, own, right, down, corner, probe, right_table, left_table, psi, window, wide):
-    size = own.shape[-1]
-    slots, modes = psi.shape[:2]
-    fill(wide, 0, own, right, down, corner, size)
     fields = []
     for slot in range(slots):
         w = window_of(wide, at, slot, size)
         window[slot, 0], window[slot, 1] = w
         fields += [product((probe[m, 0], probe[m, 1]), w) for m in range(modes)]
-    waves = both_sides(fields, right_table[...], left_table[...])
+    waves = both_sides(fields, *sided(table[1]))
     for i, wave in enumerate(waves):
         psi[i // modes, i % modes, 0], psi[i // modes, i % modes, 1] = wave
-
-
-def second_kernel(at, count, own, right, down, corner, psi, window, probe, measured,
-                  dft_right, dft_left, through_right, through_left,
+    for copy in copies[len(soon):]:
+        copy.wait()
+
+
+def second_kernel(at, count, own, right, down, corner, psi, window, probe, measured, table,
                   g_probe, g_upper, g_lower, wide, total):
     size = own.shape[-1]
     slots, modes = psi.shape[:2]
-    fill(wide, 1, own, right, down, corner, size)
+    wide[:, :size, :size] = own[...]
+    fill(wide, right, down.at[1], corner, size)
     total[...] = jnp.zeros_like(total)
+    dft, through = sided(table[0]), sided(table[1])
     w = [window_of(wide, at, slot, size) for slot in range(slots)]
     waves = [[(psi[s, m, 0], psi[s, m, 1]) for m in range(modes)] for s in range(slots)]
     fields = [product(waves[s][m], w[s]) for s in range(slots) for m in range(modes)]
-    far = both_sides(fields, dft_right[...], dft_left[...])
+    far = both_sides(fields, *dft)
     fields = []
     for s in range(slots):
         own_far = far[s * modes:(s + 1) * modes]
         intensity = sum(re * re + im * im for re, im in own_far)
-        live = jnp.where(s < count[0], 2.0, 0.0).astype(F32)
+        live = jnp.where(s < count[0, 0], 2.0, 0.0).astype(F32)
         diff = (intensity - measured[s]) * live
         fields += [(re * diff, -(im * diff)) for re, im in own_far]
-    conj = both_sides(fields, dft_right[...], dft_left[...])
+    conj = both_sides(fields, *dft)
     fields = [product(conj[s * modes + m], w[s]) for s in range(slots) for m in range(modes)]
-    start = both_sides(fields, through_right[...], through_left[...])
+    start = both_sides(fields, *through)
     for m in range(modes):
         parts = [product(start[s * modes + m], (window[s, 0], window[s, 1])) for s in range(slots)]
         g_probe[m, 0] = sum(re for re, _ in parts)
@@ -206,53 +217,58 @@
 
 VMEM = pl.BlockSpec(memory_space=pltpu.VMEM)
 SMEM = pl.BlockSpec(memory_space=pltpu.SMEM)
-HBM = pl.BlockSpec(memory_space=pl.ANY)
+HBM = pl.BlockSpec(memory_space=pltpu.HBM)
 
 
 def call(kernel, args, in_specs, outs, scratch, flops):
+    args = [
+        pltpu.with_memory_space_constraint(a, pltpu.HBM) if spec is HBM else a
+        for a, spec in zip(args, in_specs)
+    ]
     return pl.pallas_call(
         kernel,
         in_specs=in_specs,
         out_specs=[VMEM] * len(outs),
-        out_shape=[jax.ShapeDtypeStruct(shape, dtype) for shape, dtype in outs],
+        out_shape=outs,
         scratch_shapes=scratch,
         compiler_params=pltpu.CompilerParams(vmem_limit_bytes=40 * 1024 * 1024),
         cost_estimate=pl.CostEstimate(flops=flops, bytes_accessed=4 * 1024 * 1024, transcendentals=0),
     )(*args)
 
 
+def shaped(shape, dtype=F32):
+    return jax.ShapeDtypeStruct(shape, dtype)
+
+
 def on_device(object_slices, probe, measured, offsets, counts):
     layers, _, _, size = object_slices.shape
     slots = offsets.shape[-1]
     modes = probe.shape[0]
-    at = offsets.reshape(2, slots)
-    count = counts.reshape(1)
-    (dft_right, dft_left), (through_right, through_left) = tables(size)
+    measured = measured.reshape(slots, size, size)
+    table = jnp.asarray(tables(size))
     flops = slots * modes * 2 * size * (2 * size) * (6 * size) * 2
     wide = pltpu.VMEM((2, 2 * size, 2 * size), F32)
 
-    rights = [moved(object_slices[k], "tx", -1) for k in range(layers)]
-    corners = [moved_both(object_slices[k], -1, -1) for k in range(layers)]
-    downs = moved(object_slices, "ty", -1)
-
-    early = (probe, jnp.asarray(through_right), jnp.asarray(through_left))
-    early = call(
-        stage_kernel, early, [HBM] * 3, [(a.shape, a.dtype) for a in early],
-        [pltpu.SemaphoreType.DMA((3,))], flops,
-    )
-    psi, window = call(
+    right_0 = moved(object_slices[0], 0, -1)
+    corner_0 = moved(object_slices[0], -1, -1)
+    down = moved(object_slices, -1, 0)
+    right_1 = moved(object_slices[1], 0, -1)
+    corner_1 = moved(object_slices[1], -1, -1)
+
+    psi, window, at, own, *rest = call(
         first_kernel,
-        (at, object_slices, rights[0], downs, corners[0], *early),
-        [SMEM] + [VMEM] * 7,
-        [((slots, modes, 2, size, size), F32), ((slots, 2, size, size), F32)],
-        [wide], flops,
-    )
+        (offsets, object_slices, probe, table, measured, right_0, down, corner_0),
+        [HBM] * 5 + [VMEM] * 3,
+        [shaped((slots, modes, 2, size, size)), shaped((slots, 2, size, size)), shaped(offsets.shape, jnp.int32),
+         shaped((2, size, size)), shaped(probe.shape), shaped(table.shape, BF16), shaped(measured.shape)],
+        [pltpu.SMEM(offsets.shape, jnp.int32), wide, pltpu.SemaphoreType.DMA((7,))], flops,
+    )
+    probe_near, table_near, measured_near = rest
     g_probe, g_upper, g_lower = call(
         second_kernel,
-        (at, count, object_slices, rights[1], downs, corners[1], psi, window, early[0],
-         measured.reshape(slots, size, size), dft_right, dft_left, early[1], early[2]),
-        [SMEM] * 2 + [VMEM] * 12,
-        [(probe.shape, F32)] + [((layers, 2, size, 2 * size), F32)] * 2,
+        (at, counts, own, right_1, down, corner_1, psi, window, probe_near, measured_near, table_near),
+        [SMEM] * 2 + [VMEM] * 9,
+        [shaped(probe.shape)] + [shaped((layers, 2, size, 2 * size))] * 2,
         [wide, pltpu.VMEM((layers, 2, 2 * size, 2 * size), F32)], 3 * flops,
     )
 
@@ -260,14 +276,14 @@
     part = scattered(g_probe.reshape(-1, size), "ty", 1, 2)
     part = scattered(part, "ty", 2, rows // 2)
     part, g_lower = lax.optimization_barrier((part, g_lower))
-    from_above = moved(g_lower, "ty", 1)
+    from_above = moved(g_lower, 1, 0)
     bit = 1
     while bit < lax.axis_size("tx"):
         part = part + swapped(part, "tx", bit)
         bit *= 2
     g_wide = g_upper + from_above
     g_right, part = lax.optimization_barrier((g_wide[..., size:], part))
-    from_left_tile = moved(g_right, "tx", 1)
+    from_left_tile = moved(g_right, 0, 1)
     part = gathered(part, "ty", 2, rows // 2)
     part = gathered(part, "ty", 1, 2)
     object_grad = g_wide[..., :size] + from_left_tile

time: 67.3 us -> 62.1 us (0.923)
  starting transfers between devices: 26.4 us -> 17.7 us
  waiting for transfers between devices: 21.3 us -> 28.4 us
  local copies, waits for them, and re-layouts: 5.04 us -> 1.99 us
    ppermute x10, starting transfers between devices: 16.3 us -> 9.48 us  [swapped(): return lax.ppermute(array, axis, [(i, i ^ bit) for i in range(length)])]
    ppermute x10, waiting for transfers between devices: 12.6 us -> 16.7 us  [swapped(): return lax.ppermute(array, axis, [(i, i ^ bit) for i in range(length)])]
    unnamed x18 -> x2, local copies, waits for them, and re-layouts: 3.84 us -> 0.79 us
    ppermute x7, waiting for transfers between devices: 8.73 us -> 11.7 us  [the longest x3 8.27 us: moved(): lax.ppermute(array, 'tx', [(i, (i + cols_by) % cols) for i in range(cols)])]
    ppermute x7, starting transfers between devices: 10.1 us -> 8.23 us  [the longest x3 4.45 us: moved(): lax.ppermute(array, 'tx', [(i, (i + cols_by) % cols) for i in range(cols)])]
    pallas_call x3 -> x2, Pallas kernels: 11.7 us -> 11.4 us  [call(): pl.pallas_call(kernel, in_specs=in_specs, out_specs=[VMEM] * len(outs), o...]
  transfers between devices with their start and end apart: 17 -> 17, of which waited for: 11 -> 12; matrix products, arithmetic and copies ran while one was open for 3% -> 3% of each run, Pallas kernels for 5% -> 6%
where the time goes in v2:
time: 62.1 us; the launch traced here: 61.9 us
  waiting for transfers between devices  28.4 us (46%)
  starting transfers between devices  17.7 us (29%)
  Pallas kernels  11.4 us (18%)
  local copies, waits for them, and re-layouts  1.99 us (3%)
  between operations  1.53 us (2%)
  other arithmetic  0.86 us (1%)
    ppermute x10, waiting for transfers between devices, swapped(): return lax.ppermute(array, axis, [(i, i ^ bit) for i in range(length)])  16.7 us
    pallas_call x2, Pallas kernels, call(): pl.pallas_call(kernel, in_specs=in_specs, out_specs=[VMEM] * len(outs), o...  11.4 us
    ppermute x10, starting transfers between devices, swapped(): return lax.ppermute(array, axis, [(i, i ^ bit) for i in range(length)])  9.48 us
    ppermute x3, waiting for transfers between devices, moved(): lax.ppermute(array, 'tx', [(i, (i + cols_by) % cols) for i in range(cols)])  8.27 us
    ppermute x3, starting transfers between devices, moved(): lax.ppermute(array, 'tx', [(i, (i + cols_by) % cols) for i in range(cols)])  4.45 us
    ppermute x2, starting transfers between devices, moved(): lax.ppermute(array, 'ty', [(i, (i + rows_by) % rows) for i in range(rows)])  3.44 us
    ppermute x2, waiting for transfers between devices, moved(): return lax.ppermute(array, ('ty', 'tx'), pairs)  3.42 us
  transfers between devices with their start and end apart: 17, of which 12 were waited for; matrix products, arithmetic and copies ran while one was open for 3% of the time, Pallas kernels for 6%

profile of v2, /device:TPU:0, one launch (start us, length us, event | category | flops | bytes accessed | tf_op | source)
XLA Modules:
  0.0 61.9 jit_solution(17293132439087308239)
XLA Ops:
  0.6 3.4 %collective-permute-start.1 = (f32[2,2,128,128]{3,2,1,0:T(8,128)}, f32[2,2,128,128]{3,2,1,0:T(8,128)S(1)}, u32[]{:S(2)}, u32[]{:S(2)}) collective-permute-start(f32[2,2,128,128]{3,2,1,0:T(8,128)} %tile.1), channel_id=1, source_target_pairs={{0,28},{4,0},{8,4},{12,8},{16,12},{20,16},{24,20},{28,24},{1,29},{... | collective-permute-start | bytes 786440 | tf_op jit(solution)/shard_map/ppermute | solution.py:18
  4.0 1.0 %slice_bitcast_fusion = (f32[2,128,128]{2,1,0:T(8,128)S(1)}, f32[2,128,128]{2,1,0:T(8,128)S(1)}) fusion(f32[2,2,128,128]{3,2,1,0:T(8,128)} %tile.1), kind=kLoop, calls=%fused_computation.5 | loop fusion | bytes 524288 | tf_op jit(solution)/shard_map/squeeze | solution.py:255
  5.0 3.7 %collective-permute-start = (f32[2,128,128]{2,1,0:T(8,128)S(1)}, f32[2,128,128]{2,1,0:T(8,128)S(1)}, u32[]{:S(2)}, u32[]{:S(2)}) collective-permute-start(f32[2,128,128]{2,1,0:T(8,128)S(1)} %get-tuple-element.34), channel_id=1, source_target_pairs={{0,3},{1,0},{2,1},{3,2},{4,7},{5,4},{6,5},{7,6},{8,11},{9,8},{10,9... | collective-permute-start | bytes 393224 | tf_op jit(solution)/shard_map/ppermute | solution.py:20
  8.7 0.3 collective-permute-start.2
  8.9 0.4 collective-permute-start.3
  9.4 0.1 collective-permute-start.4
  10.1 2.4 %collective-permute-done.right = f32[2,128,128]{2,1,0:T(8,128)S(1)} collective-permute-done((f32[2,128,128]{2,1,0:T(8,128)S(1)}, f32[2,128,128]{2,1,0:T(8,128)S(1)}, u32[]{:S(2)}, u32[]{:S(2)}) %collective-permute-start) | collective-permute-done | bytes 131104 | tf_op jit(solution)/shard_map/ppermute | solution.py:20
  12.6 2.8 %collective-permute-done.2.corner = f32[2,128,128]{2,1,0:T(8,128)S(1)} collective-permute-done((f32[2,128,128]{2,1,0:T(8,128)S(1)}, f32[2,128,128]{2,1,0:T(8,128)S(1)}, u32[]{:S(2)}, u32[]{:S(2)}) %collective-permute-start.2) | collective-permute-done | bytes 131104 | tf_op jit(solution)/shard_map/ppermute | solution.py:26
  15.4 3.8 %shard_map.77 = (f32[4,4,2,128,128]{4,3,2,1,0:T(8,128)S(1)}, f32[4,2,128,128]{3,2,1,0:T(8,128)S(1)}, s32[2,1,1,4]{3,2,1,0:T(1,128)S(1)}, f32[2,128,128]{2,1,0:T(...) custom-call(s32[2,1,1,4]{3,2,1,0:T(1,128)} %at_in.1, ...), custom_call_target="tpu_custom_call" | custom-call | flops 1610612736 | bytes 4194304 | tf_op jit(solution)/shard_map/pallas_call | solution.py:228
  19.2 0.6 collective-permute-done.4.corner
  19.8 7.6 %shard_map.78 = (f32[4,2,128,128]{3,2,1,0:T(8,128)S(1)}, f32[2,2,128,256]{3,2,1,0:T(8,128)S(1)}, f32[2,2,128,256]{3,2,1,0:T(8,128)S(1)}) custom-call(s32[2,1,1,4]{3,2,1,0:T(1,128)S(1)} %get-tuple-element.16.at, s32[1,1]{1,0:T(1,128)S(6)} %copy.14.count, f32[2,128,128]{2,1,0:T(8,128)S(1)} %get-tuple-element.17.own, ...), custom_call_target="tpu_custom_call" | custom-call | flops 4831838208 | bytes 4194304 | tf_op jit(solution)/shard_map/pallas_call | solution.py:228
  27.6 1.5 %collective-permute-done.5 = f32[512,128]{1,0:T(8,128)S(1)} collective-permute-done((f32[512,128]{1,0:T(8,128)S(1)}, f32[512,128]{1,0:T(8,128)S(1)}, u32[]{:S(2)}, u32[]{:S(2)}) %collective-permute-start.5) | collective-permute-done | bytes 262176 | tf_op jit(solution)/shard_map/ppermute | solution.py:31
  29.1 2.2 %collective-permute-start.8 = (f32[128,128]{1,0:T(8,128)S(1)}, f32[128,128]{1,0:T(8,128)S(1)}, u32[]{:S(2)}, u32[]{:S(2)}) collective-permute-start(f32[128,128]{1,0:T(8,128)S(1)} %get-tuple-element.31), channel_id=1, source_target_pairs={{0,24},{4,28},{8,16},{12,20},{16,8},{20,12},{24,0},{28,4},{1,25},{... | collective-permute-start | bytes 196616 | tf_op jit(solution)/shard_map/ppermute | solution.py:31
  31.2 0.6 collective-permute-start.7
  31.8 0.8 %collective-permute-start.6 = (f32[128,128]{1,0:T(8,128)S(1)}, f32[128,128]{1,0:T(8,128)S(1)}, u32[]{:S(2)}, u32[]{:S(2)}) collective-permute-start(f32[128,128]{1,0:T(8,128)S(1)} %get-tuple-element.30), channel_id=1, source_target_pairs={{0,8},{4,12},{8,0},{12,4},{16,24},{20,28},{24,16},{28,20},{1,9},{5... | collective-permute-start | bytes 196616 | tf_op jit(solution)/shard_map/ppermute | solution.py:31
  32.6 1.7 %collective-permute-done.8 = f32[128,128]{1,0:T(8,128)S(1)} collective-permute-done((f32[128,128]{1,0:T(8,128)S(1)}, f32[128,128]{1,0:T(8,128)S(1)}, u32[]{:S(2)}, u32[]{:S(2)}) %collective-permute-start.8) | collective-permute-done | bytes 65568 | tf_op jit(solution)/shard_map/ppermute | solution.py:31
  34.4 1.4 %collective-permute-done.7 = f32[128,128]{1,0:T(8,128)S(1)} collective-permute-done((f32[128,128]{1,0:T(8,128)S(1)}, f32[128,128]{1,0:T(8,128)S(1)}, u32[]{:S(2)}, u32[]{:S(2)}) %collective-permute-start.7) | collective-permute-done | bytes 65568 | tf_op jit(solution)/shard_map/ppermute | solution.py:31
  35.7 0.3 collective-permute-done.6
  36.2 0.1 collective-permute-start.10
  36.2 4.9 %collective-permute-done.10 = f32[128,128]{1,0:T(8,128)S(1)} collective-permute-done((f32[128,128]{1,0:T(8,128)S(1)}, f32[128,128]{1,0:T(8,128)S(1)}, u32[]{:S(2)}, u32[]{:S(2)}) %collective-permute-start.10) | collective-permute-done | bytes 65568 | tf_op jit(solution)/shard_map/ppermute | solution.py:31
  41.2 2.2 %collective-permute-start.11 = (f32[128,128]{1,0:T(8,128)S(1)}, f32[128,128]{1,0:T(8,128)S(1)}, u32[]{:S(2)}, u32[]{:S(2)}) collective-permute-start(f32[128,128]{1,0:T(8,128)S(1)} %add.76), channel_id=1, source_target_pairs={{0,2},{1,3},{2,0},{3,1},{4,6},{5,7},{6,4},{7,5},{8,10},{9,11},{10,... | collective-permute-start | bytes 196616 | tf_op jit(solution)/shard_map/ppermute | solution.py:31
  43.4 4.5 %collective-permute-done.11 = f32[128,128]{1,0:T(8,128)S(1)} collective-permute-done((f32[128,128]{1,0:T(8,128)S(1)}, f32[128,128]{1,0:T(8,128)S(1)}, u32[]{:S(2)}, u32[]{:S(2)}) %collective-permute-start.11) | collective-permute-done | bytes 65568 | tf_op jit(solution)/shard_map/ppermute | solution.py:31
  48.0 0.8 %collective-permute-start.13 = (f32[128,128]{1,0:T(8,128)S(1)}, f32[128,128]{1,0:T(8,128)S(1)}, u32[]{:S(2)}, u32[]{:S(2)}) collective-permute-start(f32[128,128]{1,0:T(8,128)S(1)} %add.77), channel_id=1, source_target_pairs={{0,8},{4,12},{8,0},{12,4},{16,24},{20,28},{24,16},{28,20},{1,9},{5... | collective-permute-start | bytes 196616 | tf_op jit(solution)/shard_map/ppermute | solution.py:31
  48.7 0.3 collective-permute-start.14
  49.0 2.5 %collective-permute-start.15 = (f32[128,128]{1,0:T(8,128)S(1)}, f32[128,128]{1,0:T(8,128)S(1)}, u32[]{:S(2)}, u32[]{:S(2)}) collective-permute-start(f32[128,128]{1,0:T(8,128)S(1)} %add.77), channel_id=1, source_target_pairs={{0,24},{4,28},{8,16},{12,20},{16,8},{20,12},{24,0},{28,4},{1,25},{... | collective-permute-start | bytes 196616 | tf_op jit(solution)/shard_map/ppermute | solution.py:31
  51.5 0.3 collective-permute-start.12
  51.9 0.4 collective-permute-done.13
  52.3 2.0 %collective-permute-done.14 = f32[128,128]{1,0:T(8,128)S(1)} collective-permute-done((f32[128,128]{1,0:T(8,128)S(1)}, f32[128,128]{1,0:T(8,128)S(1)}, u32[]{:S(2)}, u32[]{:S(2)}) %collective-permute-start.14) | collective-permute-done | bytes 65568 | tf_op jit(solution)/shard_map/ppermute | solution.py:31
  54.3 0.1 collective-permute-start.16
  54.5 5.8 %collective-permute-done.12 = f32[2,2,128,128]{3,2,1,0:T(8,128)S(1)} collective-permute-done((f32[2,2,128,128]{3,2,1,0:T(8,128)S(1)}, f32[2,2,128,128]{3,2,1,0:T(8,128)S(1)}, u32[]{:S(2)}, u32[]{:S(2)}) %collective-permute-start.12) | collective-permute-done | bytes 262176 | tf_op jit(solution)/shard_map/ppermute | solution.py:20
  60.3 0.7 %slice_add_fusion = f32[2,2,128,128]{3,2,1,0:T(8,128)} fusion(f32[2,2,128,128]{3,2,1,0:T(8,128)S(1)} %collective-permute-done.12, f32[2,2,128,256]{3,2,1,0:T(8,128)S(1)} %add.75), kind=kLoop, calls=%fused_computation | loop fusion | flops 65536 | bytes 786432 | tf_op jit(solution)/shard_map/add | solution.py:289
  61.1 0.8 %copy-done = f32[2,512,128]{2,1,0:T(8,128)} copy-done((f32[2,512,128]{2,1,0:T(8,128)}, f32[2,512,128]{2,1,0:T(8,128)S(1)}, u32[]{:S(2)}) %copy-start) | copy-done | bytes 524312
  (24 shorter events, 0.5 us)
Async XLA Ops:
  0.6 14.7 %collective-permute-start.1 = (f32[2,2,128,128]{3,2,1,0:T(8,128)}, f32[2,2,128,128]{3,2,1,0:T(8,128)S(1)}, u32[]{:S(2)}, u32[]{:S(2)}) collective-permute-start(f32[2,2,128,128]{3,2,1,0:T(8,128)} %tile.1), channel_id=1, source_target_pairs={{0,28},{4,0},{8,4},{12,8},{16,12},{20,16},{24,20},{28,24},{1,29},{... | collective-permute-start | bytes 786440 | tf_op jit(solution)/shard_map/ppermute | solution.py:18
  5.0 7.5 %collective-permute-start = (f32[2,128,128]{2,1,0:T(8,128)S(1)}, f32[2,128,128]{2,1,0:T(8,128)S(1)}, u32[]{:S(2)}, u32[]{:S(2)}) collective-permute-start(f32[2,128,128]{2,1,0:T(8,128)S(1)} %get-tuple-element.34), channel_id=1, source_target_pairs={{0,3},{1,0},{2,1},{3,2},{4,7},{5,4},{6,5},{7,6},{8,11},{9,8},{10,9... | collective-permute-start | bytes 393224 | tf_op jit(solution)/shard_map/ppermute | solution.py:20
  8.7 6.7 %collective-permute-start.2 = (f32[2,128,128]{2,1,0:T(8,128)S(1)}, f32[2,128,128]{2,1,0:T(8,128)S(1)}, u32[]{:S(2)}, u32[]{:S(2)}) collective-permute-start(f32[2,128,128]{2,1,0:T(8,128)S(1)} %get-tuple-element.34), channel_id=1, source_target_pairs={{0,31},{1,28},{2,29},{3,30},{4,3},{5,0},{6,1},{7,2},{8,7},{9,4},{1... | collective-permute-start | bytes 393224 | tf_op jit(solution)/shard_map/ppermute | solution.py:26
  8.9 10.2 %collective-permute-start.3 = (f32[2,128,128]{2,1,0:T(8,128)S(1)}, f32[2,128,128]{2,1,0:T(8,128)S(1)}, u32[]{:S(2)}, u32[]{:S(2)}) collective-permute-start(f32[2,128,128]{2,1,0:T(8,128)S(1)} %get-tuple-element.33), channel_id=1, source_target_pairs={{0,3},{1,0},{2,1},{3,2},{4,7},{5,4},{6,5},{7,6},{8,11},{9,8},{10,9... | collective-permute-start | bytes 393224 | tf_op jit(solution)/shard_map/ppermute | solution.py:20
  9.4 10.4 %collective-permute-start.4 = (f32[2,128,128]{2,1,0:T(8,128)S(1)}, f32[2,128,128]{2,1,0:T(8,128)S(1)}, u32[]{:S(2)}, u32[]{:S(2)}) collective-permute-start(f32[2,128,128]{2,1,0:T(8,128)S(1)} %get-tuple-element.33), channel_id=1, source_target_pairs={{0,31},{1,28},{2,29},{3,30},{4,3},{5,0},{6,1},{7,2},{8,7},{9,4},{1... | collective-permute-start | bytes 393224 | tf_op jit(solution)/shard_map/ppermute | solution.py:26
  27.4 1.6 %collective-permute-start.5 = (f32[512,128]{1,0:T(8,128)S(1)}, f32[512,128]{1,0:T(8,128)S(1)}, u32[]{:S(2)}, u32[]{:S(2)}) collective-permute-start(f32[512,128]{1,0:T(8,128)S(1)} %dynamic-slice_bitcast_fusion), channel_id=1, source_target_pairs={{0,4},{4,0},{8,12},{12,8},{16,20},{20,16},{24,28},{28,24},{1,5},{5... | collective-permute-start | bytes 786440 | tf_op jit(solution)/shard_map/ppermute | solution.py:31
  29.1 5.3 %collective-permute-start.8 = (f32[128,128]{1,0:T(8,128)S(1)}, f32[128,128]{1,0:T(8,128)S(1)}, u32[]{:S(2)}, u32[]{:S(2)}) collective-permute-start(f32[128,128]{1,0:T(8,128)S(1)} %get-tuple-element.31), channel_id=1, source_target_pairs={{0,24},{4,28},{8,16},{12,20},{16,8},{20,12},{24,0},{28,4},{1,25},{... | collective-permute-start | bytes 196616 | tf_op jit(solution)/shard_map/ppermute | solution.py:31
  31.2 4.5 %collective-permute-start.7 = (f32[128,128]{1,0:T(8,128)S(1)}, f32[128,128]{1,0:T(8,128)S(1)}, u32[]{:S(2)}, u32[]{:S(2)}) collective-permute-start(f32[128,128]{1,0:T(8,128)S(1)} %get-tuple-element.32), channel_id=1, source_target_pairs={{0,16},{4,20},{8,24},{12,28},{16,0},{20,4},{24,8},{28,12},{1,17},{... | collective-permute-start | bytes 196616 | tf_op jit(solution)/shard_map/ppermute | solution.py:31
  31.8 4.3 %collective-permute-start.6 = (f32[128,128]{1,0:T(8,128)S(1)}, f32[128,128]{1,0:T(8,128)S(1)}, u32[]{:S(2)}, u32[]{:S(2)}) collective-permute-start(f32[128,128]{1,0:T(8,128)S(1)} %get-tuple-element.30), channel_id=1, source_target_pairs={{0,8},{4,12},{8,0},{12,4},{16,24},{20,28},{24,16},{28,20},{1,9},{5... | collective-permute-start | bytes 196616 | tf_op jit(solution)/shard_map/ppermute | solution.py:31
  36.1 11.8 %collective-permute-start.9 = (f32[2,2,128,256]{3,2,1,0:T(8,128)S(1)}, f32[2,2,128,256]{3,2,1,0:T(8,128)S(1)}, u32[]{:S(2)}, u32[]{:S(2)}) collective-permute-start(f32[2,2,128,256]{3,2,1,0:T(8,128)S(1)} %get-tuple-element.26), channel_id=1, source_target_pairs={{0,4},{4,8},{8,12},{12,16},{16,20},{20,24},{24,28},{28,0},{1,5},{5... | collective-permute-start | bytes 1572872 | tf_op jit(solution)/shard_map/ppermute | solution.py:18
  36.2 5.0 %collective-permute-start.10 = (f32[128,128]{1,0:T(8,128)S(1)}, f32[128,128]{1,0:T(8,128)S(1)}, u32[]{:S(2)}, u32[]{:S(2)}) collective-permute-start(f32[128,128]{1,0:T(8,128)S(1)} %fusion.1), channel_id=1, source_target_pairs={{0,1},{1,0},{2,3},{3,2},{4,5},{5,4},{6,7},{7,6},{8,9},{9,8},{10,11... | collective-permute-start | bytes 196616 | tf_op jit(solution)/shard_map/ppermute | solution.py:31
  41.2 6.6 %collective-permute-start.11 = (f32[128,128]{1,0:T(8,128)S(1)}, f32[128,128]{1,0:T(8,128)S(1)}, u32[]{:S(2)}, u32[]{:S(2)}) collective-permute-start(f32[128,128]{1,0:T(8,128)S(1)} %add.76), channel_id=1, source_target_pairs={{0,2},{1,3},{2,0},{3,1},{4,6},{5,7},{6,4},{7,5},{8,10},{9,11},{10,... | collective-permute-start | bytes 196616 | tf_op jit(solution)/shard_map/ppermute | solution.py:31
  48.0 4.3 %collective-permute-start.13 = (f32[128,128]{1,0:T(8,128)S(1)}, f32[128,128]{1,0:T(8,128)S(1)}, u32[]{:S(2)}, u32[]{:S(2)}) collective-permute-start(f32[128,128]{1,0:T(8,128)S(1)} %add.77), channel_id=1, source_target_pairs={{0,8},{4,12},{8,0},{12,4},{16,24},{20,28},{24,16},{28,20},{1,9},{5... | collective-permute-start | bytes 196616 | tf_op jit(solution)/shard_map/ppermute | solution.py:31
  48.7 5.6 %collective-permute-start.14 = (f32[128,128]{1,0:T(8,128)S(1)}, f32[128,128]{1,0:T(8,128)S(1)}, u32[]{:S(2)}, u32[]{:S(2)}) collective-permute-start(f32[128,128]{1,0:T(8,128)S(1)} %add.77), channel_id=1, source_target_pairs={{0,16},{4,20},{8,24},{12,28},{16,0},{20,4},{24,8},{28,12},{1,17},{... | collective-permute-start | bytes 196616 | tf_op jit(solution)/shard_map/ppermute | solution.py:31
  49.0 5.3 %collective-permute-start.15 = (f32[128,128]{1,0:T(8,128)S(1)}, f32[128,128]{1,0:T(8,128)S(1)}, u32[]{:S(2)}, u32[]{:S(2)}) collective-permute-start(f32[128,128]{1,0:T(8,128)S(1)} %add.77), channel_id=1, source_target_pairs={{0,24},{4,28},{8,16},{12,20},{16,8},{20,12},{24,0},{28,4},{1,25},{... | collective-permute-start | bytes 196616 | tf_op jit(solution)/shard_map/ppermute | solution.py:31
  51.5 8.8 %collective-permute-start.12 = (f32[2,2,128,128]{3,2,1,0:T(8,128)S(1)}, f32[2,2,128,128]{3,2,1,0:T(8,128)S(1)}, u32[]{:S(2)}, u32[]{:S(2)}) collective-permute-start(f32[2,2,128,128]{3,2,1,0:T(8,128)S(1)} %slice.19), channel_id=1, source_target_pairs={{0,1},{1,2},{2,3},{3,0},{4,5},{5,6},{6,7},{7,4},{8,9},{9,10},{10,1... | collective-permute-start | bytes 786440 | tf_op jit(solution)/shard_map/ppermute | solution.py:20
  54.3 6.7 %collective-permute-start.16 = (f32[512,128]{1,0:T(8,128)S(1)}, f32[512,128]{1,0:T(8,128)S(1)}, u32[]{:S(2)}, u32[]{:S(2)}) collective-permute-start(f32[512,128]{1,0:T(8,128)S(1)} %bitcast.40), channel_id=1, source_target_pairs={{0,4},{4,0},{8,12},{12,8},{16,20},{20,16},{24,28},{28,24},{1,5},{5... | collective-permute-start | bytes 786440 | tf_op jit(solution)/shard_map/ppermute | solution.py:31
  61.1 0.8 %copy-start = (f32[2,512,128]{2,1,0:T(8,128)}, f32[2,512,128]{2,1,0:T(8,128)S(1)}, u32[]{:S(2)}) copy-start(f32[2,512,128]{2,1,0:T(8,128)S(1)} %bitcast_dynamic-update-slice_fusion) | copy-start | bytes 1572868

commit v3 on v2

--- a/solution.py
+++ b/solution.py
@@ -12,17 +12,26 @@
 F32 = jnp.float32
 
 
-def moved(array, rows_by, cols_by):
+def moved(array, axis, by):
+    length = lax.axis_size(axis)
+    return lax.ppermute(array, axis, [(i, (i + by) % length) for i in range(length)])
+
+
+def from_corner(array):
     rows, cols = lax.axis_size("ty"), lax.axis_size("tx")
-    if not cols_by:
-        return lax.ppermute(array, "ty", [(i, (i + rows_by) % rows) for i in range(rows)])
-    if not rows_by:
-        return lax.ppermute(array, "tx", [(i, (i + cols_by) % cols) for i in range(cols)])
-    pairs = [
-        (a * cols + b, (a + rows_by) % rows * cols + (b + cols_by) % cols)
-        for a in range(rows)
-        for b in range(cols)
-    ]
+
+    def target(a, b):
+        if a > 0 and b > 0:
+            return a - 1, b - 1
+        if b > 0:
+            return rows - 1, b
+        return (a, cols - 1) if a < rows - 1 else (a, b)
+
+    pairs = []
+    for a in range(rows):
+        for b in range(cols):
+            down, over = target(a, b)
+            pairs.append((a * cols + b, down * cols + over))
     return lax.ppermute(array, ("ty", "tx"), pairs)
 
 
@@ -249,11 +258,11 @@
     flops = slots * modes * 2 * size * (2 * size) * (6 * size) * 2
     wide = pltpu.VMEM((2, 2 * size, 2 * size), F32)
 
-    right_0 = moved(object_slices[0], 0, -1)
-    corner_0 = moved(object_slices[0], -1, -1)
-    down = moved(object_slices, -1, 0)
-    right_1 = moved(object_slices[1], 0, -1)
-    corner_1 = moved(object_slices[1], -1, -1)
+    right_0 = moved(object_slices[0], "tx", -1)
+    corner_0 = from_corner(object_slices[0])
+    down = moved(object_slices, "ty", -1)
+    right_1 = moved(object_slices[1], "tx", -1)
+    corner_1 = from_corner(object_slices[1])
 
     psi, window, at, own, *rest = call(
         first_kernel,
@@ -276,14 +285,14 @@
     part = scattered(g_probe.reshape(-1, size), "ty", 1, 2)
     part = scattered(part, "ty", 2, rows // 2)
     part, g_lower = lax.optimization_barrier((part, g_lower))
-    from_above = moved(g_lower, 1, 0)
+    from_above = moved(g_lower, "ty", 1)
     bit = 1
     while bit < lax.axis_size("tx"):
         part = part + swapped(part, "tx", bit)
         bit *= 2
     g_wide = g_upper + from_above
     g_right, part = lax.optimization_barrier((g_wide[..., size:], part))
-    from_left_tile = moved(g_right, 0, 1)
+    from_left_tile = moved(g_right, "tx", 1)
     part = gathered(part, "ty", 2, rows // 2)
     part = gathered(part, "ty", 1, 2)
     object_grad = g_wide[..., :size] + from_left_tile

time: 62.1 us -> 62.8 us (1.011)
  starting transfers between devices: 17.7 us -> 21.7 us
  waiting for transfers between devices: 28.4 us -> 25.2 us
    ppermute x7, waiting for transfers between devices: 11.7 us -> 5.86 us  [the longest x5 4.88 us: moved(): lax.ppermute(array, axis, [(i, (i + by) % length) for i in range(length)])]
    ppermute x7, starting transfers between devices: 8.23 us -> 12.2 us  [the longest x5 7.54 us: moved(): lax.ppermute(array, axis, [(i, (i + by) % length) for i in range(length)])]
    ppermute x10, waiting for transfers between devices: 16.7 us -> 19.3 us  [swapped(): return lax.ppermute(array, axis, [(i, i ^ bit) for i in range(length)])]
where the time goes in v3:
time: 62.8 us; the launch traced here: 62.6 us
  waiting for transfers between devices  25.2 us (40%)
  starting transfers between devices  21.7 us (35%)
  Pallas kernels  11.4 us (18%)
  local copies, waits for them, and re-layouts  1.99 us (3%)
  between operations  1.49 us (2%)
  other arithmetic  0.86 us (1%)
    ppermute x10, waiting for transfers between devices, swapped(): return lax.ppermute(array, axis, [(i, i ^ bit) for i in range(length)])  19.3 us
    pallas_call x2, Pallas kernels, call(): pl.pallas_call(kernel, in_specs=in_specs, out_specs=[VMEM] * len(outs), o...  11.4 us
    ppermute x10, starting transfers between devices, swapped(): return lax.ppermute(array, axis, [(i, i ^ bit) for i in range(length)])  9.43 us
    ppermute x5, starting transfers between devices, moved(): lax.ppermute(array, axis, [(i, (i + by) % length) for i in range(length)])  7.54 us
    ppermute x5, waiting for transfers between devices, moved(): lax.ppermute(array, axis, [(i, (i + by) % length) for i in range(length)])  4.88 us
    ppermute x2, starting transfers between devices, from_corner(): return lax.ppermute(array, ('ty', 'tx'), pairs)  4.69 us
  transfers between devices with their start and end apart: 17, of which 12 were waited for; matrix products, arithmetic and copies ran while one was open for 3% of the time, Pallas kernels for 6%

profile of v3, /device:TPU:0, one launch (start us, length us, event | category | flops | bytes accessed | tf_op | source)
XLA Modules:
  0.0 62.6 jit_solution(13209369050419751078)
XLA Ops:
  0.6 3.4 %collective-permute-start.1 = (f32[2,2,128,128]{3,2,1,0:T(8,128)}, f32[2,2,128,128]{3,2,1,0:T(8,128)S(1)}, u32[]{:S(2)}, u32[]{:S(2)}) collective-permute-start(f32[2,2,128,128]{3,2,1,0:T(8,128)} %tile.1), channel_id=1, source_target_pairs={{0,28},{4,0},{8,4},{12,8},{16,12},{20,16},{24,20},{28,24},{1,29},{... | collective-permute-start | bytes 786440 | tf_op jit(solution)/shard_map/ppermute | solution.py:17
  4.0 1.0 %slice_bitcast_fusion = (f32[2,128,128]{2,1,0:T(8,128)S(1)}, f32[2,128,128]{2,1,0:T(8,128)S(1)}) fusion(f32[2,2,128,128]{3,2,1,0:T(8,128)} %tile.1), kind=kLoop, calls=%fused_computation.5 | loop fusion | bytes 524288 | tf_op jit(solution)/shard_map/squeeze | solution.py:264
  5.0 3.7 %collective-permute-start = (f32[2,128,128]{2,1,0:T(8,128)S(1)}, f32[2,128,128]{2,1,0:T(8,128)S(1)}, u32[]{:S(2)}, u32[]{:S(2)}) collective-permute-start(f32[2,128,128]{2,1,0:T(8,128)S(1)} %get-tuple-element.34), channel_id=1, source_target_pairs={{0,3},{1,0},{2,1},{3,2},{4,7},{5,4},{6,5},{7,6},{8,11},{9,8},{10,9... | collective-permute-start | bytes 393224 | tf_op jit(solution)/shard_map/ppermute | solution.py:17
  8.7 2.3 %collective-permute-start.2 = (f32[2,128,128]{2,1,0:T(8,128)S(1)}, f32[2,128,128]{2,1,0:T(8,128)S(1)}, u32[]{:S(2)}, u32[]{:S(2)}) collective-permute-start(f32[2,128,128]{2,1,0:T(8,128)S(1)} %get-tuple-element.34), channel_id=1, source_target_pairs={{0,3},{1,29},{2,30},{3,31},{4,7},{5,0},{6,1},{7,2},{8,11},{9,4},{1... | collective-permute-start | bytes 393224 | tf_op jit(solution)/shard_map/ppermute | solution.py:35
  11.0 0.4 collective-permute-start.3
  11.5 2.3 %collective-permute-start.4 = (f32[2,128,128]{2,1,0:T(8,128)S(1)}, f32[2,128,128]{2,1,0:T(8,128)S(1)}, u32[]{:S(2)}, u32[]{:S(2)}) collective-permute-start(f32[2,128,128]{2,1,0:T(8,128)S(1)} %get-tuple-element.33), channel_id=1, source_target_pairs={{0,3},{1,29},{2,30},{3,31},{4,7},{5,0},{6,1},{7,2},{8,11},{9,4},{1... | collective-permute-start | bytes 393224 | tf_op jit(solution)/shard_map/ppermute | solution.py:35
  14.5 0.9 %collective-permute-done.2.corner = f32[2,128,128]{2,1,0:T(8,128)S(1)} collective-permute-done((f32[2,128,128]{2,1,0:T(8,128)S(1)}, f32[2,128,128]{2,1,0:T(8,128)S(1)}, u32[]{:S(2)}, u32[]{:S(2)}) %collective-permute-start.2) | collective-permute-done | bytes 131104 | tf_op jit(solution)/shard_map/ppermute | solution.py:35
  15.4 3.8 %shard_map.77 = (f32[4,4,2,128,128]{4,3,2,1,0:T(8,128)S(1)}, f32[4,2,128,128]{3,2,1,0:T(8,128)S(1)}, s32[2,1,1,4]{3,2,1,0:T(1,128)S(1)}, f32[2,128,128]{2,1,0:T(...) custom-call(s32[2,1,1,4]{3,2,1,0:T(1,128)} %at_in.1, ...), custom_call_target="tpu_custom_call" | custom-call | flops 1610612736 | bytes 4194304 | tf_op jit(solution)/shard_map/pallas_call | solution.py:237
  19.2 0.1 collective-permute-done.4.corner
  19.3 7.6 %shard_map.78 = (f32[4,2,128,128]{3,2,1,0:T(8,128)S(1)}, f32[2,2,128,256]{3,2,1,0:T(8,128)S(1)}, f32[2,2,128,256]{3,2,1,0:T(8,128)S(1)}) custom-call(s32[2,1,1,4]{3,2,1,0:T(1,128)S(1)} %get-tuple-element.16.at, s32[1,1]{1,0:T(1,128)S(6)} %copy.14.count, f32[2,128,128]{2,1,0:T(8,128)S(1)} %get-tuple-element.17.own, ...), custom_call_target="tpu_custom_call" | custom-call | flops 4831838208 | bytes 4194304 | tf_op jit(solution)/shard_map/pallas_call | solution.py:237
  26.9 1.6 %collective-permute-start.5 = (f32[512,128]{1,0:T(8,128)S(1)}, f32[512,128]{1,0:T(8,128)S(1)}, u32[]{:S(2)}, u32[]{:S(2)}) collective-permute-start(f32[512,128]{1,0:T(8,128)S(1)} %dynamic-slice_bitcast_fusion), channel_id=1, source_target_pairs={{0,4},{4,0},{8,12},{12,8},{16,20},{20,16},{24,28},{28,24},{1,5},{5... | collective-permute-start | bytes 786440 | tf_op jit(solution)/shard_map/ppermute | solution.py:40
  28.5 1.2 %collective-permute-done.5 = f32[512,128]{1,0:T(8,128)S(1)} collective-permute-done((f32[512,128]{1,0:T(8,128)S(1)}, f32[512,128]{1,0:T(8,128)S(1)}, u32[]{:S(2)}, u32[]{:S(2)}) %collective-permute-start.5) | collective-permute-done | bytes 262176 | tf_op jit(solution)/shard_map/ppermute | solution.py:40
  29.8 1.9 %collective-permute-start.8 = (f32[128,128]{1,0:T(8,128)S(1)}, f32[128,128]{1,0:T(8,128)S(1)}, u32[]{:S(2)}, u32[]{:S(2)}) collective-permute-start(f32[128,128]{1,0:T(8,128)S(1)} %get-tuple-element.31), channel_id=1, source_target_pairs={{0,24},{4,28},{8,16},{12,20},{16,8},{20,12},{24,0},{28,4},{1,25},{... | collective-permute-start | bytes 196616 | tf_op jit(solution)/shard_map/ppermute | solution.py:40
  31.6 2.0 %collective-permute-start.7 = (f32[128,128]{1,0:T(8,128)S(1)}, f32[128,128]{1,0:T(8,128)S(1)}, u32[]{:S(2)}, u32[]{:S(2)}) collective-permute-start(f32[128,128]{1,0:T(8,128)S(1)} %get-tuple-element.32), channel_id=1, source_target_pairs={{0,16},{4,20},{8,24},{12,28},{16,0},{20,4},{24,8},{28,12},{1,17},{... | collective-permute-start | bytes 196616 | tf_op jit(solution)/shard_map/ppermute | solution.py:40
  33.7 1.5 %collective-permute-done.8 = f32[128,128]{1,0:T(8,128)S(1)} collective-permute-done((f32[128,128]{1,0:T(8,128)S(1)}, f32[128,128]{1,0:T(8,128)S(1)}, u32[]{:S(2)}, u32[]{:S(2)}) %collective-permute-start.8) | collective-permute-done | bytes 65568 | tf_op jit(solution)/shard_map/ppermute | solution.py:40
  35.1 1.4 %collective-permute-done.7 = f32[128,128]{1,0:T(8,128)S(1)} collective-permute-done((f32[128,128]{1,0:T(8,128)S(1)}, f32[128,128]{1,0:T(8,128)S(1)}, u32[]{:S(2)}, u32[]{:S(2)}) %collective-permute-start.7) | collective-permute-done | bytes 65568 | tf_op jit(solution)/shard_map/ppermute | solution.py:40
  36.5 1.4 %collective-permute-done.6 = f32[128,128]{1,0:T(8,128)S(1)} collective-permute-done((f32[128,128]{1,0:T(8,128)S(1)}, f32[128,128]{1,0:T(8,128)S(1)}, u32[]{:S(2)}, u32[]{:S(2)}) %collective-permute-start.6) | collective-permute-done | bytes 65568 | tf_op jit(solution)/shard_map/ppermute | solution.py:40
  38.0 0.1 collective-permute-start.10
  38.1 4.4 %collective-permute-done.10 = f32[128,128]{1,0:T(8,128)S(1)} collective-permute-done((f32[128,128]{1,0:T(8,128)S(1)}, f32[128,128]{1,0:T(8,128)S(1)}, u32[]{:S(2)}, u32[]{:S(2)}) %collective-permute-start.10) | collective-permute-done | bytes 65568 | tf_op jit(solution)/shard_map/ppermute | solution.py:40
  42.5 0.2 collective-permute-start.11
  42.8 5.7 %collective-permute-done.11 = f32[128,128]{1,0:T(8,128)S(1)} collective-permute-done((f32[128,128]{1,0:T(8,128)S(1)}, f32[128,128]{1,0:T(8,128)S(1)}, u32[]{:S(2)}, u32[]{:S(2)}) %collective-permute-start.11) | collective-permute-done | bytes 65568 | tf_op jit(solution)/shard_map/ppermute | solution.py:40
  48.5 0.1 add.75
  48.6 1.3 %collective-permute-start.13 = (f32[128,128]{1,0:T(8,128)S(1)}, f32[128,128]{1,0:T(8,128)S(1)}, u32[]{:S(2)}, u32[]{:S(2)}) collective-permute-start(f32[128,128]{1,0:T(8,128)S(1)} %add.77), channel_id=1, source_target_pairs={{0,8},{4,12},{8,0},{12,4},{16,24},{20,28},{24,16},{28,20},{1,9},{5... | collective-permute-start | bytes 196616 | tf_op jit(solution)/shard_map/ppermute | solution.py:40
  49.9 0.9 %collective-permute-start.14 = (f32[128,128]{1,0:T(8,128)S(1)}, f32[128,128]{1,0:T(8,128)S(1)}, u32[]{:S(2)}, u32[]{:S(2)}) collective-permute-start(f32[128,128]{1,0:T(8,128)S(1)} %add.77), channel_id=1, source_target_pairs={{0,16},{4,20},{8,24},{12,28},{16,0},{20,4},{24,8},{28,12},{1,17},{... | collective-permute-start | bytes 196616 | tf_op jit(solution)/shard_map/ppermute | solution.py:40
  50.8 1.4 %collective-permute-start.15 = (f32[128,128]{1,0:T(8,128)S(1)}, f32[128,128]{1,0:T(8,128)S(1)}, u32[]{:S(2)}, u32[]{:S(2)}) collective-permute-start(f32[128,128]{1,0:T(8,128)S(1)} %add.77), channel_id=1, source_target_pairs={{0,24},{4,28},{8,16},{12,20},{16,8},{20,12},{24,0},{28,4},{1,25},{... | collective-permute-start | bytes 196616 | tf_op jit(solution)/shard_map/ppermute | solution.py:40
  52.2 0.7 %collective-permute-done.13 = f32[128,128]{1,0:T(8,128)S(1)} collective-permute-done((f32[128,128]{1,0:T(8,128)S(1)}, f32[128,128]{1,0:T(8,128)S(1)}, u32[]{:S(2)}, u32[]{:S(2)}) %collective-permute-start.13) | collective-permute-done | bytes 65568 | tf_op jit(solution)/shard_map/ppermute | solution.py:40
  53.0 1.9 %collective-permute-done.14 = f32[128,128]{1,0:T(8,128)S(1)} collective-permute-done((f32[128,128]{1,0:T(8,128)S(1)}, f32[128,128]{1,0:T(8,128)S(1)}, u32[]{:S(2)}, u32[]{:S(2)}) %collective-permute-start.14) | collective-permute-done | bytes 65568 | tf_op jit(solution)/shard_map/ppermute | solution.py:40
  54.8 1.1 %collective-permute-done.15 = f32[128,128]{1,0:T(8,128)S(1)} collective-permute-done((f32[128,128]{1,0:T(8,128)S(1)}, f32[128,128]{1,0:T(8,128)S(1)}, u32[]{:S(2)}, u32[]{:S(2)}) %collective-permute-start.15) | collective-permute-done | bytes 65568 | tf_op jit(solution)/shard_map/ppermute | solution.py:40
  56.0 0.1 collective-permute-start.16
  56.1 4.9 %collective-permute-done.12 = f32[2,2,128,128]{3,2,1,0:T(8,128)S(1)} collective-permute-done((f32[2,2,128,128]{3,2,1,0:T(8,128)S(1)}, f32[2,2,128,128]{3,2,1,0:T(8,128)S(1)}, u32[]{:S(2)}, u32[]{:S(2)}) %collective-permute-start.12) | collective-permute-done | bytes 262176 | tf_op jit(solution)/shard_map/ppermute | solution.py:17
  61.0 0.7 %slice_add_fusion = f32[2,2,128,128]{3,2,1,0:T(8,128)} fusion(f32[2,2,128,128]{3,2,1,0:T(8,128)S(1)} %collective-permute-done.12, f32[2,2,128,256]{3,2,1,0:T(8,128)S(1)} %add.75), kind=kLoop, calls=%fused_computation | loop fusion | flops 65536 | bytes 786432 | tf_op jit(solution)/shard_map/add | solution.py:298
  61.8 0.8 %copy-done = f32[2,512,128]{2,1,0:T(8,128)} copy-done((f32[2,512,128]{2,1,0:T(8,128)}, f32[2,512,128]{2,1,0:T(8,128)S(1)}, u32[]{:S(2)}) %copy-start) | copy-done | bytes 524312
  (24 shorter events, 0.3 us)
Async XLA Ops:
  0.6 14.7 %collective-permute-start.1 = (f32[2,2,128,128]{3,2,1,0:T(8,128)}, f32[2,2,128,128]{3,2,1,0:T(8,128)S(1)}, u32[]{:S(2)}, u32[]{:S(2)}) collective-permute-start(f32[2,2,128,128]{3,2,1,0:T(8,128)} %tile.1), channel_id=1, source_target_pairs={{0,28},{4,0},{8,4},{12,8},{16,12},{20,16},{24,20},{28,24},{1,29},{... | collective-permute-start | bytes 786440 | tf_op jit(solution)/shard_map/ppermute | solution.py:17
  5.0 9.5 %collective-permute-start = (f32[2,128,128]{2,1,0:T(8,128)S(1)}, f32[2,128,128]{2,1,0:T(8,128)S(1)}, u32[]{:S(2)}, u32[]{:S(2)}) collective-permute-start(f32[2,128,128]{2,1,0:T(8,128)S(1)} %get-tuple-element.34), channel_id=1, source_target_pairs={{0,3},{1,0},{2,1},{3,2},{4,7},{5,4},{6,5},{7,6},{8,11},{9,8},{10,9... | collective-permute-start | bytes 393224 | tf_op jit(solution)/shard_map/ppermute | solution.py:17
  8.7 6.7 %collective-permute-start.2 = (f32[2,128,128]{2,1,0:T(8,128)S(1)}, f32[2,128,128]{2,1,0:T(8,128)S(1)}, u32[]{:S(2)}, u32[]{:S(2)}) collective-permute-start(f32[2,128,128]{2,1,0:T(8,128)S(1)} %get-tuple-element.34), channel_id=1, source_target_pairs={{0,3},{1,29},{2,30},{3,31},{4,7},{5,0},{6,1},{7,2},{8,11},{9,4},{1... | collective-permute-start | bytes 393224 | tf_op jit(solution)/shard_map/ppermute | solution.py:35
  11.0 8.1 %collective-permute-start.3 = (f32[2,128,128]{2,1,0:T(8,128)S(1)}, f32[2,128,128]{2,1,0:T(8,128)S(1)}, u32[]{:S(2)}, u32[]{:S(2)}) collective-permute-start(f32[2,128,128]{2,1,0:T(8,128)S(1)} %get-tuple-element.33), channel_id=1, source_target_pairs={{0,3},{1,0},{2,1},{3,2},{4,7},{5,4},{6,5},{7,6},{8,11},{9,8},{10,9... | collective-permute-start | bytes 393224 | tf_op jit(solution)/shard_map/ppermute | solution.py:17
  11.5 7.8 %collective-permute-start.4 = (f32[2,128,128]{2,1,0:T(8,128)S(1)}, f32[2,128,128]{2,1,0:T(8,128)S(1)}, u32[]{:S(2)}, u32[]{:S(2)}) collective-permute-start(f32[2,128,128]{2,1,0:T(8,128)S(1)} %get-tuple-element.33), channel_id=1, source_target_pairs={{0,3},{1,29},{2,30},{3,31},{4,7},{5,0},{6,1},{7,2},{8,11},{9,4},{1... | collective-permute-start | bytes 393224 | tf_op jit(solution)/shard_map/ppermute | solution.py:35
  26.9 2.7 %collective-permute-start.5 = (f32[512,128]{1,0:T(8,128)S(1)}, f32[512,128]{1,0:T(8,128)S(1)}, u32[]{:S(2)}, u32[]{:S(2)}) collective-permute-start(f32[512,128]{1,0:T(8,128)S(1)} %dynamic-slice_bitcast_fusion), channel_id=1, source_target_pairs={{0,4},{4,0},{8,12},{12,8},{16,20},{20,16},{24,28},{28,24},{1,5},{5... | collective-permute-start | bytes 786440 | tf_op jit(solution)/shard_map/ppermute | solution.py:40
  29.8 5.4 %collective-permute-start.8 = (f32[128,128]{1,0:T(8,128)S(1)}, f32[128,128]{1,0:T(8,128)S(1)}, u32[]{:S(2)}, u32[]{:S(2)}) collective-permute-start(f32[128,128]{1,0:T(8,128)S(1)} %get-tuple-element.31), channel_id=1, source_target_pairs={{0,24},{4,28},{8,16},{12,20},{16,8},{20,12},{24,0},{28,4},{1,25},{... | collective-permute-start | bytes 196616 | tf_op jit(solution)/shard_map/ppermute | solution.py:40
  31.6 4.9 %collective-permute-start.7 = (f32[128,128]{1,0:T(8,128)S(1)}, f32[128,128]{1,0:T(8,128)S(1)}, u32[]{:S(2)}, u32[]{:S(2)}) collective-permute-start(f32[128,128]{1,0:T(8,128)S(1)} %get-tuple-element.32), channel_id=1, source_target_pairs={{0,16},{4,20},{8,24},{12,28},{16,0},{20,4},{24,8},{28,12},{1,17},{... | collective-permute-start | bytes 196616 | tf_op jit(solution)/shard_map/ppermute | solution.py:40
  33.7 4.3 %collective-permute-start.6 = (f32[128,128]{1,0:T(8,128)S(1)}, f32[128,128]{1,0:T(8,128)S(1)}, u32[]{:S(2)}, u32[]{:S(2)}) collective-permute-start(f32[128,128]{1,0:T(8,128)S(1)} %get-tuple-element.30), channel_id=1, source_target_pairs={{0,8},{4,12},{8,0},{12,4},{16,24},{20,28},{24,16},{28,20},{1,9},{5... | collective-permute-start | bytes 196616 | tf_op jit(solution)/shard_map/ppermute | solution.py:40
  38.0 10.5 %collective-permute-start.9 = (f32[2,2,128,256]{3,2,1,0:T(8,128)S(1)}, f32[2,2,128,256]{3,2,1,0:T(8,128)S(1)}, u32[]{:S(2)}, u32[]{:S(2)}) collective-permute-start(f32[2,2,128,256]{3,2,1,0:T(8,128)S(1)} %get-tuple-element.26), channel_id=1, source_target_pairs={{0,4},{4,8},{8,12},{12,16},{16,20},{20,24},{24,28},{28,0},{1,5},{5... | collective-permute-start | bytes 1572872 | tf_op jit(solution)/shard_map/ppermute | solution.py:17
  38.0 4.5 %collective-permute-start.10 = (f32[128,128]{1,0:T(8,128)S(1)}, f32[128,128]{1,0:T(8,128)S(1)}, u32[]{:S(2)}, u32[]{:S(2)}) collective-permute-start(f32[128,128]{1,0:T(8,128)S(1)} %fusion.1), channel_id=1, source_target_pairs={{0,1},{1,0},{2,3},{3,2},{4,5},{5,4},{6,7},{7,6},{8,9},{9,8},{10,11... | collective-permute-start | bytes 196616 | tf_op jit(solution)/shard_map/ppermute | solution.py:40
  42.5 5.9 %collective-permute-start.11 = (f32[128,128]{1,0:T(8,128)S(1)}, f32[128,128]{1,0:T(8,128)S(1)}, u32[]{:S(2)}, u32[]{:S(2)}) collective-permute-start(f32[128,128]{1,0:T(8,128)S(1)} %add.76), channel_id=1, source_target_pairs={{0,2},{1,3},{2,0},{3,1},{4,6},{5,7},{6,4},{7,5},{8,10},{9,11},{10,... | collective-permute-start | bytes 196616 | tf_op jit(solution)/shard_map/ppermute | solution.py:40
  48.6 4.3 %collective-permute-start.13 = (f32[128,128]{1,0:T(8,128)S(1)}, f32[128,128]{1,0:T(8,128)S(1)}, u32[]{:S(2)}, u32[]{:S(2)}) collective-permute-start(f32[128,128]{1,0:T(8,128)S(1)} %add.77), channel_id=1, source_target_pairs={{0,8},{4,12},{8,0},{12,4},{16,24},{20,28},{24,16},{28,20},{1,9},{5... | collective-permute-start | bytes 196616 | tf_op jit(solution)/shard_map/ppermute | solution.py:40
  49.9 5.0 %collective-permute-start.14 = (f32[128,128]{1,0:T(8,128)S(1)}, f32[128,128]{1,0:T(8,128)S(1)}, u32[]{:S(2)}, u32[]{:S(2)}) collective-permute-start(f32[128,128]{1,0:T(8,128)S(1)} %add.77), channel_id=1, source_target_pairs={{0,16},{4,20},{8,24},{12,28},{16,0},{20,4},{24,8},{28,12},{1,17},{... | collective-permute-start | bytes 196616 | tf_op jit(solution)/shard_map/ppermute | solution.py:40
  50.8 5.2 %collective-permute-start.15 = (f32[128,128]{1,0:T(8,128)S(1)}, f32[128,128]{1,0:T(8,128)S(1)}, u32[]{:S(2)}, u32[]{:S(2)}) collective-permute-start(f32[128,128]{1,0:T(8,128)S(1)} %add.77), channel_id=1, source_target_pairs={{0,24},{4,28},{8,16},{12,20},{16,8},{20,12},{24,0},{28,4},{1,25},{... | collective-permute-start | bytes 196616 | tf_op jit(solution)/shard_map/ppermute | solution.py:40
  52.2 8.8 %collective-permute-start.12 = (f32[2,2,128,128]{3,2,1,0:T(8,128)S(1)}, f32[2,2,128,128]{3,2,1,0:T(8,128)S(1)}, u32[]{:S(2)}, u32[]{:S(2)}) collective-permute-start(f32[2,2,128,128]{3,2,1,0:T(8,128)S(1)} %slice.19), channel_id=1, source_target_pairs={{0,1},{1,2},{2,3},{3,0},{4,5},{5,6},{6,7},{7,4},{8,9},{9,10},{10,1... | collective-permute-start | bytes 786440 | tf_op jit(solution)/shard_map/ppermute | solution.py:17
  56.0 5.8 %collective-permute-start.16 = (f32[512,128]{1,0:T(8,128)S(1)}, f32[512,128]{1,0:T(8,128)S(1)}, u32[]{:S(2)}, u32[]{:S(2)}) collective-permute-start(f32[512,128]{1,0:T(8,128)S(1)} %bitcast.40), channel_id=1, source_target_pairs={{0,4},{4,0},{8,12},{12,8},{16,20},{20,16},{24,28},{28,24},{1,5},{5... | collective-permute-start | bytes 786440 | tf_op jit(solution)/shard_map/ppermute | solution.py:40
  61.8 0.8 %copy-start = (f32[2,512,128]{2,1,0:T(8,128)}, f32[2,512,128]{2,1,0:T(8,128)S(1)}, u32[]{:S(2)}) copy-start(f32[2,512,128]{2,1,0:T(8,128)S(1)} %bitcast_dynamic-update-slice_fusion) | copy-start | bytes 1572868

commit v4 on v3

--- a/solution.py
+++ b/solution.py
@@ -23,15 +23,26 @@
     def target(a, b):
         if a > 0 and b > 0:
             return a - 1, b - 1
-        if b > 0:
-            return rows - 1, b
-        return (a, cols - 1) if a < rows - 1 else (a, b)
+        if a == 0:
+            return (rows - 1, b) if b < cols - 1 else (1, b)
+        return (a if a > 1 else 0), cols - 1
 
     pairs = []
     for a in range(rows):
         for b in range(cols):
             down, over = target(a, b)
             pairs.append((a * cols + b, down * cols + over))
+    return lax.ppermute(array, ("ty", "tx"), pairs)
+
+
+def moved_open(array, axis, by):
+    length = lax.axis_size(axis)
+    return lax.ppermute(array, axis, [(i, i + by) for i in range(length) if 0 <= i + by < length])
+
+
+def corner_open(array):
+    rows, cols = lax.axis_size("ty"), lax.axis_size("tx")
+    pairs = [(a * cols + b, (a - 1) * cols + b - 1) for a in range(1, rows) for b in range(1, cols)]
     return lax.ppermute(array, ("ty", "tx"), pairs)
 
 
@@ -258,10 +269,10 @@
     flops = slots * modes * 2 * size * (2 * size) * (6 * size) * 2
     wide = pltpu.VMEM((2, 2 * size, 2 * size), F32)
 
-    right_0 = moved(object_slices[0], "tx", -1)
+    right_0 = moved_open(object_slices[0], "tx", -1)
     corner_0 = from_corner(object_slices[0])
     down = moved(object_slices, "ty", -1)
-    right_1 = moved(object_slices[1], "tx", -1)
+    right_1 = moved_open(object_slices[1], "tx", -1)
     corner_1 = from_corner(object_slices[1])
 
     psi, window, at, own, *rest = call(
@@ -290,12 +301,14 @@
     while bit < lax.axis_size("tx"):
         part = part + swapped(part, "tx", bit)
         bit *= 2
+    part, from_above = lax.optimization_barrier((part, from_above))
     g_wide = g_upper + from_above
-    g_right, part = lax.optimization_barrier((g_wide[..., size:], part))
+    g_right, g_own = lax.optimization_barrier((g_wide[..., size:], g_wide[..., :size]))
     from_left_tile = moved(g_right, "tx", 1)
+    part, g_right = lax.optimization_barrier((part, g_right))
     part = gathered(part, "ty", 2, rows // 2)
     part = gathered(part, "ty", 1, 2)
-    object_grad = g_wide[..., :size] + from_left_tile
+    object_grad = g_own + from_left_tile
     return object_grad, part.reshape(probe.shape)
 
 

time: 62.8 us -> 58.3 us (0.928)
  waiting for transfers between devices: 25.2 us -> 18 us
  starting transfers between devices: 21.7 us -> 24.3 us
    ppermute x5 -> x3, waiting for transfers between devices: 4.88 us -> 0.68 us  [moved(): lax.ppermute(array, axis, [(i, (i + by) % length) for i in range(length)])]
    ppermute x5 -> x3, starting transfers between devices: 7.54 us -> 3.67 us  [moved(): lax.ppermute(array, axis, [(i, (i + by) % length) for i in range(length)])]
    ppermute x10, starting transfers between devices: 9.43 us -> 13.1 us  [swapped(): return lax.ppermute(array, axis, [(i, i ^ bit) for i in range(length)])]
    ppermute x10, waiting for transfers between devices: 19.3 us -> 15.9 us  [swapped(): return lax.ppermute(array, axis, [(i, i ^ bit) for i in range(length)])]
    ppermute x0 -> x2, starting transfers between devices: none -> 2.57 us  [moved_open(): lax.ppermute(array, axis, [(i, i + by) for i in range(length) if 0 <= i +...]
  transfers between devices with their start and end apart: 17 -> 17, of which waited for: 12 -> 11; matrix products, arithmetic and copies ran while one was open for 3% -> 3% of each run, Pallas kernels for 6% -> 7%
where the time goes in v4:
time: 58.3 us; the launch traced here: 58.1 us
  starting transfers between devices  24.3 us (42%)
  waiting for transfers between devices  18 us (31%)
  Pallas kernels  11.4 us (20%)
  local copies, waits for them, and re-layouts  2 us (3%)
  between operations  1.48 us (3%)
  other arithmetic  0.86 us (1%)
    ppermute x10, waiting for transfers between devices, swapped(): return lax.ppermute(array, axis, [(i, i ^ bit) for i in range(length)])  15.9 us
    ppermute x10, starting transfers between devices, swapped(): return lax.ppermute(array, axis, [(i, i ^ bit) for i in range(length)])  13.1 us
    pallas_call x2, Pallas kernels, call(): pl.pallas_call(kernel, in_specs=in_specs, out_specs=[VMEM] * len(outs), o...  11.4 us
    ppermute x2, starting transfers between devices, from_corner(): return lax.ppermute(array, ('ty', 'tx'), pairs)  4.89 us
    ppermute x3, starting transfers between devices, moved(): lax.ppermute(array, axis, [(i, (i + by) % length) for i in range(length)])  3.67 us
    ppermute x2, starting transfers between devices, moved_open(): lax.ppermute(array, axis, [(i, i + by) for i in range(length) if 0 <= i +...  2.57 us
    ppermute x2, waiting for transfers between devices, from_corner(): return lax.ppermute(array, ('ty', 'tx'), pairs)  1.46 us
  transfers between devices with their start and end apart: 17, of which 11 were waited for; matrix products, arithmetic and copies ran while one was open for 3% of the time, Pallas kernels for 7%

profile of v4, /device:TPU:0, one launch (start us, length us, event | category | flops | bytes accessed | tf_op | source)
XLA Modules:
  0.0 58.1 jit_solution(1151462841030401231)
XLA Ops:
  0.6 3.4 %collective-permute-start.1 = (f32[2,2,128,128]{3,2,1,0:T(8,128)}, f32[2,2,128,128]{3,2,1,0:T(8,128)S(1)}, u32[]{:S(2)}, u32[]{:S(2)}) collective-permute-start(f32[2,2,128,128]{3,2,1,0:T(8,128)} %tile.1), channel_id=1, source_target_pairs={{0,28},{4,0},{8,4},{12,8},{16,12},{20,16},{24,20},{28,24},{1,29},{... | collective-permute-start | bytes 786440 | tf_op jit(solution)/shard_map/ppermute | solution.py:17
  4.0 1.0 %slice_bitcast_fusion = (f32[2,128,128]{2,1,0:T(8,128)S(1)}, f32[2,128,128]{2,1,0:T(8,128)S(1)}) fusion(f32[2,2,128,128]{3,2,1,0:T(8,128)} %tile.1), kind=kLoop, calls=%fused_computation.4 | loop fusion | bytes 524288 | tf_op jit(solution)/shard_map/squeeze | solution.py:275
  5.0 1.3 %collective-permute-start = (f32[2,128,128]{2,1,0:T(8,128)S(1)}, f32[2,128,128]{2,1,0:T(8,128)S(1)}, u32[]{:S(2)}, u32[]{:S(2)}) collective-permute-start(f32[2,128,128]{2,1,0:T(8,128)S(1)} %get-tuple-element.42), channel_id=1, source_target_pairs={{1,0},{2,1},{3,2},{5,4},{6,5},{7,6},{9,8},{10,9},{11,10},{13,12},{... | collective-permute-start | bytes 393224 | tf_op jit(solution)/shard_map/ppermute | solution.py:40
  6.3 0.7 %collective-permute-start.2 = (f32[2,128,128]{2,1,0:T(8,128)S(1)}, f32[2,128,128]{2,1,0:T(8,128)S(1)}, u32[]{:S(2)}, u32[]{:S(2)}) collective-permute-start(f32[2,128,128]{2,1,0:T(8,128)S(1)} %get-tuple-element.42), channel_id=1, source_target_pairs={{0,28},{1,29},{2,30},{3,7},{4,3},{5,0},{6,1},{7,2},{8,11},{9,4},{1... | collective-permute-start | bytes 393224 | tf_op jit(solution)/shard_map/ppermute | solution.py:35
  7.0 1.3 %collective-permute-start.3 = (f32[2,128,128]{2,1,0:T(8,128)S(1)}, f32[2,128,128]{2,1,0:T(8,128)S(1)}, u32[]{:S(2)}, u32[]{:S(2)}) collective-permute-start(f32[2,128,128]{2,1,0:T(8,128)S(1)} %get-tuple-element.41), channel_id=1, source_target_pairs={{1,0},{2,1},{3,2},{5,4},{6,5},{7,6},{9,8},{10,9},{11,10},{13,12},{... | collective-permute-start | bytes 393224 | tf_op jit(solution)/shard_map/ppermute | solution.py:40
  8.3 4.2 %collective-permute-start.4 = (f32[2,128,128]{2,1,0:T(8,128)S(1)}, f32[2,128,128]{2,1,0:T(8,128)S(1)}, u32[]{:S(2)}, u32[]{:S(2)}) collective-permute-start(f32[2,128,128]{2,1,0:T(8,128)S(1)} %get-tuple-element.41), channel_id=1, source_target_pairs={{0,28},{1,29},{2,30},{3,7},{4,3},{5,0},{6,1},{7,2},{8,11},{9,4},{1... | collective-permute-start | bytes 393224 | tf_op jit(solution)/shard_map/ppermute | solution.py:35
  13.2 3.8 %shard_map.77 = (f32[4,4,2,128,128]{4,3,2,1,0:T(8,128)S(1)}, f32[4,2,128,128]{3,2,1,0:T(8,128)S(1)}, s32[2,1,1,4]{3,2,1,0:T(1,128)S(1)}, f32[2,128,128]{2,1,0:T(...) custom-call(s32[2,1,1,4]{3,2,1,0:T(1,128)} %at_in.1, ...), custom_call_target="tpu_custom_call" | custom-call | flops 1610612736 | bytes 4194304 | tf_op jit(solution)/shard_map/pallas_call | solution.py:248
  17.0 1.5 %collective-permute-done.4.corner = f32[2,128,128]{2,1,0:T(8,128)S(1)} collective-permute-done((f32[2,128,128]{2,1,0:T(8,128)S(1)}, f32[2,128,128]{2,1,0:T(8,128)S(1)}, u32[]{:S(2)}, u32[]{:S(2)}) %collective-permute-start.4) | collective-permute-done | bytes 131104 | tf_op jit(solution)/shard_map/ppermute | solution.py:35
  18.4 7.6 %shard_map.78 = (f32[4,2,128,128]{3,2,1,0:T(8,128)S(1)}, f32[2,2,128,256]{3,2,1,0:T(8,128)S(1)}, f32[2,2,128,256]{3,2,1,0:T(8,128)S(1)}) custom-call(s32[2,1,1,4]{3,2,1,0:T(1,128)S(1)} %get-tuple-element.19.at, s32[1,1]{1,0:T(1,128)S(6)} %copy.14.count, f32[2,128,128]{2,1,0:T(8,128)S(1)} %get-tuple-element.20.own, ...), custom_call_target="tpu_custom_call" | custom-call | flops 4831838208 | bytes 4194304 | tf_op jit(solution)/shard_map/pallas_call | solution.py:248
  26.1 1.7 %collective-permute-start.5 = (f32[512,128]{1,0:T(8,128)S(1)}, f32[512,128]{1,0:T(8,128)S(1)}, u32[]{:S(2)}, u32[]{:S(2)}) collective-permute-start(f32[512,128]{1,0:T(8,128)S(1)} %dynamic-slice_bitcast_fusion), channel_id=1, source_target_pairs={{0,4},{4,0},{8,12},{12,8},{16,20},{20,16},{24,28},{28,24},{1,5},{5... | collective-permute-start | bytes 786440 | tf_op jit(solution)/shard_map/ppermute | solution.py:51
  27.8 1.2 %collective-permute-done.5 = f32[512,128]{1,0:T(8,128)S(1)} collective-permute-done((f32[512,128]{1,0:T(8,128)S(1)}, f32[512,128]{1,0:T(8,128)S(1)}, u32[]{:S(2)}, u32[]{:S(2)}) %collective-permute-start.5) | collective-permute-done | bytes 262176 | tf_op jit(solution)/shard_map/ppermute | solution.py:51
  29.0 1.3 %collective-permute-start.8 = (f32[128,128]{1,0:T(8,128)S(1)}, f32[128,128]{1,0:T(8,128)S(1)}, u32[]{:S(2)}, u32[]{:S(2)}) collective-permute-start(f32[128,128]{1,0:T(8,128)S(1)} %get-tuple-element.39), channel_id=1, source_target_pairs={{0,24},{4,28},{8,16},{12,20},{16,8},{20,12},{24,0},{28,4},{1,25},{... | collective-permute-start | bytes 196616 | tf_op jit(solution)/shard_map/ppermute | solution.py:51
  30.3 1.7 %collective-permute-start.7 = (f32[128,128]{1,0:T(8,128)S(1)}, f32[128,128]{1,0:T(8,128)S(1)}, u32[]{:S(2)}, u32[]{:S(2)}) collective-permute-start(f32[128,128]{1,0:T(8,128)S(1)} %get-tuple-element.40), channel_id=1, source_target_pairs={{0,16},{4,20},{8,24},{12,28},{16,0},{20,4},{24,8},{28,12},{1,17},{... | collective-permute-start | bytes 196616 | tf_op jit(solution)/shard_map/ppermute | solution.py:51
  32.1 0.5 collective-permute-start.6
  32.6 2.0 %collective-permute-done.8 = f32[128,128]{1,0:T(8,128)S(1)} collective-permute-done((f32[128,128]{1,0:T(8,128)S(1)}, f32[128,128]{1,0:T(8,128)S(1)}, u32[]{:S(2)}, u32[]{:S(2)}) %collective-permute-start.8) | collective-permute-done | bytes 65568 | tf_op jit(solution)/shard_map/ppermute | solution.py:51
  34.6 1.2 %collective-permute-done.7 = f32[128,128]{1,0:T(8,128)S(1)} collective-permute-done((f32[128,128]{1,0:T(8,128)S(1)}, f32[128,128]{1,0:T(8,128)S(1)}, u32[]{:S(2)}, u32[]{:S(2)}) %collective-permute-start.7) | collective-permute-done | bytes 65568 | tf_op jit(solution)/shard_map/ppermute | solution.py:51
  35.8 0.6 collective-permute-done.6
  36.4 1.6 %collective-permute-start.9 = (f32[128,128]{1,0:T(8,128)S(1)}, f32[128,128]{1,0:T(8,128)S(1)}, u32[]{:S(2)}, u32[]{:S(2)}) collective-permute-start(f32[128,128]{1,0:T(8,128)S(1)} %fusion.1), channel_id=1, source_target_pairs={{0,1},{1,0},{2,3},{3,2},{4,5},{5,4},{6,7},{7,6},{8,9},{9,8},{10,11... | collective-permute-start | bytes 196616 | tf_op jit(solution)/shard_map/ppermute | solution.py:51
  38.1 3.4 %collective-permute-done.9 = f32[128,128]{1,0:T(8,128)S(1)} collective-permute-done((f32[128,128]{1,0:T(8,128)S(1)}, f32[128,128]{1,0:T(8,128)S(1)}, u32[]{:S(2)}, u32[]{:S(2)}) %collective-permute-start.9) | collective-permute-done | bytes 65568 | tf_op jit(solution)/shard_map/ppermute | solution.py:51
  41.5 2.7 %collective-permute-start.10 = (f32[128,128]{1,0:T(8,128)S(1)}, f32[128,128]{1,0:T(8,128)S(1)}, u32[]{:S(2)}, u32[]{:S(2)}) collective-permute-start(f32[128,128]{1,0:T(8,128)S(1)} %add.75), channel_id=1, source_target_pairs={{0,2},{1,3},{2,0},{3,1},{4,6},{5,7},{6,4},{7,5},{8,10},{9,11},{10,... | collective-permute-start | bytes 196616 | tf_op jit(solution)/shard_map/ppermute | solution.py:51
  44.1 4.0 %collective-permute-done.10 = f32[128,128]{1,0:T(8,128)S(1)} collective-permute-done((f32[128,128]{1,0:T(8,128)S(1)}, f32[128,128]{1,0:T(8,128)S(1)}, u32[]{:S(2)}, u32[]{:S(2)}) %collective-permute-start.10) | collective-permute-done | bytes 65568 | tf_op jit(solution)/shard_map/ppermute | solution.py:51
  48.3 0.2 collective-permute-start.12
  48.5 0.9 %collective-permute-start.13 = (f32[128,128]{1,0:T(8,128)S(1)}, f32[128,128]{1,0:T(8,128)S(1)}, u32[]{:S(2)}, u32[]{:S(2)}) collective-permute-start(f32[128,128]{1,0:T(8,128)S(1)} %add.76), channel_id=1, source_target_pairs={{0,8},{4,12},{8,0},{12,4},{16,24},{20,28},{24,16},{28,20},{1,9},{5... | collective-permute-start | bytes 196616 | tf_op jit(solution)/shard_map/ppermute | solution.py:51
  49.4 1.1 %collective-permute-start.14 = (f32[128,128]{1,0:T(8,128)S(1)}, f32[128,128]{1,0:T(8,128)S(1)}, u32[]{:S(2)}, u32[]{:S(2)}) collective-permute-start(f32[128,128]{1,0:T(8,128)S(1)} %add.76), channel_id=1, source_target_pairs={{0,16},{4,20},{8,24},{12,28},{16,0},{20,4},{24,8},{28,12},{1,17},{... | collective-permute-start | bytes 196616 | tf_op jit(solution)/shard_map/ppermute | solution.py:51
  50.5 1.5 %collective-permute-start.15 = (f32[128,128]{1,0:T(8,128)S(1)}, f32[128,128]{1,0:T(8,128)S(1)}, u32[]{:S(2)}, u32[]{:S(2)}) collective-permute-start(f32[128,128]{1,0:T(8,128)S(1)} %add.76), channel_id=1, source_target_pairs={{0,24},{4,28},{8,16},{12,20},{16,8},{20,12},{24,0},{28,4},{1,25},{... | collective-permute-start | bytes 196616 | tf_op jit(solution)/shard_map/ppermute | solution.py:51
  52.0 1.1 %collective-permute-done.13 = f32[128,128]{1,0:T(8,128)S(1)} collective-permute-done((f32[128,128]{1,0:T(8,128)S(1)}, f32[128,128]{1,0:T(8,128)S(1)}, u32[]{:S(2)}, u32[]{:S(2)}) %collective-permute-start.13) | collective-permute-done | bytes 65568 | tf_op jit(solution)/shard_map/ppermute | solution.py:51
  53.1 1.1 %collective-permute-done.14 = f32[128,128]{1,0:T(8,128)S(1)} collective-permute-done((f32[128,128]{1,0:T(8,128)S(1)}, f32[128,128]{1,0:T(8,128)S(1)}, u32[]{:S(2)}, u32[]{:S(2)}) %collective-permute-start.14) | collective-permute-done | bytes 65568 | tf_op jit(solution)/shard_map/ppermute | solution.py:51
  54.3 1.4 %collective-permute-done.15 = f32[128,128]{1,0:T(8,128)S(1)} collective-permute-done((f32[128,128]{1,0:T(8,128)S(1)}, f32[128,128]{1,0:T(8,128)S(1)}, u32[]{:S(2)}, u32[]{:S(2)}) %collective-permute-start.15) | collective-permute-done | bytes 65568 | tf_op jit(solution)/shard_map/ppermute | solution.py:51
  55.6 0.1 collective-permute-start.16
  55.8 0.7 %collective-permute-done.12 = f32[2,2,128,128]{3,2,1,0:T(8,128)S(1)} collective-permute-done((f32[2,2,128,128]{3,2,1,0:T(8,128)S(1)}, f32[2,2,128,128]{3,2,1,0:T(8,128)S(1)}, u32[]{:S(2)}, u32[]{:S(2)}) %collective-permute-start.12) | collective-permute-done | bytes 262176 | tf_op jit(solution)/shard_map/ppermute | solution.py:17
  56.5 0.7 %add.78 = f32[2,2,128,128]{3,2,1,0:T(8,128)} add(f32[2,2,128,128]{3,2,1,0:T(8,128)S(1)} %get-tuple-element.32, f32[2,2,128,128]{3,2,1,0:T(8,128)S(1)} %collective-permute-done.12) | non-fusion elementwise | flops 65536 | bytes 786432 | tf_op jit(solution)/shard_map/add | solution.py:311
  57.3 0.8 %copy-done = f32[2,512,128]{2,1,0:T(8,128)} copy-done((f32[2,512,128]{2,1,0:T(8,128)}, f32[2,512,128]{2,1,0:T(8,128)S(1)}, u32[]{:S(2)}) %copy-start) | copy-done | bytes 524312
  (24 shorter events, 0.5 us)
Async XLA Ops:
  0.6 12.5 %collective-permute-start.1 = (f32[2,2,128,128]{3,2,1,0:T(8,128)}, f32[2,2,128,128]{3,2,1,0:T(8,128)S(1)}, u32[]{:S(2)}, u32[]{:S(2)}) collective-permute-start(f32[2,2,128,128]{3,2,1,0:T(8,128)} %tile.1), channel_id=1, source_target_pairs={{0,28},{4,0},{8,4},{12,8},{16,12},{20,16},{24,20},{28,24},{1,29},{... | collective-permute-start | bytes 786440 | tf_op jit(solution)/shard_map/ppermute | solution.py:17
  5.0 8.1 %collective-permute-start = (f32[2,128,128]{2,1,0:T(8,128)S(1)}, f32[2,128,128]{2,1,0:T(8,128)S(1)}, u32[]{:S(2)}, u32[]{:S(2)}) collective-permute-start(f32[2,128,128]{2,1,0:T(8,128)S(1)} %get-tuple-element.42), channel_id=1, source_target_pairs={{1,0},{2,1},{3,2},{5,4},{6,5},{7,6},{9,8},{10,9},{11,10},{13,12},{... | collective-permute-start | bytes 393224 | tf_op jit(solution)/shard_map/ppermute | solution.py:40
  6.3 6.8 %collective-permute-start.2 = (f32[2,128,128]{2,1,0:T(8,128)S(1)}, f32[2,128,128]{2,1,0:T(8,128)S(1)}, u32[]{:S(2)}, u32[]{:S(2)}) collective-permute-start(f32[2,128,128]{2,1,0:T(8,128)S(1)} %get-tuple-element.42), channel_id=1, source_target_pairs={{0,28},{1,29},{2,30},{3,7},{4,3},{5,0},{6,1},{7,2},{8,11},{9,4},{1... | collective-permute-start | bytes 393224 | tf_op jit(solution)/shard_map/ppermute | solution.py:35
  7.0 9.9 %collective-permute-start.3 = (f32[2,128,128]{2,1,0:T(8,128)S(1)}, f32[2,128,128]{2,1,0:T(8,128)S(1)}, u32[]{:S(2)}, u32[]{:S(2)}) collective-permute-start(f32[2,128,128]{2,1,0:T(8,128)S(1)} %get-tuple-element.41), channel_id=1, source_target_pairs={{1,0},{2,1},{3,2},{5,4},{6,5},{7,6},{9,8},{10,9},{11,10},{13,12},{... | collective-permute-start | bytes 393224 | tf_op jit(solution)/shard_map/ppermute | solution.py:40
  8.3 10.1 %collective-permute-start.4 = (f32[2,128,128]{2,1,0:T(8,128)S(1)}, f32[2,128,128]{2,1,0:T(8,128)S(1)}, u32[]{:S(2)}, u32[]{:S(2)}) collective-permute-start(f32[2,128,128]{2,1,0:T(8,128)S(1)} %get-tuple-element.41), channel_id=1, source_target_pairs={{0,28},{1,29},{2,30},{3,7},{4,3},{5,0},{6,1},{7,2},{8,11},{9,4},{1... | collective-permute-start | bytes 393224 | tf_op jit(solution)/shard_map/ppermute | solution.py:35
  26.1 2.9 %collective-permute-start.5 = (f32[512,128]{1,0:T(8,128)S(1)}, f32[512,128]{1,0:T(8,128)S(1)}, u32[]{:S(2)}, u32[]{:S(2)}) collective-permute-start(f32[512,128]{1,0:T(8,128)S(1)} %dynamic-slice_bitcast_fusion), channel_id=1, source_target_pairs={{0,4},{4,0},{8,12},{12,8},{16,20},{20,16},{24,28},{28,24},{1,5},{5... | collective-permute-start | bytes 786440 | tf_op jit(solution)/shard_map/ppermute | solution.py:51
  29.0 5.5 %collective-permute-start.8 = (f32[128,128]{1,0:T(8,128)S(1)}, f32[128,128]{1,0:T(8,128)S(1)}, u32[]{:S(2)}, u32[]{:S(2)}) collective-permute-start(f32[128,128]{1,0:T(8,128)S(1)} %get-tuple-element.39), channel_id=1, source_target_pairs={{0,24},{4,28},{8,16},{12,20},{16,8},{20,12},{24,0},{28,4},{1,25},{... | collective-permute-start | bytes 196616 | tf_op jit(solution)/shard_map/ppermute | solution.py:51
  30.3 5.4 %collective-permute-start.7 = (f32[128,128]{1,0:T(8,128)S(1)}, f32[128,128]{1,0:T(8,128)S(1)}, u32[]{:S(2)}, u32[]{:S(2)}) collective-permute-start(f32[128,128]{1,0:T(8,128)S(1)} %get-tuple-element.40), channel_id=1, source_target_pairs={{0,16},{4,20},{8,24},{12,28},{16,0},{20,4},{24,8},{28,12},{1,17},{... | collective-permute-start | bytes 196616 | tf_op jit(solution)/shard_map/ppermute | solution.py:51
  32.1 4.3 %collective-permute-start.6 = (f32[128,128]{1,0:T(8,128)S(1)}, f32[128,128]{1,0:T(8,128)S(1)}, u32[]{:S(2)}, u32[]{:S(2)}) collective-permute-start(f32[128,128]{1,0:T(8,128)S(1)} %get-tuple-element.38), channel_id=1, source_target_pairs={{0,8},{4,12},{8,0},{12,4},{16,24},{20,28},{24,16},{28,20},{1,9},{5... | collective-permute-start | bytes 196616 | tf_op jit(solution)/shard_map/ppermute | solution.py:51
  36.4 11.8 %collective-permute-start.11 = (f32[2,2,128,256]{3,2,1,0:T(8,128)S(1)}, f32[2,2,128,256]{3,2,1,0:T(8,128)S(1)}, u32[]{:S(2)}, u32[]{:S(2)}) collective-permute-start(f32[2,2,128,256]{3,2,1,0:T(8,128)S(1)} %get-tuple-element.30), channel_id=1, source_target_pairs={{0,4},{4,8},{8,12},{12,16},{16,20},{20,24},{24,28},{28,0},{1,5},{5... | collective-permute-start | bytes 1572872 | tf_op jit(solution)/shard_map/ppermute | solution.py:17
  36.4 5.0 %collective-permute-start.9 = (f32[128,128]{1,0:T(8,128)S(1)}, f32[128,128]{1,0:T(8,128)S(1)}, u32[]{:S(2)}, u32[]{:S(2)}) collective-permute-start(f32[128,128]{1,0:T(8,128)S(1)} %fusion.1), channel_id=1, source_target_pairs={{0,1},{1,0},{2,3},{3,2},{4,5},{5,4},{6,7},{7,6},{8,9},{9,8},{10,11... | collective-permute-start | bytes 196616 | tf_op jit(solution)/shard_map/ppermute | solution.py:51
  41.5 6.6 %collective-permute-start.10 = (f32[128,128]{1,0:T(8,128)S(1)}, f32[128,128]{1,0:T(8,128)S(1)}, u32[]{:S(2)}, u32[]{:S(2)}) collective-permute-start(f32[128,128]{1,0:T(8,128)S(1)} %add.75), channel_id=1, source_target_pairs={{0,2},{1,3},{2,0},{3,1},{4,6},{5,7},{6,4},{7,5},{8,10},{9,11},{10,... | collective-permute-start | bytes 196616 | tf_op jit(solution)/shard_map/ppermute | solution.py:51
  48.3 8.2 %collective-permute-start.12 = (f32[2,2,128,128]{3,2,1,0:T(8,128)S(1)}, f32[2,2,128,128]{3,2,1,0:T(8,128)S(1)}, u32[]{:S(2)}, u32[]{:S(2)}) collective-permute-start(f32[2,2,128,128]{3,2,1,0:T(8,128)S(1)} %get-tuple-element.33), channel_id=1, source_target_pairs={{0,1},{1,2},{2,3},{3,0},{4,5},{5,6},{6,7},{7,4},{8,9},{9,10},{10,1... | collective-permute-start | bytes 786440 | tf_op jit(solution)/shard_map/ppermute | solution.py:17
  48.5 4.6 %collective-permute-start.13 = (f32[128,128]{1,0:T(8,128)S(1)}, f32[128,128]{1,0:T(8,128)S(1)}, u32[]{:S(2)}, u32[]{:S(2)}) collective-permute-start(f32[128,128]{1,0:T(8,128)S(1)} %add.76), channel_id=1, source_target_pairs={{0,8},{4,12},{8,0},{12,4},{16,24},{20,28},{24,16},{28,20},{1,9},{5... | collective-permute-start | bytes 196616 | tf_op jit(solution)/shard_map/ppermute | solution.py:51
  49.4 4.9 %collective-permute-start.14 = (f32[128,128]{1,0:T(8,128)S(1)}, f32[128,128]{1,0:T(8,128)S(1)}, u32[]{:S(2)}, u32[]{:S(2)}) collective-permute-start(f32[128,128]{1,0:T(8,128)S(1)} %add.76), channel_id=1, source_target_pairs={{0,16},{4,20},{8,24},{12,28},{16,0},{20,4},{24,8},{28,12},{1,17},{... | collective-permute-start | bytes 196616 | tf_op jit(solution)/shard_map/ppermute | solution.py:51
  50.5 5.2 %collective-permute-start.15 = (f32[128,128]{1,0:T(8,128)S(1)}, f32[128,128]{1,0:T(8,128)S(1)}, u32[]{:S(2)}, u32[]{:S(2)}) collective-permute-start(f32[128,128]{1,0:T(8,128)S(1)} %add.76), channel_id=1, source_target_pairs={{0,24},{4,28},{8,16},{12,20},{16,8},{20,12},{24,0},{28,4},{1,25},{... | collective-permute-start | bytes 196616 | tf_op jit(solution)/shard_map/ppermute | solution.py:51
  55.6 1.6 %collective-permute-start.16 = (f32[512,128]{1,0:T(8,128)S(1)}, f32[512,128]{1,0:T(8,128)S(1)}, u32[]{:S(2)}, u32[]{:S(2)}) collective-permute-start(f32[512,128]{1,0:T(8,128)S(1)} %bitcast.40), channel_id=1, source_target_pairs={{0,4},{4,0},{8,12},{12,8},{16,20},{20,16},{24,28},{28,24},{1,5},{5... | collective-permute-start | bytes 786440 | tf_op jit(solution)/shard_map/ppermute | solution.py:51
  57.3 0.8 %copy-start = (f32[2,512,128]{2,1,0:T(8,128)}, f32[2,512,128]{2,1,0:T(8,128)S(1)}, u32[]{:S(2)}) copy-start(f32[2,512,128]{2,1,0:T(8,128)S(1)} %bitcast_dynamic-update-slice_fusion) | copy-start | bytes 1572868

commit v5 on v4

--- a/solution.py
+++ b/solution.py
@@ -140,7 +140,8 @@
     return (a[0] * b[0] - a[1] * b[1], a[0] * b[1] + a[1] * b[0])
 
 
-def fill(wide, right, down, corner, size):
+def fill(wide, own, right, down, corner, size):
+    wide[:, :size, :size] = own[...]
     wide[:, :size, size:] = right[...]
     wide[:, size:, :size] = down[...]
     wide[:, size:, size:] = corner[...]
@@ -172,19 +173,21 @@
         total[c, rows, :] += pltpu.roll(padded, col, axis=1)
 
 
-def first_kernel(at_in, tile, probe_in, table_in, measured_in, right, down, corner,
-                 psi, window, at_out, own, probe, table, measured, at, wide, sems):
+def near_kernel(*refs):
+    count = (len(refs) - 1) // 2
+    copies = [
+        pltpu.make_async_copy(refs[i], refs[count + i], refs[-1].at[i]) for i in range(count)
+    ]
+    for copy in copies:
+        copy.start()
+    for copy in copies:
+        copy.wait()
+
+
+def first_kernel(at, tile, probe, table, right, down, corner, psi, window, wide):
     size = right.shape[-1]
     slots, modes = psi.shape[:2]
-    soon = [(at_in, at), (tile.at[0], wide.at[:, pl.ds(0, size), pl.ds(0, size)]), (probe_in, probe),
-            (table_in, table)]
-    later = [(tile.at[1], own), (measured_in, measured), (at_in, at_out)]
-    copies = [pltpu.make_async_copy(a, b, sems.at[i]) for i, (a, b) in enumerate(soon + later)]
-    for copy in copies:
-        copy.start()
-    fill(wide, right, down.at[0], corner, size)
-    for copy in copies[:len(soon)]:
-        copy.wait()
+    fill(wide, tile.at[0], right, down.at[0], corner, size)
     fields = []
     for slot in range(slots):
         w = window_of(wide, at, slot, size)
@@ -193,17 +196,13 @@
     waves = both_sides(fields, *sided(table[1]))
     for i, wave in enumerate(waves):
         psi[i // modes, i % modes, 0], psi[i // modes, i % modes, 1] = wave
-    for copy in copies[len(soon):]:
-        copy.wait()
-
-
-def second_kernel(at, count, own, right, down, corner, psi, window, probe, measured, table,
-                  g_probe, g_upper, g_lower, wide, total):
-    size = own.shape[-1]
+
+
+def second_kernel(at, count, tile, right, down, corner, psi, window, probe, measured, table,
+                  g_probe, g_windows, wide):
+    size = right.shape[-1]
     slots, modes = psi.shape[:2]
-    wide[:, :size, :size] = own[...]
-    fill(wide, right, down.at[1], corner, size)
-    total[...] = jnp.zeros_like(total)
+    fill(wide, tile.at[1], right, down.at[1], corner, size)
     dft, through = sided(table[0]), sided(table[1])
     w = [window_of(wide, at, slot, size) for slot in range(slots)]
     waves = [[(psi[s, m, 0], psi[s, m, 1]) for m in range(modes)] for s in range(slots)]
@@ -229,8 +228,16 @@
             (conj, waves[s]),
         )):
             parts = [product(grads[s * modes + m], by[m]) for m in range(modes)]
-            pair = (sum(re for re, _ in parts), -sum(im for _, im in parts))
-            add_window(total.at[layer], at, s, pair, size)
+            g_windows[layer, s, 0] = sum(re for re, _ in parts)
+            g_windows[layer, s, 1] = -sum(im for _, im in parts)
+
+
+def object_kernel(at, g_windows, g_upper, g_lower, total):
+    layers, slots, _, size, _ = g_windows.shape
+    total[...] = jnp.zeros_like(total)
+    for s in range(slots):
+        for layer in range(layers):
+            add_window(total.at[layer], at, s, (g_windows[layer, s, 0], g_windows[layer, s, 1]), size)
     g_upper[...] = total[:, :, :size, :]
     g_lower[...] = total[:, :, size:, :]
 
@@ -251,7 +258,7 @@
         out_specs=[VMEM] * len(outs),
         out_shape=outs,
         scratch_shapes=scratch,
-        compiler_params=pltpu.CompilerParams(vmem_limit_bytes=40 * 1024 * 1024),
+        compiler_params=pltpu.CompilerParams(vmem_limit_bytes=24 * 1024 * 1024),
         cost_estimate=pl.CostEstimate(flops=flops, bytes_accessed=4 * 1024 * 1024, transcendentals=0),
     )(*args)
 
@@ -270,31 +277,39 @@
     wide = pltpu.VMEM((2, 2 * size, 2 * size), F32)
 
     right_0 = moved_open(object_slices[0], "tx", -1)
-    corner_0 = from_corner(object_slices[0])
+    right_1 = moved_open(object_slices[1], "tx", -1)
     down = moved(object_slices, "ty", -1)
-    right_1 = moved_open(object_slices[1], "tx", -1)
-    corner_1 = from_corner(object_slices[1])
-
-    psi, window, at, own, *rest = call(
+    corner_0 = moved(right_0, "ty", -1)
+    corner_1 = moved(right_1, "ty", -1)
+    far = (offsets, object_slices, probe, table, measured)
+    at, tile, probe_near, table_near, measured_near = call(
+        near_kernel, far, [HBM] * len(far), [shaped(a.shape, a.dtype) for a in far],
+        [pltpu.SemaphoreType.DMA((len(far),))], flops,
+    )
+    psi, window = call(
         first_kernel,
-        (offsets, object_slices, probe, table, measured, right_0, down, corner_0),
-        [HBM] * 5 + [VMEM] * 3,
-        [shaped((slots, modes, 2, size, size)), shaped((slots, 2, size, size)), shaped(offsets.shape, jnp.int32),
-         shaped((2, size, size)), shaped(probe.shape), shaped(table.shape, BF16), shaped(measured.shape)],
-        [pltpu.SMEM(offsets.shape, jnp.int32), wide, pltpu.SemaphoreType.DMA((7,))], flops,
-    )
-    probe_near, table_near, measured_near = rest
-    g_probe, g_upper, g_lower = call(
+        (at, tile, probe_near, table_near, right_0, down, corner_0),
+        [SMEM] + [VMEM] * 6,
+        [shaped((slots, modes, 2, size, size)), shaped((slots, 2, size, size))],
+        [wide], flops,
+    )
+    g_probe, g_windows = call(
         second_kernel,
-        (at, counts, own, right_1, down, corner_1, psi, window, probe_near, measured_near, table_near),
+        (at, counts, tile, right_1, down, corner_1, psi, window, probe_near, measured_near, table_near),
         [SMEM] * 2 + [VMEM] * 9,
-        [shaped(probe.shape)] + [shaped((layers, 2, size, 2 * size))] * 2,
-        [wide, pltpu.VMEM((layers, 2, 2 * size, 2 * size), F32)], 3 * flops,
+        [shaped(probe.shape), shaped((layers, slots, 2, size, size))],
+        [wide], 3 * flops,
     )
 
     rows = lax.axis_size("ty")
     part = scattered(g_probe.reshape(-1, size), "ty", 1, 2)
+    part, g_windows = lax.optimization_barrier((part, g_windows))
     part = scattered(part, "ty", 2, rows // 2)
+    g_upper, g_lower = call(
+        object_kernel, (at, g_windows), [SMEM, VMEM],
+        [shaped((layers, 2, size, 2 * size))] * 2,
+        [pltpu.VMEM((layers, 2, 2 * size, 2 * size), F32)], flops // 4,
+    )
     part, g_lower = lax.optimization_barrier((part, g_lower))
     from_above = moved(g_lower, "ty", 1)
     bit = 1

time: 58.3 us -> 55.9 us (0.959)
  starting transfers between devices: 24.3 us -> 20.2 us
  Pallas kernels: 11.4 us -> 12.7 us
    ppermute x2 -> x0, starting transfers between devices: 4.89 us -> none  [from_corner(): return lax.ppermute(array, ('ty', 'tx'), pairs)]
    ppermute x2, waiting for transfers between devices: 0.01 us -> 2.76 us  [moved_open(): lax.ppermute(array, axis, [(i, i + by) for i in range(length) if 0 <= i +...]
    ppermute x3 -> x5, starting transfers between devices: 3.67 us -> 6.27 us  [moved(): lax.ppermute(array, axis, [(i, (i + by) % length) for i in range(length)])]
    ppermute x10, starting transfers between devices: 13.1 us -> 11.4 us  [swapped(): return lax.ppermute(array, axis, [(i, i ^ bit) for i in range(length)])]
    ppermute x2 -> x0, waiting for transfers between devices: 1.46 us -> none  [from_corner(): return lax.ppermute(array, ('ty', 'tx'), pairs)]
    pallas_call x2 -> x4, Pallas kernels: 11.4 us -> 12.7 us  [call(): pl.pallas_call(kernel, in_specs=in_specs, out_specs=[VMEM] * len(outs), o...]
    ppermute x10, waiting for transfers between devices: 15.9 us -> 14.8 us  [swapped(): return lax.ppermute(array, axis, [(i, i ^ bit) for i in range(length)])]
  transfers between devices with their start and end apart: 17 -> 17, of which waited for: 11 -> 12; matrix products, arithmetic and copies ran while one was open for 3% -> 2% of each run, Pallas kernels for 7% -> 10%
where the time goes in v5:
time: 55.9 us; the launch traced here: 55.7 us
  starting transfers between devices  20.2 us (36%)
  waiting for transfers between devices  18.4 us (33%)
  Pallas kernels  12.7 us (23%)
  local copies, waits for them, and re-layouts  2 us (4%)
  between operations  1.54 us (3%)
  other arithmetic  0.87 us (2%)
    ppermute x10, waiting for transfers between devices, swapped(): return lax.ppermute(array, axis, [(i, i ^ bit) for i in range(length)])  14.8 us
    pallas_call x4, Pallas kernels, call(): pl.pallas_call(kernel, in_specs=in_specs, out_specs=[VMEM] * len(outs), o...  12.7 us
    ppermute x10, starting transfers between devices, swapped(): return lax.ppermute(array, axis, [(i, i ^ bit) for i in range(length)])  11.4 us
    ppermute x5, starting transfers between devices, moved(): lax.ppermute(array, axis, [(i, (i + by) % length) for i in range(length)])  6.27 us
    ppermute x2, waiting for transfers between devices, moved_open(): lax.ppermute(array, axis, [(i, i + by) for i in range(length) if 0 <= i +...  2.76 us
    ppermute x2, starting transfers between devices, moved_open(): lax.ppermute(array, axis, [(i, i + by) for i in range(length) if 0 <= i +...  2.57 us
  transfers between devices with their start and end apart: 17, of which 12 were waited for; matrix products, arithmetic and copies ran while one was open for 2% of the time, Pallas kernels for 10%

profile of v5, /device:TPU:0, one launch (start us, length us, event | category | flops | bytes accessed | tf_op | source)
XLA Modules:
  0.0 55.7 jit_solution(14832981842991798879)
XLA Ops:
  0.6 1.0 %slice_bitcast_fusion = (f32[2,128,128]{2,1,0:T(8,128)S(1)}, f32[2,128,128]{2,1,0:T(8,128)S(1)}) fusion(f32[2,2,128,128]{3,2,1,0:T(8,128)} %refs_1_.1), kind=kLoop, calls=%fused_computation.4 | loop fusion | bytes 524288 | tf_op jit(solution)/shard_map/squeeze | solution.py:279
  1.6 1.3 %collective-permute-start.3 = (f32[2,128,128]{2,1,0:T(8,128)S(1)}, f32[2,128,128]{2,1,0:T(8,128)S(1)}, u32[]{:S(2)}, u32[]{:S(2)}) collective-permute-start(f32[2,128,128]{2,1,0:T(8,128)S(1)} %get-tuple-element.47), channel_id=1, source_target_pairs={{1,0},{2,1},{3,2},{5,4},{6,5},{7,6},{9,8},{10,9},{11,10},{13,12},{... | collective-permute-start | bytes 393224 | tf_op jit(solution)/shard_map/ppermute | solution.py:40
  2.9 3.4 %collective-permute-start.1 = (f32[2,2,128,128]{3,2,1,0:T(8,128)}, f32[2,2,128,128]{3,2,1,0:T(8,128)S(1)}, u32[]{:S(2)}, u32[]{:S(2)}) collective-permute-start(f32[2,2,128,128]{3,2,1,0:T(8,128)} %refs_1_.1), channel_id=1, source_target_pairs={{0,28},{4,0},{8,4},{12,8},{16,12},{20,16},{24,20},{28,24},{1,29},{... | collective-permute-start | bytes 786440 | tf_op jit(solution)/shard_map/ppermute | solution.py:17
  6.3 1.3 %collective-permute-start = (f32[2,128,128]{2,1,0:T(8,128)S(1)}, f32[2,128,128]{2,1,0:T(8,128)S(1)}, u32[]{:S(2)}, u32[]{:S(2)}) collective-permute-start(f32[2,128,128]{2,1,0:T(8,128)S(1)} %get-tuple-element.48), channel_id=1, source_target_pairs={{1,0},{2,1},{3,2},{5,4},{6,5},{7,6},{9,8},{10,9},{11,10},{13,12},{... | collective-permute-start | bytes 393224 | tf_op jit(solution)/shard_map/ppermute | solution.py:40
  8.3 1.9 %collective-permute-done.3.right = f32[2,128,128]{2,1,0:T(8,128)S(1)} collective-permute-done((f32[2,128,128]{2,1,0:T(8,128)S(1)}, f32[2,128,128]{2,1,0:T(8,128)S(1)}, u32[]{:S(2)}, u32[]{:S(2)}) %collective-permute-start.3) | collective-permute-done | bytes 131104 | tf_op jit(solution)/shard_map/ppermute | solution.py:40
  10.1 1.1 %collective-permute-start.4 = (f32[2,128,128]{2,1,0:T(8,128)S(1)}, f32[2,128,128]{2,1,0:T(8,128)S(1)}, u32[]{:S(2)}, u32[]{:S(2)}) collective-permute-start(f32[2,128,128]{2,1,0:T(8,128)S(1)} %collective-permute-done.3.right), channel_id=1, source_target_pairs={{0,28},{4,0},{8,4},{12,8},{16,12},{20,16},{24,20},{28,24},{1,29},{... | collective-permute-start | bytes 393224 | tf_op jit(solution)/shard_map/ppermute | solution.py:17
  11.2 1.4 %shard_map.77 = (s32[2,1,1,4]{3,2,1,0:T(1,128)S(1)}, f32[2,2,128,128]{3,2,1,0:T(8,128)S(1)}, f32[4,2,128,128]{3,2,1,0:T(8,128)S(1)}, bf16[2,2,256,256]{3,2,1,0:T(8,128)(2,1)S(1)}, f32[4,128,128]{2,1,0:T(8,128)S(1)}) custom-call(s32[2,1,1,4]{3,2,1,0:T(1,128)} %refs_0_.1, f32[2,2,128,128]{3,2,1,0:T(8,128)} %refs_1_.1, f32[4,2,128,128]{3,2,1,0:T(8,128)} %refs_2_.1, ...), custom_call_target="tpu_custom_call" | custom-call | flops 1610612736 | bytes 4194304 | tf_op jit(solution)/shard_map/pallas_call | solution.py:255
  12.6 0.9 %collective-permute-done.right = f32[2,128,128]{2,1,0:T(8,128)S(1)} collective-permute-done((f32[2,128,128]{2,1,0:T(8,128)S(1)}, f32[2,128,128]{2,1,0:T(8,128)S(1)}, u32[]{:S(2)}, u32[]{:S(2)}) %collective-permute-start) | collective-permute-done | bytes 131104 | tf_op jit(solution)/shard_map/ppermute | solution.py:40
  13.5 1.6 %collective-permute-start.2 = (f32[2,128,128]{2,1,0:T(8,128)S(1)}, f32[2,128,128]{2,1,0:T(8,128)S(1)}, u32[]{:S(2)}, u32[]{:S(2)}) collective-permute-start(f32[2,128,128]{2,1,0:T(8,128)S(1)} %collective-permute-done.right), channel_id=1, source_target_pairs={{0,28},{4,0},{8,4},{12,8},{16,12},{20,16},{24,20},{28,24},{1,29},{... | collective-permute-start | bytes 393224 | tf_op jit(solution)/shard_map/ppermute | solution.py:17
  15.1 3.0 %shard_map.78 = (f32[4,4,2,128,128]{4,3,2,1,0:T(8,128)S(1)}, f32[4,2,128,128]{3,2,1,0:T(8,128)S(1)}) custom-call(s32[2,1,1,4]{3,2,1,0:T(1,128)S(1)} %get-tuple-element.22.at, f32[2,2,128,128]{3,2,1,0:T(8,128)S(1)} %get-tuple-element.23.tile, f32[4,2,128,128]{3,2,1,0:T(8,128)S(1)} %get-tuple-element.24.probe, ...), custom_call_target="tpu_custom_call" | custom-call | flops 1610612736 | bytes 4194304 | tf_op jit(solution)/shard_map/pallas_call | solution.py:255
  18.1 7.1 %shard_map.79 = (f32[4,2,128,128]{3,2,1,0:T(8,128)S(1)}, f32[2,4,2,128,128]{4,3,2,1,0:T(8,128)S(1)}) custom-call(s32[2,1,1,4]{3,2,1,0:T(1,128)S(1)} %get-tuple-element.22.at, s32[1,1]{1,0:T(1,128)S(6)} %copy.14.count, f32[2,2,128,128]{3,2,1,0:T(8,128)S(1)} %get-tuple-element.23.tile, f32[2,128,128]{2,1,0:T(8,128)S(1)} %collective-permute-done.right, ...), custom_call_target="tpu_custom_call" | custom-call | flops 4831838208 | bytes 4194304 | tf_op jit(solution)/shard_map/pallas_call | solution.py:255
  25.4 1.5 %collective-permute-done.5 = f32[512,128]{1,0:T(8,128)S(1)} collective-permute-done((f32[512,128]{1,0:T(8,128)S(1)}, f32[512,128]{1,0:T(8,128)S(1)}, u32[]{:S(2)}, u32[]{:S(2)}) %collective-permute-start.5) | collective-permute-done | bytes 262176 | tf_op jit(solution)/shard_map/ppermute | solution.py:51
  26.9 2.4 %collective-permute-start.8 = (f32[128,128]{1,0:T(8,128)S(1)}, f32[128,128]{1,0:T(8,128)S(1)}, u32[]{:S(2)}, u32[]{:S(2)}) collective-permute-start(f32[128,128]{1,0:T(8,128)S(1)} %get-tuple-element.45), channel_id=1, source_target_pairs={{0,24},{4,28},{8,16},{12,20},{16,8},{20,12},{24,0},{28,4},{1,25},{... | collective-permute-start | bytes 196616 | tf_op jit(solution)/shard_map/ppermute | solution.py:51
  29.3 0.5 collective-permute-start.7
  29.8 0.7 %collective-permute-start.6 = (f32[128,128]{1,0:T(8,128)S(1)}, f32[128,128]{1,0:T(8,128)S(1)}, u32[]{:S(2)}, u32[]{:S(2)}) collective-permute-start(f32[128,128]{1,0:T(8,128)S(1)} %get-tuple-element.44), channel_id=1, source_target_pairs={{0,8},{4,12},{8,0},{12,4},{16,24},{20,28},{24,16},{28,20},{1,9},{5... | collective-permute-start | bytes 196616 | tf_op jit(solution)/shard_map/ppermute | solution.py:51
  30.4 1.2 %shard_map.80 = (f32[2,2,128,256]{3,2,1,0:T(8,128)S(1)}, f32[2,2,128,256]{3,2,1,0:T(8,128)S(1)}) custom-call(s32[2,1,1,4]{3,2,1,0:T(1,128)S(1)} %get-tuple-element.22.at, f32[2,4,2,128,128]{4,3,2,1,0:T(8,128)S(1)} %get-tuple-element.31.g_windows), custom_call_target="tpu_custom_call" | custom-call | flops 402653184 | bytes 4194304 | tf_op jit(solution)/shard_map/pallas_call | solution.py:255
  31.7 0.5 collective-permute-done.8
  32.1 1.4 %collective-permute-done.7 = f32[128,128]{1,0:T(8,128)S(1)} collective-permute-done((f32[128,128]{1,0:T(8,128)S(1)}, f32[128,128]{1,0:T(8,128)S(1)}, u32[]{:S(2)}, u32[]{:S(2)}) %collective-permute-start.7) | collective-permute-done | bytes 65568 | tf_op jit(solution)/shard_map/ppermute | solution.py:51
  33.5 0.5 collective-permute-done.6
  34.1 1.6 %collective-permute-start.9 = (f32[128,128]{1,0:T(8,128)S(1)}, f32[128,128]{1,0:T(8,128)S(1)}, u32[]{:S(2)}, u32[]{:S(2)}) collective-permute-start(f32[128,128]{1,0:T(8,128)S(1)} %fusion.1), channel_id=1, source_target_pairs={{0,1},{1,0},{2,3},{3,2},{4,5},{5,4},{6,7},{7,6},{8,9},{9,8},{10,11... | collective-permute-start | bytes 196616 | tf_op jit(solution)/shard_map/ppermute | solution.py:51
  35.7 3.4 %collective-permute-done.9 = f32[128,128]{1,0:T(8,128)S(1)} collective-permute-done((f32[128,128]{1,0:T(8,128)S(1)}, f32[128,128]{1,0:T(8,128)S(1)}, u32[]{:S(2)}, u32[]{:S(2)}) %collective-permute-start.9) | collective-permute-done | bytes 65568 | tf_op jit(solution)/shard_map/ppermute | solution.py:51
  39.1 2.6 %collective-permute-start.10 = (f32[128,128]{1,0:T(8,128)S(1)}, f32[128,128]{1,0:T(8,128)S(1)}, u32[]{:S(2)}, u32[]{:S(2)}) collective-permute-start(f32[128,128]{1,0:T(8,128)S(1)} %add.75), channel_id=1, source_target_pairs={{0,2},{1,3},{2,0},{3,1},{4,6},{5,7},{6,4},{7,5},{8,10},{9,11},{10,... | collective-permute-start | bytes 196616 | tf_op jit(solution)/shard_map/ppermute | solution.py:51
  41.7 4.1 %collective-permute-done.10 = f32[128,128]{1,0:T(8,128)S(1)} collective-permute-done((f32[128,128]{1,0:T(8,128)S(1)}, f32[128,128]{1,0:T(8,128)S(1)}, u32[]{:S(2)}, u32[]{:S(2)}) %collective-permute-start.10) | collective-permute-done | bytes 65568 | tf_op jit(solution)/shard_map/ppermute | solution.py:51
  46.1 0.9 %collective-permute-start.13 = (f32[128,128]{1,0:T(8,128)S(1)}, f32[128,128]{1,0:T(8,128)S(1)}, u32[]{:S(2)}, u32[]{:S(2)}) collective-permute-start(f32[128,128]{1,0:T(8,128)S(1)} %add.76), channel_id=1, source_target_pairs={{0,8},{4,12},{8,0},{12,4},{16,24},{20,28},{24,16},{28,20},{1,9},{5... | collective-permute-start | bytes 196616 | tf_op jit(solution)/shard_map/ppermute | solution.py:51
  47.0 0.9 %collective-permute-start.14 = (f32[128,128]{1,0:T(8,128)S(1)}, f32[128,128]{1,0:T(8,128)S(1)}, u32[]{:S(2)}, u32[]{:S(2)}) collective-permute-start(f32[128,128]{1,0:T(8,128)S(1)} %add.76), channel_id=1, source_target_pairs={{0,16},{4,20},{8,24},{12,28},{16,0},{20,4},{24,8},{28,12},{1,17},{... | collective-permute-start | bytes 196616 | tf_op jit(solution)/shard_map/ppermute | solution.py:51
  47.9 1.6 %collective-permute-start.15 = (f32[128,128]{1,0:T(8,128)S(1)}, f32[128,128]{1,0:T(8,128)S(1)}, u32[]{:S(2)}, u32[]{:S(2)}) collective-permute-start(f32[128,128]{1,0:T(8,128)S(1)} %add.76), channel_id=1, source_target_pairs={{0,24},{4,28},{8,16},{12,20},{16,8},{20,12},{24,0},{28,4},{1,25},{... | collective-permute-start | bytes 196616 | tf_op jit(solution)/shard_map/ppermute | solution.py:51
  49.6 0.7 %collective-permute-done.13 = f32[128,128]{1,0:T(8,128)S(1)} collective-permute-done((f32[128,128]{1,0:T(8,128)S(1)}, f32[128,128]{1,0:T(8,128)S(1)}, u32[]{:S(2)}, u32[]{:S(2)}) %collective-permute-start.13) | collective-permute-done | bytes 65568 | tf_op jit(solution)/shard_map/ppermute | solution.py:51
  50.4 1.6 %collective-permute-done.14 = f32[128,128]{1,0:T(8,128)S(1)} collective-permute-done((f32[128,128]{1,0:T(8,128)S(1)}, f32[128,128]{1,0:T(8,128)S(1)}, u32[]{:S(2)}, u32[]{:S(2)}) %collective-permute-start.14) | collective-permute-done | bytes 65568 | tf_op jit(solution)/shard_map/ppermute | solution.py:51
  52.0 1.1 %collective-permute-done.15 = f32[128,128]{1,0:T(8,128)S(1)} collective-permute-done((f32[128,128]{1,0:T(8,128)S(1)}, f32[128,128]{1,0:T(8,128)S(1)}, u32[]{:S(2)}, u32[]{:S(2)}) %collective-permute-start.15) | collective-permute-done | bytes 65568 | tf_op jit(solution)/shard_map/ppermute | solution.py:51
  53.3 0.9 %collective-permute-done.12 = f32[2,2,128,128]{3,2,1,0:T(8,128)S(1)} collective-permute-done((f32[2,2,128,128]{3,2,1,0:T(8,128)S(1)}, f32[2,2,128,128]{3,2,1,0:T(8,128)S(1)}, u32[]{:S(2)}, u32[]{:S(2)}) %collective-permute-start.12) | collective-permute-done | bytes 262176 | tf_op jit(solution)/shard_map/ppermute | solution.py:17
  54.1 0.7 %add.78 = f32[2,2,128,128]{3,2,1,0:T(8,128)} add(f32[2,2,128,128]{3,2,1,0:T(8,128)S(1)} %get-tuple-element.38, f32[2,2,128,128]{3,2,1,0:T(8,128)S(1)} %collective-permute-done.12) | non-fusion elementwise | flops 65536 | bytes 786432 | tf_op jit(solution)/shard_map/add | solution.py:326
  54.9 0.8 %copy-done = f32[2,512,128]{2,1,0:T(8,128)} copy-done((f32[2,512,128]{2,1,0:T(8,128)}, f32[2,512,128]{2,1,0:T(8,128)S(1)}, u32[]{:S(2)}) %copy-start) | copy-done | bytes 524312
  (26 shorter events, 0.8 us)
Async XLA Ops:
  1.6 8.5 %collective-permute-start.3 = (f32[2,128,128]{2,1,0:T(8,128)S(1)}, f32[2,128,128]{2,1,0:T(8,128)S(1)}, u32[]{:S(2)}, u32[]{:S(2)}) collective-permute-start(f32[2,128,128]{2,1,0:T(8,128)S(1)} %get-tuple-element.47), channel_id=1, source_target_pairs={{1,0},{2,1},{3,2},{5,4},{6,5},{7,6},{9,8},{10,9},{11,10},{13,12},{... | collective-permute-start | bytes 393224 | tf_op jit(solution)/shard_map/ppermute | solution.py:40
  2.9 12.2 %collective-permute-start.1 = (f32[2,2,128,128]{3,2,1,0:T(8,128)}, f32[2,2,128,128]{3,2,1,0:T(8,128)S(1)}, u32[]{:S(2)}, u32[]{:S(2)}) collective-permute-start(f32[2,2,128,128]{3,2,1,0:T(8,128)} %refs_1_.1), channel_id=1, source_target_pairs={{0,28},{4,0},{8,4},{12,8},{16,12},{20,16},{24,20},{28,24},{1,29},{... | collective-permute-start | bytes 786440 | tf_op jit(solution)/shard_map/ppermute | solution.py:17
  6.3 7.2 %collective-permute-start = (f32[2,128,128]{2,1,0:T(8,128)S(1)}, f32[2,128,128]{2,1,0:T(8,128)S(1)}, u32[]{:S(2)}, u32[]{:S(2)}) collective-permute-start(f32[2,128,128]{2,1,0:T(8,128)S(1)} %get-tuple-element.48), channel_id=1, source_target_pairs={{1,0},{2,1},{3,2},{5,4},{6,5},{7,6},{9,8},{10,9},{11,10},{13,12},{... | collective-permute-start | bytes 393224 | tf_op jit(solution)/shard_map/ppermute | solution.py:40
  10.1 4.9 %collective-permute-start.4 = (f32[2,128,128]{2,1,0:T(8,128)S(1)}, f32[2,128,128]{2,1,0:T(8,128)S(1)}, u32[]{:S(2)}, u32[]{:S(2)}) collective-permute-start(f32[2,128,128]{2,1,0:T(8,128)S(1)} %collective-permute-done.3.right), channel_id=1, source_target_pairs={{0,28},{4,0},{8,4},{12,8},{16,12},{20,16},{24,20},{28,24},{1,29},{... | collective-permute-start | bytes 393224 | tf_op jit(solution)/shard_map/ppermute | solution.py:17
  13.5 4.6 %collective-permute-start.2 = (f32[2,128,128]{2,1,0:T(8,128)S(1)}, f32[2,128,128]{2,1,0:T(8,128)S(1)}, u32[]{:S(2)}, u32[]{:S(2)}) collective-permute-start(f32[2,128,128]{2,1,0:T(8,128)S(1)} %collective-permute-done.right), channel_id=1, source_target_pairs={{0,28},{4,0},{8,4},{12,8},{16,12},{20,16},{24,20},{28,24},{1,29},{... | collective-permute-start | bytes 393224 | tf_op jit(solution)/shard_map/ppermute | solution.py:17
  25.2 1.6 %collective-permute-start.5 = (f32[512,128]{1,0:T(8,128)S(1)}, f32[512,128]{1,0:T(8,128)S(1)}, u32[]{:S(2)}, u32[]{:S(2)}) collective-permute-start(f32[512,128]{1,0:T(8,128)S(1)} %dynamic-slice_bitcast_fusion), channel_id=1, source_target_pairs={{0,4},{4,0},{8,12},{12,8},{16,20},{20,16},{24,28},{28,24},{1,5},{5... | collective-permute-start | bytes 786440 | tf_op jit(solution)/shard_map/ppermute | solution.py:51
  26.9 5.2 %collective-permute-start.8 = (f32[128,128]{1,0:T(8,128)S(1)}, f32[128,128]{1,0:T(8,128)S(1)}, u32[]{:S(2)}, u32[]{:S(2)}) collective-permute-start(f32[128,128]{1,0:T(8,128)S(1)} %get-tuple-element.45), channel_id=1, source_target_pairs={{0,24},{4,28},{8,16},{12,20},{16,8},{20,12},{24,0},{28,4},{1,25},{... | collective-permute-start | bytes 196616 | tf_op jit(solution)/shard_map/ppermute | solution.py:51
  29.3 4.3 %collective-permute-start.7 = (f32[128,128]{1,0:T(8,128)S(1)}, f32[128,128]{1,0:T(8,128)S(1)}, u32[]{:S(2)}, u32[]{:S(2)}) collective-permute-start(f32[128,128]{1,0:T(8,128)S(1)} %get-tuple-element.46), channel_id=1, source_target_pairs={{0,16},{4,20},{8,24},{12,28},{16,0},{20,4},{24,8},{28,12},{1,17},{... | collective-permute-start | bytes 196616 | tf_op jit(solution)/shard_map/ppermute | solution.py:51
  29.8 4.3 %collective-permute-start.6 = (f32[128,128]{1,0:T(8,128)S(1)}, f32[128,128]{1,0:T(8,128)S(1)}, u32[]{:S(2)}, u32[]{:S(2)}) collective-permute-start(f32[128,128]{1,0:T(8,128)S(1)} %get-tuple-element.44), channel_id=1, source_target_pairs={{0,8},{4,12},{8,0},{12,4},{16,24},{20,28},{24,16},{28,20},{1,9},{5... | collective-permute-start | bytes 196616 | tf_op jit(solution)/shard_map/ppermute | solution.py:51
  34.1 11.7 %collective-permute-start.11 = (f32[2,2,128,256]{3,2,1,0:T(8,128)S(1)}, f32[2,2,128,256]{3,2,1,0:T(8,128)S(1)}, u32[]{:S(2)}, u32[]{:S(2)}) collective-permute-start(f32[2,2,128,256]{3,2,1,0:T(8,128)S(1)} %get-tuple-element.36), channel_id=1, source_target_pairs={{0,4},{4,8},{8,12},{12,16},{16,20},{20,24},{24,28},{28,0},{1,5},{5... | collective-permute-start | bytes 1572872 | tf_op jit(solution)/shard_map/ppermute | solution.py:17
  34.1 5.0 %collective-permute-start.9 = (f32[128,128]{1,0:T(8,128)S(1)}, f32[128,128]{1,0:T(8,128)S(1)}, u32[]{:S(2)}, u32[]{:S(2)}) collective-permute-start(f32[128,128]{1,0:T(8,128)S(1)} %fusion.1), channel_id=1, source_target_pairs={{0,1},{1,0},{2,3},{3,2},{4,5},{5,4},{6,7},{7,6},{8,9},{9,8},{10,11... | collective-permute-start | bytes 196616 | tf_op jit(solution)/shard_map/ppermute | solution.py:51
  39.1 6.6 %collective-permute-start.10 = (f32[128,128]{1,0:T(8,128)S(1)}, f32[128,128]{1,0:T(8,128)S(1)}, u32[]{:S(2)}, u32[]{:S(2)}) collective-permute-start(f32[128,128]{1,0:T(8,128)S(1)} %add.75), channel_id=1, source_target_pairs={{0,2},{1,3},{2,0},{3,1},{4,6},{5,7},{6,4},{7,5},{8,10},{9,11},{10,... | collective-permute-start | bytes 196616 | tf_op jit(solution)/shard_map/ppermute | solution.py:51
  45.9 8.2 %collective-permute-start.12 = (f32[2,2,128,128]{3,2,1,0:T(8,128)S(1)}, f32[2,2,128,128]{3,2,1,0:T(8,128)S(1)}, u32[]{:S(2)}, u32[]{:S(2)}) collective-permute-start(f32[2,2,128,128]{3,2,1,0:T(8,128)S(1)} %get-tuple-element.39), channel_id=1, source_target_pairs={{0,1},{1,2},{2,3},{3,0},{4,5},{5,6},{6,7},{7,4},{8,9},{9,10},{10,1... | collective-permute-start | bytes 786440 | tf_op jit(solution)/shard_map/ppermute | solution.py:17
  46.1 4.3 %collective-permute-start.13 = (f32[128,128]{1,0:T(8,128)S(1)}, f32[128,128]{1,0:T(8,128)S(1)}, u32[]{:S(2)}, u32[]{:S(2)}) collective-permute-start(f32[128,128]{1,0:T(8,128)S(1)} %add.76), channel_id=1, source_target_pairs={{0,8},{4,12},{8,0},{12,4},{16,24},{20,28},{24,16},{28,20},{1,9},{5... | collective-permute-start | bytes 196616 | tf_op jit(solution)/shard_map/ppermute | solution.py:51
  47.0 5.0 %collective-permute-start.14 = (f32[128,128]{1,0:T(8,128)S(1)}, f32[128,128]{1,0:T(8,128)S(1)}, u32[]{:S(2)}, u32[]{:S(2)}) collective-permute-start(f32[128,128]{1,0:T(8,128)S(1)} %add.76), channel_id=1, source_target_pairs={{0,16},{4,20},{8,24},{12,28},{16,0},{20,4},{24,8},{28,12},{1,17},{... | collective-permute-start | bytes 196616 | tf_op jit(solution)/shard_map/ppermute | solution.py:51
  47.9 5.2 %collective-permute-start.15 = (f32[128,128]{1,0:T(8,128)S(1)}, f32[128,128]{1,0:T(8,128)S(1)}, u32[]{:S(2)}, u32[]{:S(2)}) collective-permute-start(f32[128,128]{1,0:T(8,128)S(1)} %add.76), channel_id=1, source_target_pairs={{0,24},{4,28},{8,16},{12,20},{16,8},{20,12},{24,0},{28,4},{1,25},{... | collective-permute-start | bytes 196616 | tf_op jit(solution)/shard_map/ppermute | solution.py:51
  53.1 1.8 %collective-permute-start.16 = (f32[512,128]{1,0:T(8,128)S(1)}, f32[512,128]{1,0:T(8,128)S(1)}, u32[]{:S(2)}, u32[]{:S(2)}) collective-permute-start(f32[512,128]{1,0:T(8,128)S(1)} %bitcast.40), channel_id=1, source_target_pairs={{0,4},{4,0},{8,12},{12,8},{16,20},{20,16},{24,28},{28,24},{1,5},{5... | collective-permute-start | bytes 786440 | tf_op jit(solution)/shard_map/ppermute | solution.py:51
  54.9 0.8 %copy-start = (f32[2,512,128]{2,1,0:T(8,128)}, f32[2,512,128]{2,1,0:T(8,128)S(1)}, u32[]{:S(2)}) copy-start(f32[2,512,128]{2,1,0:T(8,128)S(1)} %bitcast_dynamic-update-slice_fusion) | copy-start | bytes 1572868

commit v6 on v5

--- a/solution.py
+++ b/solution.py
@@ -66,7 +66,7 @@
     me = (lax.axis_index(axis) // unit) % ways
     out = jnp.zeros((ways,) + part.shape, part.dtype)
     out = lax.dynamic_update_index_in_dim(out, part, me, 0)
-    for d in range(1, ways):
+    for d in range(ways - 1, 0, -1):
         out = lax.dynamic_update_index_in_dim(out, swapped(part, axis, d * unit), me ^ d, 0)
     return out.reshape(-1, part.shape[-1])
 
@@ -284,7 +284,7 @@
     far = (offsets, object_slices, probe, table, measured)
     at, tile, probe_near, table_near, measured_near = call(
         near_kernel, far, [HBM] * len(far), [shaped(a.shape, a.dtype) for a in far],
-        [pltpu.SemaphoreType.DMA((len(far),))], flops,
+        [pltpu.SemaphoreType.DMA((len(far),))], 4 * flops,
     )
     psi, window = call(
         first_kernel,

time: 55.9 us -> 55.6 us (level)
  no operation moved by 1% of the time
where the time goes in v6:
time: 55.6 us; the launch traced here: 55.4 us
  starting transfers between devices  20.4 us (37%)
  waiting for transfers between devices  18.2 us (33%)
  Pallas kernels  12.4 us (22%)
  local copies, waits for them, and re-layouts  2 us (4%)
  between operations  1.55 us (3%)
  other arithmetic  0.86 us (2%)
    ppermute x10, waiting for transfers between devices, swapped(): return lax.ppermute(array, axis, [(i, i ^ bit) for i in range(length)])  14.3 us
    pallas_call x4, Pallas kernels, call(): pl.pallas_call(kernel, in_specs=in_specs, out_specs=[VMEM] * len(outs), o...  12.4 us
    ppermute x10, starting transfers between devices, swapped(): return lax.ppermute(array, axis, [(i, i ^ bit) for i in range(length)])  11.5 us
    ppermute x5, starting transfers between devices, moved(): lax.ppermute(array, axis, [(i, (i + by) % length) for i in range(length)])  6.32 us
    ppermute x2, waiting for transfers between devices, moved_open(): lax.ppermute(array, axis, [(i, i + by) for i in range(length) if 0 <= i +...  2.76 us
    ppermute x2, starting transfers between devices, moved_open(): lax.ppermute(array, axis, [(i, i + by) for i in range(length) if 0 <= i +...  2.57 us
    ppermute x5, waiting for transfers between devices, moved(): lax.ppermute(array, axis, [(i, (i + by) % length) for i in range(length)])  1.22 us
  transfers between devices with their start and end apart: 17, of which 12 were waited for; matrix products, arithmetic and copies ran while one was open for 2% of the time, Pallas kernels for 10%

profile of v6, /device:TPU:0, one launch (start us, length us, event | category | flops | bytes accessed | tf_op | source)
XLA Modules:
  0.0 55.4 jit_solution(16065648118748791967)
XLA Ops:
  0.6 1.0 %slice_bitcast_fusion = (f32[2,128,128]{2,1,0:T(8,128)S(1)}, f32[2,128,128]{2,1,0:T(8,128)S(1)}) fusion(f32[2,2,128,128]{3,2,1,0:T(8,128)} %refs_1_.1), kind=kLoop, calls=%fused_computation.4 | loop fusion | bytes 524288 | tf_op jit(solution)/shard_map/squeeze | solution.py:279
  1.6 1.3 %collective-permute-start.3 = (f32[2,128,128]{2,1,0:T(8,128)S(1)}, f32[2,128,128]{2,1,0:T(8,128)S(1)}, u32[]{:S(2)}, u32[]{:S(2)}) collective-permute-start(f32[2,128,128]{2,1,0:T(8,128)S(1)} %get-tuple-element.47), channel_id=1, source_target_pairs={{1,0},{2,1},{3,2},{5,4},{6,5},{7,6},{9,8},{10,9},{11,10},{13,12},{... | collective-permute-start | bytes 393224 | tf_op jit(solution)/shard_map/ppermute | solution.py:40
  2.9 3.4 %collective-permute-start.1 = (f32[2,2,128,128]{3,2,1,0:T(8,128)}, f32[2,2,128,128]{3,2,1,0:T(8,128)S(1)}, u32[]{:S(2)}, u32[]{:S(2)}) collective-permute-start(f32[2,2,128,128]{3,2,1,0:T(8,128)} %refs_1_.1), channel_id=1, source_target_pairs={{0,28},{4,0},{8,4},{12,8},{16,12},{20,16},{24,20},{28,24},{1,29},{... | collective-permute-start | bytes 786440 | tf_op jit(solution)/shard_map/ppermute | solution.py:17
  6.3 1.3 %collective-permute-start = (f32[2,128,128]{2,1,0:T(8,128)S(1)}, f32[2,128,128]{2,1,0:T(8,128)S(1)}, u32[]{:S(2)}, u32[]{:S(2)}) collective-permute-start(f32[2,128,128]{2,1,0:T(8,128)S(1)} %get-tuple-element.48), channel_id=1, source_target_pairs={{1,0},{2,1},{3,2},{5,4},{6,5},{7,6},{9,8},{10,9},{11,10},{13,12},{... | collective-permute-start | bytes 393224 | tf_op jit(solution)/shard_map/ppermute | solution.py:40
  7.6 2.5 %collective-permute-done.3.right = f32[2,128,128]{2,1,0:T(8,128)S(1)} collective-permute-done((f32[2,128,128]{2,1,0:T(8,128)S(1)}, f32[2,128,128]{2,1,0:T(8,128)S(1)}, u32[]{:S(2)}, u32[]{:S(2)}) %collective-permute-start.3) | collective-permute-done | bytes 131104 | tf_op jit(solution)/shard_map/ppermute | solution.py:40
  10.1 1.1 %collective-permute-start.4 = (f32[2,128,128]{2,1,0:T(8,128)S(1)}, f32[2,128,128]{2,1,0:T(8,128)S(1)}, u32[]{:S(2)}, u32[]{:S(2)}) collective-permute-start(f32[2,128,128]{2,1,0:T(8,128)S(1)} %collective-permute-done.3.right), channel_id=1, source_target_pairs={{0,28},{4,0},{8,4},{12,8},{16,12},{20,16},{24,20},{28,24},{1,29},{... | collective-permute-start | bytes 393224 | tf_op jit(solution)/shard_map/ppermute | solution.py:17
  11.2 1.4 %shard_map.77 = (s32[2,1,1,4]{3,2,1,0:T(1,128)S(1)}, f32[2,2,128,128]{3,2,1,0:T(8,128)S(1)}, f32[4,2,128,128]{3,2,1,0:T(8,128)S(1)}, bf16[2,2,256,256]{3,2,1,0:T(8,128)(2,1)S(1)}, f32[4,128,128]{2,1,0:T(8,128)S(1)}) custom-call(s32[2,1,1,4]{3,2,1,0:T(1,128)} %refs_0_.1, f32[2,2,128,128]{3,2,1,0:T(8,128)} %refs_1_.1, f32[4,2,128,128]{3,2,1,0:T(8,128)} %refs_2_.1, ...), custom_call_target="tpu_custom_call" | custom-call | flops 6442450944 | bytes 4194304 | tf_op jit(solution)/shard_map/pallas_call | solution.py:255
  13.5 1.6 %collective-permute-start.2 = (f32[2,128,128]{2,1,0:T(8,128)S(1)}, f32[2,128,128]{2,1,0:T(8,128)S(1)}, u32[]{:S(2)}, u32[]{:S(2)}) collective-permute-start(f32[2,128,128]{2,1,0:T(8,128)S(1)} %collective-permute-done.right), channel_id=1, source_target_pairs={{0,28},{4,0},{8,4},{12,8},{16,12},{20,16},{24,20},{28,24},{1,29},{... | collective-permute-start | bytes 393224 | tf_op jit(solution)/shard_map/ppermute | solution.py:17
  15.1 2.9 %shard_map.78 = (f32[4,4,2,128,128]{4,3,2,1,0:T(8,128)S(1)}, f32[4,2,128,128]{3,2,1,0:T(8,128)S(1)}) custom-call(s32[2,1,1,4]{3,2,1,0:T(1,128)S(1)} %get-tuple-element.22.at, f32[2,2,128,128]{3,2,1,0:T(8,128)S(1)} %get-tuple-element.23.tile, f32[4,2,128,128]{3,2,1,0:T(8,128)S(1)} %get-tuple-element.24.probe, ...), custom_call_target="tpu_custom_call" | custom-call | flops 1610612736 | bytes 4194304 | tf_op jit(solution)/shard_map/pallas_call | solution.py:255
  18.1 6.8 %shard_map.79 = (f32[4,2,128,128]{3,2,1,0:T(8,128)S(1)}, f32[2,4,2,128,128]{4,3,2,1,0:T(8,128)S(1)}) custom-call(s32[2,1,1,4]{3,2,1,0:T(1,128)S(1)} %get-tuple-element.22.at, s32[1,1]{1,0:T(1,128)S(6)} %copy.14.count, f32[2,2,128,128]{3,2,1,0:T(8,128)S(1)} %get-tuple-element.23.tile, f32[2,128,128]{2,1,0:T(8,128)S(1)} %collective-permute-done.right, ...), custom_call_target="tpu_custom_call" | custom-call | flops 4831838208 | bytes 4194304 | tf_op jit(solution)/shard_map/pallas_call | solution.py:255
  25.1 1.5 %collective-permute-done.5 = f32[512,128]{1,0:T(8,128)S(1)} collective-permute-done((f32[512,128]{1,0:T(8,128)S(1)}, f32[512,128]{1,0:T(8,128)S(1)}, u32[]{:S(2)}, u32[]{:S(2)}) %collective-permute-start.5) | collective-permute-done | bytes 262176 | tf_op jit(solution)/shard_map/ppermute | solution.py:51
  26.6 2.4 %collective-permute-start.8 = (f32[128,128]{1,0:T(8,128)S(1)}, f32[128,128]{1,0:T(8,128)S(1)}, u32[]{:S(2)}, u32[]{:S(2)}) collective-permute-start(f32[128,128]{1,0:T(8,128)S(1)} %get-tuple-element.45), channel_id=1, source_target_pairs={{0,24},{4,28},{8,16},{12,20},{16,8},{20,12},{24,0},{28,4},{1,25},{... | collective-permute-start | bytes 196616 | tf_op jit(solution)/shard_map/ppermute | solution.py:51
  29.0 0.5 collective-permute-start.7
  29.5 0.7 %collective-permute-start.6 = (f32[128,128]{1,0:T(8,128)S(1)}, f32[128,128]{1,0:T(8,128)S(1)}, u32[]{:S(2)}, u32[]{:S(2)}) collective-permute-start(f32[128,128]{1,0:T(8,128)S(1)} %get-tuple-element.44), channel_id=1, source_target_pairs={{0,8},{4,12},{8,0},{12,4},{16,24},{20,28},{24,16},{28,20},{1,9},{5... | collective-permute-start | bytes 196616 | tf_op jit(solution)/shard_map/ppermute | solution.py:51
  30.2 1.2 %shard_map.80 = (f32[2,2,128,256]{3,2,1,0:T(8,128)S(1)}, f32[2,2,128,256]{3,2,1,0:T(8,128)S(1)}) custom-call(s32[2,1,1,4]{3,2,1,0:T(1,128)S(1)} %get-tuple-element.22.at, f32[2,4,2,128,128]{4,3,2,1,0:T(8,128)S(1)} %get-tuple-element.31.g_windows), custom_call_target="tpu_custom_call" | custom-call | flops 402653184 | bytes 4194304 | tf_op jit(solution)/shard_map/pallas_call | solution.py:255
  31.4 0.5 collective-permute-done.8
  31.8 1.4 %collective-permute-done.7 = f32[128,128]{1,0:T(8,128)S(1)} collective-permute-done((f32[128,128]{1,0:T(8,128)S(1)}, f32[128,128]{1,0:T(8,128)S(1)}, u32[]{:S(2)}, u32[]{:S(2)}) %collective-permute-start.7) | collective-permute-done | bytes 65568 | tf_op jit(solution)/shard_map/ppermute | solution.py:51
  33.3 0.5 collective-permute-done.6
  33.8 1.6 %collective-permute-start.9 = (f32[128,128]{1,0:T(8,128)S(1)}, f32[128,128]{1,0:T(8,128)S(1)}, u32[]{:S(2)}, u32[]{:S(2)}) collective-permute-start(f32[128,128]{1,0:T(8,128)S(1)} %fusion.1), channel_id=1, source_target_pairs={{0,1},{1,0},{2,3},{3,2},{4,5},{5,4},{6,7},{7,6},{8,9},{9,8},{10,11... | collective-permute-start | bytes 196616 | tf_op jit(solution)/shard_map/ppermute | solution.py:51
  35.5 3.4 %collective-permute-done.9 = f32[128,128]{1,0:T(8,128)S(1)} collective-permute-done((f32[128,128]{1,0:T(8,128)S(1)}, f32[128,128]{1,0:T(8,128)S(1)}, u32[]{:S(2)}, u32[]{:S(2)}) %collective-permute-start.9) | collective-permute-done | bytes 65568 | tf_op jit(solution)/shard_map/ppermute | solution.py:51
  38.8 2.7 %collective-permute-start.10 = (f32[128,128]{1,0:T(8,128)S(1)}, f32[128,128]{1,0:T(8,128)S(1)}, u32[]{:S(2)}, u32[]{:S(2)}) collective-permute-start(f32[128,128]{1,0:T(8,128)S(1)} %add.75), channel_id=1, source_target_pairs={{0,2},{1,3},{2,0},{3,1},{4,6},{5,7},{6,4},{7,5},{8,10},{9,11},{10,... | collective-permute-start | bytes 196616 | tf_op jit(solution)/shard_map/ppermute | solution.py:51
  41.5 4.0 %collective-permute-done.10 = f32[128,128]{1,0:T(8,128)S(1)} collective-permute-done((f32[128,128]{1,0:T(8,128)S(1)}, f32[128,128]{1,0:T(8,128)S(1)}, u32[]{:S(2)}, u32[]{:S(2)}) %collective-permute-start.10) | collective-permute-done | bytes 65568 | tf_op jit(solution)/shard_map/ppermute | solution.py:51
  45.6 0.2 collective-permute-start.12
  45.8 1.3 %collective-permute-start.13 = (f32[128,128]{1,0:T(8,128)S(1)}, f32[128,128]{1,0:T(8,128)S(1)}, u32[]{:S(2)}, u32[]{:S(2)}) collective-permute-start(f32[128,128]{1,0:T(8,128)S(1)} %add.76), channel_id=1, source_target_pairs={{0,24},{4,28},{8,16},{12,20},{16,8},{20,12},{24,0},{28,4},{1,25},{... | collective-permute-start | bytes 196616 | tf_op jit(solution)/shard_map/ppermute | solution.py:51
  47.1 1.1 %collective-permute-start.14 = (f32[128,128]{1,0:T(8,128)S(1)}, f32[128,128]{1,0:T(8,128)S(1)}, u32[]{:S(2)}, u32[]{:S(2)}) collective-permute-start(f32[128,128]{1,0:T(8,128)S(1)} %add.76), channel_id=1, source_target_pairs={{0,16},{4,20},{8,24},{12,28},{16,0},{20,4},{24,8},{28,12},{1,17},{... | collective-permute-start | bytes 196616 | tf_op jit(solution)/shard_map/ppermute | solution.py:51
  48.2 1.1 %collective-permute-start.15 = (f32[128,128]{1,0:T(8,128)S(1)}, f32[128,128]{1,0:T(8,128)S(1)}, u32[]{:S(2)}, u32[]{:S(2)}) collective-permute-start(f32[128,128]{1,0:T(8,128)S(1)} %add.76), channel_id=1, source_target_pairs={{0,8},{4,12},{8,0},{12,4},{16,24},{20,28},{24,16},{28,20},{1,9},{5... | collective-permute-start | bytes 196616 | tf_op jit(solution)/shard_map/ppermute | solution.py:51
  49.4 2.1 %collective-permute-done.13 = f32[128,128]{1,0:T(8,128)S(1)} collective-permute-done((f32[128,128]{1,0:T(8,128)S(1)}, f32[128,128]{1,0:T(8,128)S(1)}, u32[]{:S(2)}, u32[]{:S(2)}) %collective-permute-start.13) | collective-permute-done | bytes 65568 | tf_op jit(solution)/shard_map/ppermute | solution.py:51
  51.5 0.3 collective-permute-done.14
  51.8 0.6 %collective-permute-done.15 = f32[128,128]{1,0:T(8,128)S(1)} collective-permute-done((f32[128,128]{1,0:T(8,128)S(1)}, f32[128,128]{1,0:T(8,128)S(1)}, u32[]{:S(2)}, u32[]{:S(2)}) %collective-permute-start.15) | collective-permute-done | bytes 65568 | tf_op jit(solution)/shard_map/ppermute | solution.py:51
  52.6 1.2 %collective-permute-done.12 = f32[2,2,128,128]{3,2,1,0:T(8,128)S(1)} collective-permute-done((f32[2,2,128,128]{3,2,1,0:T(8,128)S(1)}, f32[2,2,128,128]{3,2,1,0:T(8,128)S(1)}, u32[]{:S(2)}, u32[]{:S(2)}) %collective-permute-start.12) | collective-permute-done | bytes 262176 | tf_op jit(solution)/shard_map/ppermute | solution.py:17
  53.8 0.7 %add.78 = f32[2,2,128,128]{3,2,1,0:T(8,128)} add(f32[2,2,128,128]{3,2,1,0:T(8,128)S(1)} %get-tuple-element.38, f32[2,2,128,128]{3,2,1,0:T(8,128)S(1)} %collective-permute-done.12) | non-fusion elementwise | flops 65536 | bytes 786432 | tf_op jit(solution)/shard_map/add | solution.py:326
  54.6 0.8 %copy-done = f32[2,512,128]{2,1,0:T(8,128)} copy-done((f32[2,512,128]{2,1,0:T(8,128)}, f32[2,512,128]{2,1,0:T(8,128)S(1)}, u32[]{:S(2)}) %copy-start) | copy-done | bytes 524312
  (26 shorter events, 0.8 us)
Async XLA Ops:
  1.6 8.5 %collective-permute-start.3 = (f32[2,128,128]{2,1,0:T(8,128)S(1)}, f32[2,128,128]{2,1,0:T(8,128)S(1)}, u32[]{:S(2)}, u32[]{:S(2)}) collective-permute-start(f32[2,128,128]{2,1,0:T(8,128)S(1)} %get-tuple-element.47), channel_id=1, source_target_pairs={{1,0},{2,1},{3,2},{5,4},{6,5},{7,6},{9,8},{10,9},{11,10},{13,12},{... | collective-permute-start | bytes 393224 | tf_op jit(solution)/shard_map/ppermute | solution.py:40
  2.9 12.2 %collective-permute-start.1 = (f32[2,2,128,128]{3,2,1,0:T(8,128)}, f32[2,2,128,128]{3,2,1,0:T(8,128)S(1)}, u32[]{:S(2)}, u32[]{:S(2)}) collective-permute-start(f32[2,2,128,128]{3,2,1,0:T(8,128)} %refs_1_.1), channel_id=1, source_target_pairs={{0,28},{4,0},{8,4},{12,8},{16,12},{20,16},{24,20},{28,24},{1,29},{... | collective-permute-start | bytes 786440 | tf_op jit(solution)/shard_map/ppermute | solution.py:17
  6.3 7.2 %collective-permute-start = (f32[2,128,128]{2,1,0:T(8,128)S(1)}, f32[2,128,128]{2,1,0:T(8,128)S(1)}, u32[]{:S(2)}, u32[]{:S(2)}) collective-permute-start(f32[2,128,128]{2,1,0:T(8,128)S(1)} %get-tuple-element.48), channel_id=1, source_target_pairs={{1,0},{2,1},{3,2},{5,4},{6,5},{7,6},{9,8},{10,9},{11,10},{13,12},{... | collective-permute-start | bytes 393224 | tf_op jit(solution)/shard_map/ppermute | solution.py:40
  10.1 4.9 %collective-permute-start.4 = (f32[2,128,128]{2,1,0:T(8,128)S(1)}, f32[2,128,128]{2,1,0:T(8,128)S(1)}, u32[]{:S(2)}, u32[]{:S(2)}) collective-permute-start(f32[2,128,128]{2,1,0:T(8,128)S(1)} %collective-permute-done.3.right), channel_id=1, source_target_pairs={{0,28},{4,0},{8,4},{12,8},{16,12},{20,16},{24,20},{28,24},{1,29},{... | collective-permute-start | bytes 393224 | tf_op jit(solution)/shard_map/ppermute | solution.py:17
  13.5 4.5 %collective-permute-start.2 = (f32[2,128,128]{2,1,0:T(8,128)S(1)}, f32[2,128,128]{2,1,0:T(8,128)S(1)}, u32[]{:S(2)}, u32[]{:S(2)}) collective-permute-start(f32[2,128,128]{2,1,0:T(8,128)S(1)} %collective-permute-done.right), channel_id=1, source_target_pairs={{0,28},{4,0},{8,4},{12,8},{16,12},{20,16},{24,20},{28,24},{1,29},{... | collective-permute-start | bytes 393224 | tf_op jit(solution)/shard_map/ppermute | solution.py:17
  24.9 1.6 %collective-permute-start.5 = (f32[512,128]{1,0:T(8,128)S(1)}, f32[512,128]{1,0:T(8,128)S(1)}, u32[]{:S(2)}, u32[]{:S(2)}) collective-permute-start(f32[512,128]{1,0:T(8,128)S(1)} %dynamic-slice_bitcast_fusion), channel_id=1, source_target_pairs={{0,4},{4,0},{8,12},{12,8},{16,20},{20,16},{24,28},{28,24},{1,5},{5... | collective-permute-start | bytes 786440 | tf_op jit(solution)/shard_map/ppermute | solution.py:51
  26.6 5.2 %collective-permute-start.8 = (f32[128,128]{1,0:T(8,128)S(1)}, f32[128,128]{1,0:T(8,128)S(1)}, u32[]{:S(2)}, u32[]{:S(2)}) collective-permute-start(f32[128,128]{1,0:T(8,128)S(1)} %get-tuple-element.45), channel_id=1, source_target_pairs={{0,24},{4,28},{8,16},{12,20},{16,8},{20,12},{24,0},{28,4},{1,25},{... | collective-permute-start | bytes 196616 | tf_op jit(solution)/shard_map/ppermute | solution.py:51
  29.0 4.3 %collective-permute-start.7 = (f32[128,128]{1,0:T(8,128)S(1)}, f32[128,128]{1,0:T(8,128)S(1)}, u32[]{:S(2)}, u32[]{:S(2)}) collective-permute-start(f32[128,128]{1,0:T(8,128)S(1)} %get-tuple-element.46), channel_id=1, source_target_pairs={{0,16},{4,20},{8,24},{12,28},{16,0},{20,4},{24,8},{28,12},{1,17},{... | collective-permute-start | bytes 196616 | tf_op jit(solution)/shard_map/ppermute | solution.py:51
  29.5 4.3 %collective-permute-start.6 = (f32[128,128]{1,0:T(8,128)S(1)}, f32[128,128]{1,0:T(8,128)S(1)}, u32[]{:S(2)}, u32[]{:S(2)}) collective-permute-start(f32[128,128]{1,0:T(8,128)S(1)} %get-tuple-element.44), channel_id=1, source_target_pairs={{0,8},{4,12},{8,0},{12,4},{16,24},{20,28},{24,16},{28,20},{1,9},{5... | collective-permute-start | bytes 196616 | tf_op jit(solution)/shard_map/ppermute | solution.py:51
  33.8 11.7 %collective-permute-start.11 = (f32[2,2,128,256]{3,2,1,0:T(8,128)S(1)}, f32[2,2,128,256]{3,2,1,0:T(8,128)S(1)}, u32[]{:S(2)}, u32[]{:S(2)}) collective-permute-start(f32[2,2,128,256]{3,2,1,0:T(8,128)S(1)} %get-tuple-element.36), channel_id=1, source_target_pairs={{0,4},{4,8},{8,12},{12,16},{16,20},{20,24},{24,28},{28,0},{1,5},{5... | collective-permute-start | bytes 1572872 | tf_op jit(solution)/shard_map/ppermute | solution.py:17
  33.8 5.0 %collective-permute-start.9 = (f32[128,128]{1,0:T(8,128)S(1)}, f32[128,128]{1,0:T(8,128)S(1)}, u32[]{:S(2)}, u32[]{:S(2)}) collective-permute-start(f32[128,128]{1,0:T(8,128)S(1)} %fusion.1), channel_id=1, source_target_pairs={{0,1},{1,0},{2,3},{3,2},{4,5},{5,4},{6,7},{7,6},{8,9},{9,8},{10,11... | collective-permute-start | bytes 196616 | tf_op jit(solution)/shard_map/ppermute | solution.py:51
  38.8 6.6 %collective-permute-start.10 = (f32[128,128]{1,0:T(8,128)S(1)}, f32[128,128]{1,0:T(8,128)S(1)}, u32[]{:S(2)}, u32[]{:S(2)}) collective-permute-start(f32[128,128]{1,0:T(8,128)S(1)} %add.75), channel_id=1, source_target_pairs={{0,2},{1,3},{2,0},{3,1},{4,6},{5,7},{6,4},{7,5},{8,10},{9,11},{10,... | collective-permute-start | bytes 196616 | tf_op jit(solution)/shard_map/ppermute | solution.py:51
  45.6 8.2 %collective-permute-start.12 = (f32[2,2,128,128]{3,2,1,0:T(8,128)S(1)}, f32[2,2,128,128]{3,2,1,0:T(8,128)S(1)}, u32[]{:S(2)}, u32[]{:S(2)}) collective-permute-start(f32[2,2,128,128]{3,2,1,0:T(8,128)S(1)} %get-tuple-element.39), channel_id=1, source_target_pairs={{0,1},{1,2},{2,3},{3,0},{4,5},{5,6},{6,7},{7,4},{8,9},{9,10},{10,1... | collective-permute-start | bytes 786440 | tf_op jit(solution)/shard_map/ppermute | solution.py:17
  45.8 5.7 %collective-permute-start.13 = (f32[128,128]{1,0:T(8,128)S(1)}, f32[128,128]{1,0:T(8,128)S(1)}, u32[]{:S(2)}, u32[]{:S(2)}) collective-permute-start(f32[128,128]{1,0:T(8,128)S(1)} %add.76), channel_id=1, source_target_pairs={{0,24},{4,28},{8,16},{12,20},{16,8},{20,12},{24,0},{28,4},{1,25},{... | collective-permute-start | bytes 196616 | tf_op jit(solution)/shard_map/ppermute | solution.py:51
  47.1 4.7 %collective-permute-start.14 = (f32[128,128]{1,0:T(8,128)S(1)}, f32[128,128]{1,0:T(8,128)S(1)}, u32[]{:S(2)}, u32[]{:S(2)}) collective-permute-start(f32[128,128]{1,0:T(8,128)S(1)} %add.76), channel_id=1, source_target_pairs={{0,16},{4,20},{8,24},{12,28},{16,0},{20,4},{24,8},{28,12},{1,17},{... | collective-permute-start | bytes 196616 | tf_op jit(solution)/shard_map/ppermute | solution.py:51
  48.2 4.3 %collective-permute-start.15 = (f32[128,128]{1,0:T(8,128)S(1)}, f32[128,128]{1,0:T(8,128)S(1)}, u32[]{:S(2)}, u32[]{:S(2)}) collective-permute-start(f32[128,128]{1,0:T(8,128)S(1)} %add.76), channel_id=1, source_target_pairs={{0,8},{4,12},{8,0},{12,4},{16,24},{20,28},{24,16},{28,20},{1,9},{5... | collective-permute-start | bytes 196616 | tf_op jit(solution)/shard_map/ppermute | solution.py:51
  52.5 2.1 %collective-permute-start.16 = (f32[512,128]{1,0:T(8,128)S(1)}, f32[512,128]{1,0:T(8,128)S(1)}, u32[]{:S(2)}, u32[]{:S(2)}) collective-permute-start(f32[512,128]{1,0:T(8,128)S(1)} %bitcast.40), channel_id=1, source_target_pairs={{0,4},{4,0},{8,12},{12,8},{16,20},{20,16},{24,28},{28,24},{1,5},{5... | collective-permute-start | bytes 786440 | tf_op jit(solution)/shard_map/ppermute | solution.py:51
  54.6 0.8 %copy-start = (f32[2,512,128]{2,1,0:T(8,128)}, f32[2,512,128]{2,1,0:T(8,128)S(1)}, u32[]{:S(2)}) copy-start(f32[2,512,128]{2,1,0:T(8,128)S(1)} %bitcast_dynamic-update-slice_fusion) | copy-start | bytes 1572868

commit v7 on v6

--- a/solution.py
+++ b/solution.py
@@ -58,7 +58,7 @@
 def scattered(part, axis, unit, ways):
     me = (lax.axis_index(axis) // unit) % ways
     blocks = part.reshape(ways, -1, part.shape[-1])
-    others = [swapped(picked(blocks, me ^ d), axis, d * unit) for d in range(1, ways)]
+    others = [swapped(picked(blocks, me ^ d), axis, d * unit) for d in range(ways - 1, 0, -1)]
     return functools.reduce(jnp.add, others, picked(blocks, me))
 
 

time: 55.6 us -> 55.6 us (level)
  waiting for transfers between devices: 18.2 us -> 16.6 us
  starting transfers between devices: 20.4 us -> 21.6 us
    ppermute x5, starting transfers between devices: 6.32 us -> 7.68 us  [moved(): lax.ppermute(array, axis, [(i, (i + by) % length) for i in range(length)])]
    ppermute x5, waiting for transfers between devices: 1.22 us -> 0.01 us  [moved(): lax.ppermute(array, axis, [(i, (i + by) % length) for i in range(length)])]
  transfers between devices with their start and end apart: 17 -> 17, of which waited for: 12 -> 11; matrix products, arithmetic and copies ran while one was open for 2% -> 2% of each run, Pallas kernels for 10% -> 10%
where the time goes in v7:
time: 55.6 us; the launch traced here: 55 us
  starting transfers between devices  21.6 us (39%)
  waiting for transfers between devices  16.6 us (30%)
  Pallas kernels  12.4 us (22%)
  local copies, waits for them, and re-layouts  2 us (4%)
  between operations  1.56 us (3%)
  other arithmetic  0.86 us (2%)
    ppermute x10, waiting for transfers between devices, swapped(): return lax.ppermute(array, axis, [(i, i ^ bit) for i in range(length)])  13.8 us
    pallas_call x4, Pallas kernels, call(): pl.pallas_call(kernel, in_specs=in_specs, out_specs=[VMEM] * len(outs), o...  12.4 us
    ppermute x10, starting transfers between devices, swapped(): return lax.ppermute(array, axis, [(i, i ^ bit) for i in range(length)])  11.4 us
    ppermute x5, starting transfers between devices, moved(): lax.ppermute(array, axis, [(i, (i + by) % length) for i in range(length)])  7.68 us
    ppermute x2, waiting for transfers between devices, moved_open(): lax.ppermute(array, axis, [(i, i + by) for i in range(length) if 0 <= i +...  2.76 us
    ppermute x2, starting transfers between devices, moved_open(): lax.ppermute(array, axis, [(i, i + by) for i in range(length) if 0 <= i +...  2.57 us
  transfers between devices with their start and end apart: 17, of which 11 were waited for; matrix products, arithmetic and copies ran while one was open for 2% of the time, Pallas kernels for 10%

profile of v7, /device:TPU:0, one launch (start us, length us, event | category | flops | bytes accessed | tf_op | source)
XLA Modules:
  0.0 55.0 jit_solution(14666379851222796046)
XLA Ops:
  0.6 1.0 %slice_bitcast_fusion = (f32[2,128,128]{2,1,0:T(8,128)S(1)}, f32[2,128,128]{2,1,0:T(8,128)S(1)}) fusion(f32[2,2,128,128]{3,2,1,0:T(8,128)} %refs_1_.1), kind=kLoop, calls=%fused_computation.4 | loop fusion | bytes 524288 | tf_op jit(solution)/shard_map/squeeze | solution.py:279
  1.6 1.3 %collective-permute-start.3 = (f32[2,128,128]{2,1,0:T(8,128)S(1)}, f32[2,128,128]{2,1,0:T(8,128)S(1)}, u32[]{:S(2)}, u32[]{:S(2)}) collective-permute-start(f32[2,128,128]{2,1,0:T(8,128)S(1)} %get-tuple-element.47), channel_id=1, source_target_pairs={{1,0},{2,1},{3,2},{5,4},{6,5},{7,6},{9,8},{10,9},{11,10},{13,12},{... | collective-permute-start | bytes 393224 | tf_op jit(solution)/shard_map/ppermute | solution.py:40
  2.9 3.4 %collective-permute-start.1 = (f32[2,2,128,128]{3,2,1,0:T(8,128)}, f32[2,2,128,128]{3,2,1,0:T(8,128)S(1)}, u32[]{:S(2)}, u32[]{:S(2)}) collective-permute-start(f32[2,2,128,128]{3,2,1,0:T(8,128)} %refs_1_.1), channel_id=1, source_target_pairs={{0,28},{4,0},{8,4},{12,8},{16,12},{20,16},{24,20},{28,24},{1,29},{... | collective-permute-start | bytes 786440 | tf_op jit(solution)/shard_map/ppermute | solution.py:17
  6.3 1.3 %collective-permute-start = (f32[2,128,128]{2,1,0:T(8,128)S(1)}, f32[2,128,128]{2,1,0:T(8,128)S(1)}, u32[]{:S(2)}, u32[]{:S(2)}) collective-permute-start(f32[2,128,128]{2,1,0:T(8,128)S(1)} %get-tuple-element.48), channel_id=1, source_target_pairs={{1,0},{2,1},{3,2},{5,4},{6,5},{7,6},{9,8},{10,9},{11,10},{13,12},{... | collective-permute-start | bytes 393224 | tf_op jit(solution)/shard_map/ppermute | solution.py:40
  7.6 2.5 %collective-permute-done.3.right = f32[2,128,128]{2,1,0:T(8,128)S(1)} collective-permute-done((f32[2,128,128]{2,1,0:T(8,128)S(1)}, f32[2,128,128]{2,1,0:T(8,128)S(1)}, u32[]{:S(2)}, u32[]{:S(2)}) %collective-permute-start.3) | collective-permute-done | bytes 131104 | tf_op jit(solution)/shard_map/ppermute | solution.py:40
  10.1 1.1 %collective-permute-start.4 = (f32[2,128,128]{2,1,0:T(8,128)S(1)}, f32[2,128,128]{2,1,0:T(8,128)S(1)}, u32[]{:S(2)}, u32[]{:S(2)}) collective-permute-start(f32[2,128,128]{2,1,0:T(8,128)S(1)} %collective-permute-done.3.right), channel_id=1, source_target_pairs={{0,28},{4,0},{8,4},{12,8},{16,12},{20,16},{24,20},{28,24},{1,29},{... | collective-permute-start | bytes 393224 | tf_op jit(solution)/shard_map/ppermute | solution.py:17
  11.2 1.4 %shard_map.77 = (s32[2,1,1,4]{3,2,1,0:T(1,128)S(1)}, f32[2,2,128,128]{3,2,1,0:T(8,128)S(1)}, f32[4,2,128,128]{3,2,1,0:T(8,128)S(1)}, bf16[2,2,256,256]{3,2,1,0:T(8,128)(2,1)S(1)}, f32[4,128,128]{2,1,0:T(8,128)S(1)}) custom-call(s32[2,1,1,4]{3,2,1,0:T(1,128)} %refs_0_.1, f32[2,2,128,128]{3,2,1,0:T(8,128)} %refs_1_.1, f32[4,2,128,128]{3,2,1,0:T(8,128)} %refs_2_.1, ...), custom_call_target="tpu_custom_call" | custom-call | flops 6442450944 | bytes 4194304 | tf_op jit(solution)/shard_map/pallas_call | solution.py:255
  13.3 0.2 collective-permute-done.right
  13.5 1.6 %collective-permute-start.2 = (f32[2,128,128]{2,1,0:T(8,128)S(1)}, f32[2,128,128]{2,1,0:T(8,128)S(1)}, u32[]{:S(2)}, u32[]{:S(2)}) collective-permute-start(f32[2,128,128]{2,1,0:T(8,128)S(1)} %collective-permute-done.right), channel_id=1, source_target_pairs={{0,28},{4,0},{8,4},{12,8},{16,12},{20,16},{24,20},{28,24},{1,29},{... | collective-permute-start | bytes 393224 | tf_op jit(solution)/shard_map/ppermute | solution.py:17
  15.1 2.9 %shard_map.78 = (f32[4,4,2,128,128]{4,3,2,1,0:T(8,128)S(1)}, f32[4,2,128,128]{3,2,1,0:T(8,128)S(1)}) custom-call(s32[2,1,1,4]{3,2,1,0:T(1,128)S(1)} %get-tuple-element.22.at, f32[2,2,128,128]{3,2,1,0:T(8,128)S(1)} %get-tuple-element.23.tile, f32[4,2,128,128]{3,2,1,0:T(8,128)S(1)} %get-tuple-element.24.probe, ...), custom_call_target="tpu_custom_call" | custom-call | flops 1610612736 | bytes 4194304 | tf_op jit(solution)/shard_map/pallas_call | solution.py:255
  18.1 6.8 %shard_map.79 = (f32[4,2,128,128]{3,2,1,0:T(8,128)S(1)}, f32[2,4,2,128,128]{4,3,2,1,0:T(8,128)S(1)}) custom-call(s32[2,1,1,4]{3,2,1,0:T(1,128)S(1)} %get-tuple-element.22.at, s32[1,1]{1,0:T(1,128)S(6)} %copy.14.count, f32[2,2,128,128]{3,2,1,0:T(8,128)S(1)} %get-tuple-element.23.tile, f32[2,128,128]{2,1,0:T(8,128)S(1)} %collective-permute-done.right, ...), custom_call_target="tpu_custom_call" | custom-call | flops 4831838208 | bytes 4194304 | tf_op jit(solution)/shard_map/pallas_call | solution.py:255
  25.0 1.5 %collective-permute-done.5 = f32[512,128]{1,0:T(8,128)S(1)} collective-permute-done((f32[512,128]{1,0:T(8,128)S(1)}, f32[512,128]{1,0:T(8,128)S(1)}, u32[]{:S(2)}, u32[]{:S(2)}) %collective-permute-start.5) | collective-permute-done | bytes 262176 | tf_op jit(solution)/shard_map/ppermute | solution.py:51
  26.6 1.5 %collective-permute-start.8 = (f32[128,128]{1,0:T(8,128)S(1)}, f32[128,128]{1,0:T(8,128)S(1)}, u32[]{:S(2)}, u32[]{:S(2)}) collective-permute-start(f32[128,128]{1,0:T(8,128)S(1)} %get-tuple-element.45), channel_id=1, source_target_pairs={{0,8},{4,12},{8,0},{12,4},{16,24},{20,28},{24,16},{28,20},{1,9},{5... | collective-permute-start | bytes 196616 | tf_op jit(solution)/shard_map/ppermute | solution.py:51
  28.0 1.5 %collective-permute-start.7 = (f32[128,128]{1,0:T(8,128)S(1)}, f32[128,128]{1,0:T(8,128)S(1)}, u32[]{:S(2)}, u32[]{:S(2)}) collective-permute-start(f32[128,128]{1,0:T(8,128)S(1)} %get-tuple-element.46), channel_id=1, source_target_pairs={{0,16},{4,20},{8,24},{12,28},{16,0},{20,4},{24,8},{28,12},{1,17},{... | collective-permute-start | bytes 196616 | tf_op jit(solution)/shard_map/ppermute | solution.py:51
  29.6 0.6 %collective-permute-start.6 = (f32[128,128]{1,0:T(8,128)S(1)}, f32[128,128]{1,0:T(8,128)S(1)}, u32[]{:S(2)}, u32[]{:S(2)}) collective-permute-start(f32[128,128]{1,0:T(8,128)S(1)} %get-tuple-element.44), channel_id=1, source_target_pairs={{0,24},{4,28},{8,16},{12,20},{16,8},{20,12},{24,0},{28,4},{1,25},{... | collective-permute-start | bytes 196616 | tf_op jit(solution)/shard_map/ppermute | solution.py:51
  30.1 1.2 %shard_map.80 = (f32[2,2,128,256]{3,2,1,0:T(8,128)S(1)}, f32[2,2,128,256]{3,2,1,0:T(8,128)S(1)}) custom-call(s32[2,1,1,4]{3,2,1,0:T(1,128)S(1)} %get-tuple-element.22.at, f32[2,4,2,128,128]{4,3,2,1,0:T(8,128)S(1)} %get-tuple-element.31.g_windows), custom_call_target="tpu_custom_call" | custom-call | flops 402653184 | bytes 4194304 | tf_op jit(solution)/shard_map/pallas_call | solution.py:255
  31.4 0.9 %collective-permute-done.7 = f32[128,128]{1,0:T(8,128)S(1)} collective-permute-done((f32[128,128]{1,0:T(8,128)S(1)}, f32[128,128]{1,0:T(8,128)S(1)}, u32[]{:S(2)}, u32[]{:S(2)}) %collective-permute-start.7) | collective-permute-done | bytes 65568 | tf_op jit(solution)/shard_map/ppermute | solution.py:51
  32.3 2.4 %collective-permute-done.6 = f32[128,128]{1,0:T(8,128)S(1)} collective-permute-done((f32[128,128]{1,0:T(8,128)S(1)}, f32[128,128]{1,0:T(8,128)S(1)}, u32[]{:S(2)}, u32[]{:S(2)}) %collective-permute-start.6) | collective-permute-done | bytes 65568 | tf_op jit(solution)/shard_map/ppermute | solution.py:51
  34.8 1.6 %collective-permute-start.9 = (f32[128,128]{1,0:T(8,128)S(1)}, f32[128,128]{1,0:T(8,128)S(1)}, u32[]{:S(2)}, u32[]{:S(2)}) collective-permute-start(f32[128,128]{1,0:T(8,128)S(1)} %fusion.1), channel_id=1, source_target_pairs={{0,1},{1,0},{2,3},{3,2},{4,5},{5,4},{6,7},{7,6},{8,9},{9,8},{10,11... | collective-permute-start | bytes 196616 | tf_op jit(solution)/shard_map/ppermute | solution.py:51
  36.4 2.7 %collective-permute-done.9 = f32[128,128]{1,0:T(8,128)S(1)} collective-permute-done((f32[128,128]{1,0:T(8,128)S(1)}, f32[128,128]{1,0:T(8,128)S(1)}, u32[]{:S(2)}, u32[]{:S(2)}) %collective-permute-start.9) | collective-permute-done | bytes 65568 | tf_op jit(solution)/shard_map/ppermute | solution.py:51
  39.1 2.6 %collective-permute-start.10 = (f32[128,128]{1,0:T(8,128)S(1)}, f32[128,128]{1,0:T(8,128)S(1)}, u32[]{:S(2)}, u32[]{:S(2)}) collective-permute-start(f32[128,128]{1,0:T(8,128)S(1)} %add.75), channel_id=1, source_target_pairs={{0,2},{1,3},{2,0},{3,1},{4,6},{5,7},{6,4},{7,5},{8,10},{9,11},{10,... | collective-permute-start | bytes 196616 | tf_op jit(solution)/shard_map/ppermute | solution.py:51
  41.8 2.6 %collective-permute-done.10 = f32[128,128]{1,0:T(8,128)S(1)} collective-permute-done((f32[128,128]{1,0:T(8,128)S(1)}, f32[128,128]{1,0:T(8,128)S(1)}, u32[]{:S(2)}, u32[]{:S(2)}) %collective-permute-start.10) | collective-permute-done | bytes 65568 | tf_op jit(solution)/shard_map/ppermute | solution.py:51
  44.5 1.6 %collective-permute-start.12 = (f32[2,2,128,128]{3,2,1,0:T(8,128)S(1)}, f32[2,2,128,128]{3,2,1,0:T(8,128)S(1)}, u32[]{:S(2)}, u32[]{:S(2)}) collective-permute-start(f32[2,2,128,128]{3,2,1,0:T(8,128)S(1)} %get-tuple-element.39), channel_id=1, source_target_pairs={{0,1},{1,2},{2,3},{3,0},{4,5},{5,6},{6,7},{7,4},{8,9},{9,10},{10,1... | collective-permute-start | bytes 786440 | tf_op jit(solution)/shard_map/ppermute | solution.py:17
  46.1 0.9 %collective-permute-start.13 = (f32[128,128]{1,0:T(8,128)S(1)}, f32[128,128]{1,0:T(8,128)S(1)}, u32[]{:S(2)}, u32[]{:S(2)}) collective-permute-start(f32[128,128]{1,0:T(8,128)S(1)} %add.76), channel_id=1, source_target_pairs={{0,24},{4,28},{8,16},{12,20},{16,8},{20,12},{24,0},{28,4},{1,25},{... | collective-permute-start | bytes 196616 | tf_op jit(solution)/shard_map/ppermute | solution.py:51
  47.0 1.3 %collective-permute-start.14 = (f32[128,128]{1,0:T(8,128)S(1)}, f32[128,128]{1,0:T(8,128)S(1)}, u32[]{:S(2)}, u32[]{:S(2)}) collective-permute-start(f32[128,128]{1,0:T(8,128)S(1)} %add.76), channel_id=1, source_target_pairs={{0,16},{4,20},{8,24},{12,28},{16,0},{20,4},{24,8},{28,12},{1,17},{... | collective-permute-start | bytes 196616 | tf_op jit(solution)/shard_map/ppermute | solution.py:51
  48.3 1.3 %collective-permute-start.15 = (f32[128,128]{1,0:T(8,128)S(1)}, f32[128,128]{1,0:T(8,128)S(1)}, u32[]{:S(2)}, u32[]{:S(2)}) collective-permute-start(f32[128,128]{1,0:T(8,128)S(1)} %add.76), channel_id=1, source_target_pairs={{0,8},{4,12},{8,0},{12,4},{16,24},{20,28},{24,16},{28,20},{1,9},{5... | collective-permute-start | bytes 196616 | tf_op jit(solution)/shard_map/ppermute | solution.py:51
  49.6 2.2 %collective-permute-done.13 = f32[128,128]{1,0:T(8,128)S(1)} collective-permute-done((f32[128,128]{1,0:T(8,128)S(1)}, f32[128,128]{1,0:T(8,128)S(1)}, u32[]{:S(2)}, u32[]{:S(2)}) %collective-permute-start.13) | collective-permute-done | bytes 65568 | tf_op jit(solution)/shard_map/ppermute | solution.py:51
  51.9 0.1 collective-permute-done.14
  52.0 0.6 %collective-permute-done.15 = f32[128,128]{1,0:T(8,128)S(1)} collective-permute-done((f32[128,128]{1,0:T(8,128)S(1)}, f32[128,128]{1,0:T(8,128)S(1)}, u32[]{:S(2)}, u32[]{:S(2)}) %collective-permute-start.15) | collective-permute-done | bytes 65568 | tf_op jit(solution)/shard_map/ppermute | solution.py:51
  52.8 0.7 %add.78 = f32[2,2,128,128]{3,2,1,0:T(8,128)} add(f32[2,2,128,128]{3,2,1,0:T(8,128)S(1)} %get-tuple-element.38, f32[2,2,128,128]{3,2,1,0:T(8,128)S(1)} %collective-permute-done.12) | non-fusion elementwise | flops 65536 | bytes 786432 | tf_op jit(solution)/shard_map/add | solution.py:326
  53.5 0.7 %collective-permute-done.16 = f32[512,128]{1,0:T(8,128)S(1)} collective-permute-done((f32[512,128]{1,0:T(8,128)S(1)}, f32[512,128]{1,0:T(8,128)S(1)}, u32[]{:S(2)}, u32[]{:S(2)}) %collective-permute-start.16) | collective-permute-done | bytes 262176 | tf_op jit(solution)/shard_map/ppermute | solution.py:51
  54.2 0.8 %copy-done = f32[2,512,128]{2,1,0:T(8,128)} copy-done((f32[2,512,128]{2,1,0:T(8,128)}, f32[2,512,128]{2,1,0:T(8,128)S(1)}, u32[]{:S(2)}) %copy-start) | copy-done | bytes 524312
  (26 shorter events, 0.6 us)
Async XLA Ops:
  1.6 8.5 %collective-permute-start.3 = (f32[2,128,128]{2,1,0:T(8,128)S(1)}, f32[2,128,128]{2,1,0:T(8,128)S(1)}, u32[]{:S(2)}, u32[]{:S(2)}) collective-permute-start(f32[2,128,128]{2,1,0:T(8,128)S(1)} %get-tuple-element.47), channel_id=1, source_target_pairs={{1,0},{2,1},{3,2},{5,4},{6,5},{7,6},{9,8},{10,9},{11,10},{13,12},{... | collective-permute-start | bytes 393224 | tf_op jit(solution)/shard_map/ppermute | solution.py:40
  2.9 12.2 %collective-permute-start.1 = (f32[2,2,128,128]{3,2,1,0:T(8,128)}, f32[2,2,128,128]{3,2,1,0:T(8,128)S(1)}, u32[]{:S(2)}, u32[]{:S(2)}) collective-permute-start(f32[2,2,128,128]{3,2,1,0:T(8,128)} %refs_1_.1), channel_id=1, source_target_pairs={{0,28},{4,0},{8,4},{12,8},{16,12},{20,16},{24,20},{28,24},{1,29},{... | collective-permute-start | bytes 786440 | tf_op jit(solution)/shard_map/ppermute | solution.py:17
  6.3 7.2 %collective-permute-start = (f32[2,128,128]{2,1,0:T(8,128)S(1)}, f32[2,128,128]{2,1,0:T(8,128)S(1)}, u32[]{:S(2)}, u32[]{:S(2)}) collective-permute-start(f32[2,128,128]{2,1,0:T(8,128)S(1)} %get-tuple-element.48), channel_id=1, source_target_pairs={{1,0},{2,1},{3,2},{5,4},{6,5},{7,6},{9,8},{10,9},{11,10},{13,12},{... | collective-permute-start | bytes 393224 | tf_op jit(solution)/shard_map/ppermute | solution.py:40
  10.1 4.9 %collective-permute-start.4 = (f32[2,128,128]{2,1,0:T(8,128)S(1)}, f32[2,128,128]{2,1,0:T(8,128)S(1)}, u32[]{:S(2)}, u32[]{:S(2)}) collective-permute-start(f32[2,128,128]{2,1,0:T(8,128)S(1)} %collective-permute-done.3.right), channel_id=1, source_target_pairs={{0,28},{4,0},{8,4},{12,8},{16,12},{20,16},{24,20},{28,24},{1,29},{... | collective-permute-start | bytes 393224 | tf_op jit(solution)/shard_map/ppermute | solution.py:17
  13.5 4.5 %collective-permute-start.2 = (f32[2,128,128]{2,1,0:T(8,128)S(1)}, f32[2,128,128]{2,1,0:T(8,128)S(1)}, u32[]{:S(2)}, u32[]{:S(2)}) collective-permute-start(f32[2,128,128]{2,1,0:T(8,128)S(1)} %collective-permute-done.right), channel_id=1, source_target_pairs={{0,28},{4,0},{8,4},{12,8},{16,12},{20,16},{24,20},{28,24},{1,29},{... | collective-permute-start | bytes 393224 | tf_op jit(solution)/shard_map/ppermute | solution.py:17
  24.9 1.6 %collective-permute-start.5 = (f32[512,128]{1,0:T(8,128)S(1)}, f32[512,128]{1,0:T(8,128)S(1)}, u32[]{:S(2)}, u32[]{:S(2)}) collective-permute-start(f32[512,128]{1,0:T(8,128)S(1)} %dynamic-slice_bitcast_fusion), channel_id=1, source_target_pairs={{0,4},{4,0},{8,12},{12,8},{16,20},{20,16},{24,28},{28,24},{1,5},{5... | collective-permute-start | bytes 786440 | tf_op jit(solution)/shard_map/ppermute | solution.py:51
  26.6 4.8 %collective-permute-start.8 = (f32[128,128]{1,0:T(8,128)S(1)}, f32[128,128]{1,0:T(8,128)S(1)}, u32[]{:S(2)}, u32[]{:S(2)}) collective-permute-start(f32[128,128]{1,0:T(8,128)S(1)} %get-tuple-element.45), channel_id=1, source_target_pairs={{0,8},{4,12},{8,0},{12,4},{16,24},{20,28},{24,16},{28,20},{1,9},{5... | collective-permute-start | bytes 196616 | tf_op jit(solution)/shard_map/ppermute | solution.py:51
  28.0 4.3 %collective-permute-start.7 = (f32[128,128]{1,0:T(8,128)S(1)}, f32[128,128]{1,0:T(8,128)S(1)}, u32[]{:S(2)}, u32[]{:S(2)}) collective-permute-start(f32[128,128]{1,0:T(8,128)S(1)} %get-tuple-element.46), channel_id=1, source_target_pairs={{0,16},{4,20},{8,24},{12,28},{16,0},{20,4},{24,8},{28,12},{1,17},{... | collective-permute-start | bytes 196616 | tf_op jit(solution)/shard_map/ppermute | solution.py:51
  29.6 5.2 %collective-permute-start.6 = (f32[128,128]{1,0:T(8,128)S(1)}, f32[128,128]{1,0:T(8,128)S(1)}, u32[]{:S(2)}, u32[]{:S(2)}) collective-permute-start(f32[128,128]{1,0:T(8,128)S(1)} %get-tuple-element.44), channel_id=1, source_target_pairs={{0,24},{4,28},{8,16},{12,20},{16,8},{20,12},{24,0},{28,4},{1,25},{... | collective-permute-start | bytes 196616 | tf_op jit(solution)/shard_map/ppermute | solution.py:51
  34.7 9.7 %collective-permute-start.11 = (f32[2,2,128,256]{3,2,1,0:T(8,128)S(1)}, f32[2,2,128,256]{3,2,1,0:T(8,128)S(1)}, u32[]{:S(2)}, u32[]{:S(2)}) collective-permute-start(f32[2,2,128,256]{3,2,1,0:T(8,128)S(1)} %get-tuple-element.36), channel_id=1, source_target_pairs={{0,4},{4,8},{8,12},{12,16},{16,20},{20,24},{24,28},{28,0},{1,5},{5... | collective-permute-start | bytes 1572872 | tf_op jit(solution)/shard_map/ppermute | solution.py:17
  34.8 4.3 %collective-permute-start.9 = (f32[128,128]{1,0:T(8,128)S(1)}, f32[128,128]{1,0:T(8,128)S(1)}, u32[]{:S(2)}, u32[]{:S(2)}) collective-permute-start(f32[128,128]{1,0:T(8,128)S(1)} %fusion.1), channel_id=1, source_target_pairs={{0,1},{1,0},{2,3},{3,2},{4,5},{5,4},{6,7},{7,6},{8,9},{9,8},{10,11... | collective-permute-start | bytes 196616 | tf_op jit(solution)/shard_map/ppermute | solution.py:51
  39.1 5.2 %collective-permute-start.10 = (f32[128,128]{1,0:T(8,128)S(1)}, f32[128,128]{1,0:T(8,128)S(1)}, u32[]{:S(2)}, u32[]{:S(2)}) collective-permute-start(f32[128,128]{1,0:T(8,128)S(1)} %add.75), channel_id=1, source_target_pairs={{0,2},{1,3},{2,0},{3,1},{4,6},{5,7},{6,4},{7,5},{8,10},{9,11},{10,... | collective-permute-start | bytes 196616 | tf_op jit(solution)/shard_map/ppermute | solution.py:51
  44.5 8.2 %collective-permute-start.12 = (f32[2,2,128,128]{3,2,1,0:T(8,128)S(1)}, f32[2,2,128,128]{3,2,1,0:T(8,128)S(1)}, u32[]{:S(2)}, u32[]{:S(2)}) collective-permute-start(f32[2,2,128,128]{3,2,1,0:T(8,128)S(1)} %get-tuple-element.39), channel_id=1, source_target_pairs={{0,1},{1,2},{2,3},{3,0},{4,5},{5,6},{6,7},{7,4},{8,9},{9,10},{10,1... | collective-permute-start | bytes 786440 | tf_op jit(solution)/shard_map/ppermute | solution.py:17
  46.1 5.8 %collective-permute-start.13 = (f32[128,128]{1,0:T(8,128)S(1)}, f32[128,128]{1,0:T(8,128)S(1)}, u32[]{:S(2)}, u32[]{:S(2)}) collective-permute-start(f32[128,128]{1,0:T(8,128)S(1)} %add.76), channel_id=1, source_target_pairs={{0,24},{4,28},{8,16},{12,20},{16,8},{20,12},{24,0},{28,4},{1,25},{... | collective-permute-start | bytes 196616 | tf_op jit(solution)/shard_map/ppermute | solution.py:51
  47.0 5.0 %collective-permute-start.14 = (f32[128,128]{1,0:T(8,128)S(1)}, f32[128,128]{1,0:T(8,128)S(1)}, u32[]{:S(2)}, u32[]{:S(2)}) collective-permute-start(f32[128,128]{1,0:T(8,128)S(1)} %add.76), channel_id=1, source_target_pairs={{0,16},{4,20},{8,24},{12,28},{16,0},{20,4},{24,8},{28,12},{1,17},{... | collective-permute-start | bytes 196616 | tf_op jit(solution)/shard_map/ppermute | solution.py:51
  48.3 4.3 %collective-permute-start.15 = (f32[128,128]{1,0:T(8,128)S(1)}, f32[128,128]{1,0:T(8,128)S(1)}, u32[]{:S(2)}, u32[]{:S(2)}) collective-permute-start(f32[128,128]{1,0:T(8,128)S(1)} %add.76), channel_id=1, source_target_pairs={{0,8},{4,12},{8,0},{12,4},{16,24},{20,28},{24,16},{28,20},{1,9},{5... | collective-permute-start | bytes 196616 | tf_op jit(solution)/shard_map/ppermute | solution.py:51
  52.6 1.6 %collective-permute-start.16 = (f32[512,128]{1,0:T(8,128)S(1)}, f32[512,128]{1,0:T(8,128)S(1)}, u32[]{:S(2)}, u32[]{:S(2)}) collective-permute-start(f32[512,128]{1,0:T(8,128)S(1)} %bitcast.40), channel_id=1, source_target_pairs={{0,4},{4,0},{8,12},{12,8},{16,20},{20,16},{24,28},{28,24},{1,5},{5... | collective-permute-start | bytes 786440 | tf_op jit(solution)/shard_map/ppermute | solution.py:51
  54.2 0.8 %copy-start = (f32[2,512,128]{2,1,0:T(8,128)}, f32[2,512,128]{2,1,0:T(8,128)S(1)}, u32[]{:S(2)}) copy-start(f32[2,512,128]{2,1,0:T(8,128)S(1)} %bitcast_dynamic-update-slice_fusion) | copy-start | bytes 1572868
